TPU v7x, 32 devices: a whole 2x2x4 slice. The times are simulated.
32 devices in a mesh: seq: 8 (over z, x), tp: 4 (over y, core).
Axes of the slice: x: 2, y: 2, z: 4, core: 2. Of those that a mesh axis runs over, the one named last changes fastest.
Arguments:
- inputs: bfloat16 [2048, 768], P('seq'), may hold values from -6 to 6
- value_weight: bfloat16 [768, 768], P(None, 'tp'), may hold values from -0.21875 to 0.21875
- value_bias: float32 [768], P('tp'), may hold values from -3 to 3
- out_weight: bfloat16 [768, 768], P('tp'), may hold values from -0.21875 to 0.21875
- out_bias: float32 [768], replicated, may hold values from -3 to 3
- first_gain: float32 [768], replicated, may hold values from 0.5 to 1.5
- first_shift: float32 [768], replicated, may hold values from -3 to 3
- up_weight: bfloat16 [768, 3072], P(None, 'tp'), may hold values from -0.21875 to 0.21875
- up_bias: float32 [3072], P('tp'), may hold values from -3 to 3
- down_weight: bfloat16 [3072, 768], P('tp'), may hold values from -0.109375 to 0.109375
- down_bias: float32 [768], replicated, may hold values from -3 to 3
- second_gain: float32 [768], replicated, may hold values from 0.5 to 1.5
- second_shift: float32 [768], replicated, may hold values from -3 to 3
- conv_weight: float32 [12, 65], P('tp'), may hold values from -0.75 to 0.75
- query_codes: int32 [2048, 12, 32], P('seq', 'tp'), may hold values from 0 to 255
- key_codes: int32 [2048, 12, 32], P('seq', 'tp'), may hold values from 0 to 255
- masked: int32 [2048], P('seq'), may hold values from 0 to 1, as said below
- out_grad: float32 [2048, 768], P('seq'), may hold values from -6 to 6
Outputs:
- output: bfloat16 [2048, 768], P('seq')
- input_grad: float32 [2048, 768], P('seq')
- grad_value_weight: float32 [768, 768], P(None, 'tp')
- grad_value_bias: float32 [768], P('tp')
- grad_out_weight: float32 [768, 768], P('tp')
- grad_out_bias: float32 [768], replicated
- grad_first_gain: float32 [768], replicated
- grad_first_shift: float32 [768], replicated
- grad_up_weight: float32 [768, 3072], P(None, 'tp')
- grad_up_bias: float32 [3072], P('tp')
- grad_down_weight: float32 [3072, 768], P('tp')
- grad_down_bias: float32 [768], replicated
- grad_second_gain: float32 [768], replicated
- grad_second_shift: float32 [768], replicated
- grad_conv_weight: float32 [12, 65], P('tp')
Inputs may be any that keep to these rules, and one draw needn't show every extreme that they name: `masked`: the rows of one device (256 tokens) hold between max(12, 1) and 64 ones; the rows of some device hold exactly 64.
All inputs are finite; a program needn't handle non-finite values.
Results may differ from a plain program's by a relative error of at most 0.017.
Values may be sent and summed in bfloat16 or wider, within the bound.
No kernel may reach another device: no remote copies, remote signals or barrier semaphores. Data moves between devices by JAX's collectives and lax.ppermute only.
A program may use at most 64 MiB of HBM per device.

v0:
```python
from functools import partial

import jax
import jax.numpy as jnp
from jax import lax
from jax.sharding import PartitionSpec as P

HASHES = 32
BUCKETS = 256


def extended(block, sides, width):
    for axis, dim in sides:
        count = lax.axis_size(axis)
        forward = [(i, i + 1) for i in range(count - 1)]
        backward = [(target, source) for source, target in forward]
        low = lax.ppermute(
            lax.slice_in_dim(block, block.shape[dim] - width, None, axis=dim), axis, forward
        )
        high = lax.ppermute(lax.slice_in_dim(block, 0, width, axis=dim), axis, backward)
        block = jnp.concatenate([low, block, high], axis=dim)
    return block


def shortened(array):
    return jax.tree.map(lambda a: a.astype(jnp.bfloat16) if a.dtype == jnp.float32 else a, array)


def norm_rows(features, norm_gain, norm_shift):
    centre = features - jnp.mean(features, -1, keepdims=True)
    spread = jnp.mean(centre * centre, -1, keepdims=True)
    return centre * lax.rsqrt(spread + 1e-05) * norm_gain + norm_shift


def attend(value_sum, conv_term):
    scaled = value_sum * lax.rsqrt(jnp.mean(value_sum * value_sum, -1, keepdims=True) + 1e-05)
    return scaled + conv_term


def one_hot(bucket_codes):
    return (bucket_codes[..., None] == lax.broadcasted_iota(jnp.int32, (1, 1, BUCKETS), 2)).astype(
        jnp.bfloat16
    )


def build_tables(row_block, bucket_codes):

    def build_one_head(operands):
        return jnp.einsum(
            "rmb,rc->mbc", one_hot(operands[1]), operands[0], preferred_element_type=jnp.float32
        )

    return lax.map(
        build_one_head, (jnp.swapaxes(row_block, 0, 1), jnp.swapaxes(bucket_codes, 0, 1))
    )


def read_tables(tables, bucket_codes):

    def read_one_head(operands):
        return jnp.einsum(
            "rmb,mbc->rc", one_hot(operands[1]), operands[0], preferred_element_type=jnp.float32
        )

    return jnp.swapaxes(lax.map(read_one_head, (tables, jnp.swapaxes(bucket_codes, 0, 1))), 0, 1)


def conv_rows(padded, conv_weight, head_dim):
    kernel = jnp.repeat(conv_weight.T, head_dim, axis=1)[:, None, :]
    return lax.conv_general_dilated(
        padded[None],
        kernel,
        (1,),
        "VALID",
        dimension_numbers=("NWC", "WIO", "NWC"),
        feature_group_count=padded.shape[-1],
        precision=lax.Precision.HIGHEST,
    )[0]


def inner_rows(left_side, right_side):
    return lax.dot_general(
        left_side, right_side, (((0,), (0,)), ((), ())), preferred_element_type=jnp.float32
    )


def times_trans(left_side, right_side):
    return lax.dot_general(
        left_side, right_side, (((1,), (1,)), ((), ())), preferred_element_type=jnp.float32
    )


def per_device(
    inputs,
    value_weight,
    value_bias,
    out_weight,
    out_bias,
    first_gain,
    first_shift,
    up_weight,
    up_bias,
    down_weight,
    down_bias,
    second_gain,
    second_shift,
    conv_weight,
    query_codes,
    key_codes,
    masked,
    out_grad,
):
    tokens = inputs.shape[0]
    local_heads = conv_weight.shape[0]
    local_width = value_weight.shape[1]
    head_dim = local_width // local_heads
    half_width = (conv_weight.shape[1] - 1) // 2
    projected = jnp.dot(inputs, value_weight, preferred_element_type=jnp.float32) + value_bias
    value_low = projected.reshape(tokens, local_heads, head_dim).astype(jnp.bfloat16)
    tables = build_tables(value_low, key_codes)
    tables_low = lax.psum(tables, "seq").astype(jnp.bfloat16)
    bucket_reads = read_tables(tables_low, query_codes) / HASHES
    value_flat = value_low.reshape(tokens, local_width)
    padded_values = extended(value_flat, (("seq", 0),), half_width).astype(jnp.float32)
    conv_term = conv_rows(padded_values, conv_weight, head_dim).reshape(
        tokens, local_heads, head_dim
    )
    context, attend_back = jax.vjp(attend, bucket_reads, conv_term)
    context_low = context.reshape(tokens, local_width).astype(jnp.bfloat16)
    hidden = (
        inputs.astype(jnp.float32)
        + lax.psum(jnp.dot(context_low, out_weight, preferred_element_type=jnp.float32), "tp")
        + out_bias
    )
    first, first_back = jax.vjp(norm_rows, hidden, first_gain, first_shift)
    first_low = first.astype(jnp.bfloat16)
    pre_act = jnp.dot(first_low, up_weight, preferred_element_type=jnp.float32) + up_bias
    activated, gelu_back = jax.vjp(partial(jax.nn.gelu, approximate=False), pre_act)
    act_low = activated.astype(jnp.bfloat16)
    second = (
        first
        + lax.psum(
            jnp.dot(act_low, down_weight, preferred_element_type=jnp.float32).astype(jnp.bfloat16),
            "tp",
        ).astype(jnp.float32)
        + down_bias
    )
    output, second_back = jax.vjp(norm_rows, second, second_gain, second_shift)
    cotangent = out_grad * masked.astype(jnp.float32)[:, None]
    grad_second, grad_second_gain, grad_second_shift = second_back(cotangent)
    grad_down = grad_second.astype(jnp.bfloat16)
    grad_down_bias = jnp.sum(grad_second, 0)
    grad_down_weight = inner_rows(act_low, grad_down)
    grad_pre = gelu_back(times_trans(grad_down, down_weight))[0].astype(jnp.bfloat16)
    grad_up_bias = jnp.sum(grad_pre.astype(jnp.float32), 0)
    grad_up_weight = inner_rows(first_low, grad_pre)
    grad_first = grad_second + lax.psum(times_trans(grad_pre, up_weight), "tp")
    grad_hidden, grad_first_gain, grad_first_shift = first_back(grad_first)
    grad_attn = grad_hidden.astype(jnp.bfloat16)
    grad_out_bias = jnp.sum(grad_hidden, 0)
    grad_out_weight = inner_rows(context_low, grad_attn)
    grad_context = times_trans(grad_attn, out_weight).astype(jnp.bfloat16)
    grad_reads, grad_conv = attend_back(
        grad_context.astype(jnp.float32).reshape(tokens, local_heads, head_dim)
    )
    grad_read_low = (grad_reads / HASHES).astype(jnp.bfloat16)
    grad_tables = build_tables(grad_read_low, query_codes)
    grad_tables_low = jax.tree.map(
        lambda part: part.astype(jnp.float32), lax.psum(shortened(grad_tables), "seq")
    ).astype(jnp.bfloat16)
    grad_table_rows = read_tables(grad_tables_low, key_codes)
    padded_grads = extended(grad_context, (("seq", 0),), half_width).astype(jnp.float32)
    grad_conv_values = conv_rows(padded_grads, conv_weight[:, ::-1], head_dim).reshape(
        tokens, local_heads, head_dim
    )
    grad_conv_weight = jax.vjp(
        lambda weight: conv_rows(padded_values, weight, head_dim), conv_weight
    )[1](grad_conv.reshape(tokens, local_width))[0]
    grad_values = (
        (grad_table_rows + grad_conv_values).reshape(tokens, local_width).astype(jnp.bfloat16)
    )
    grad_value_bias = jnp.sum(grad_values.astype(jnp.float32), 0)
    grad_value_weight = inner_rows(inputs, grad_values)
    input_grad = grad_hidden + lax.psum(
        times_trans(grad_values, value_weight).astype(jnp.bfloat16), "tp"
    ).astype(jnp.float32)
    all_sums = (
        lax.psum(grad_first_gain.astype(jnp.bfloat16), "seq").astype(jnp.float32),
        lax.psum(grad_first_shift.astype(jnp.bfloat16), "seq").astype(jnp.float32),
        lax.psum(grad_out_weight.astype(jnp.bfloat16), "seq").astype(jnp.float32),
        lax.psum(grad_out_bias.astype(jnp.bfloat16), "seq").astype(jnp.float32),
        lax.psum(grad_value_weight.astype(jnp.bfloat16), "seq").astype(jnp.float32),
        lax.psum(grad_value_bias.astype(jnp.bfloat16), "seq").astype(jnp.float32),
        lax.psum(grad_conv_weight.astype(jnp.bfloat16), "seq").astype(jnp.float32),
        lax.psum(grad_second_gain.astype(jnp.bfloat16), "seq").astype(jnp.float32),
        lax.psum(grad_second_shift.astype(jnp.bfloat16), "seq").astype(jnp.float32),
        lax.psum(grad_down_weight.astype(jnp.bfloat16), "seq").astype(jnp.float32),
        lax.psum(grad_down_bias.astype(jnp.bfloat16), "seq").astype(jnp.float32),
        lax.psum(grad_up_weight.astype(jnp.bfloat16), "seq").astype(jnp.float32),
        lax.psum(grad_up_bias.astype(jnp.bfloat16), "seq").astype(jnp.float32),
    )
    (
        sum_first_gain,
        sum_first_shift,
        sum_out_weight,
        sum_out_bias,
        sum_value_weight,
        sum_value_bias,
        sum_conv_weight,
        sum_second_gain,
        sum_second_shift,
        sum_down_weight,
        sum_down_bias,
        sum_up_weight,
        sum_up_bias,
    ) = all_sums
    return (
        output.astype(jnp.bfloat16),
        input_grad,
        sum_value_weight,
        sum_value_bias,
        sum_out_weight,
        sum_out_bias,
        sum_first_gain,
        sum_first_shift,
        sum_up_weight,
        sum_up_bias,
        sum_down_weight,
        sum_down_bias,
        sum_second_gain,
        sum_second_shift,
        sum_conv_weight,
    )


def solution(mesh):
    return jax.shard_map(
        per_device,
        mesh=mesh,
        in_specs=(
            P("seq", None),
            P(None, "tp"),
            P("tp"),
            P("tp", None),
            P(),
            P(),
            P(),
            P(None, "tp"),
            P("tp"),
            P("tp", None),
            P(),
            P(),
            P(),
            P("tp", None),
            P("seq", "tp", None),
            P("seq", "tp", None),
            P("seq"),
            P("seq", None),
        ),
        out_specs=(
            P("seq", None),
            P("seq", None),
            P(None, "tp"),
            P("tp"),
            P("tp", None),
            P(),
            P(),
            P(),
            P(None, "tp"),
            P("tp"),
            P("tp", None),
            P(),
            P(),
            P(),
            P("tp", None),
        ),
        check_vma=False,
    )
```

profile of v0, /device:TPU:0, one launch (start us, length us, event | category | flops | bytes accessed | tf_op | source)
XLA Modules:
  0.0 749.4 jit_solution(16085329001564793787)
XLA Ops:
  8.8 4.8 collective-permute-start
  15.0 12.7 %while.44 = (s32[]{:T(128)}, f32[3,32,256,64]{2,3,1,0:T(8,128)}, s32[3,256,32]{1,2,0:T(8,128)}, bf16[3,256,64]{1,2,0:T(8,128)(2,1)S(1)}) while((s32[]{:T(128)}, f32[3,32,256,64]{2,3,1,0:T(8,128)}, s32[3,256,32]{1,2,0:T(8,128)}, bf16[3,256,64]{1,2,0:T(8,128)(2,1)S(1)}) %tuple.121), condition=%wide.region_1.2_spmd.clone, body=%wide.region_0.1_spmd.sunk.clone | while | flops 270532608 | bytes 2229305 | solution.py:53
  15.7 3.5 bitcast_dynamic-update-slice_fusion.6
  20.0 3.5 bitcast_dynamic-update-slice_fusion.6
  24.2 3.5 bitcast_dynamic-update-slice_fusion.6
  27.7 247.6 %all-reduce.21 = bf16[3,32,256,64]{2,3,1,0:T(8,128)(2,1)} all-reduce(f32[3,32,256,64]{2,3,1,0:T(8,128)} %get-tuple-element.103), channel_id=1, replica_groups=mesh['seq'=8,'tp'=4] {'seq'}, use_global_device_ids=true, to_apply=%region_2.3 | all-reduce | flops 1572864 | bytes 9437184 | tf_op jit(solution)/shard_map/psum | solution.py:121
  275.3 13.1 %while.45 = (s32[]{:T(128)}, f32[3,256,64]{1,2,0:T(8,128)S(1)}, s32[3,256,32]{1,2,0:T(8,128)}, bf16[3,32,256,64]{2,3,1,0:T(8,128)(2,1)}) while((s32[]{:T(128)}, f32[3,256,64]{1,2,0:T(8,128)S(1)}, s32[3,256,32]{1,2,0:T(8,128)}, bf16[3,32,256,64]{2,3,1,0:T(8,128)(2,1)}) %tuple.117), condition=%wide.region_4.5_spmd.clone, body=%wide.region_3.4_spmd.sunk.clone | while | flops 270532608 | bytes 1213497 | solution.py:65
  276.0 3.6 fusion.99
  280.4 3.6 fusion.99
  284.8 3.6 fusion.99
  294.3 34.0 %all-reduce.10.cloned.1.call-done = f32[256,768]{1,0:T(8,128)} async-done(((f32[256,768]{1,0:T(8,128)}), f32[256,768]{1,0:T(8,128)}) %all-reduce.10.cloned.1.call-update) | async-done | bytes 786448 | tf_op jit(solution)/shard_map/psum | solution.py:132
  329.9 3.2 multiply_convert_fusion
  335.2 32.7 %all-reduce.12.cloned.1.call-done = bf16[256,768]{1,0:T(8,128)(2,1)} async-done(((bf16[256,768]{1,0:T(8,128)(2,1)}), bf16[256,768]{1,0:T(8,128)(2,1)}) %all-reduce.12.cloned.1.call-update) | async-done | bytes 393232 | tf_op jit(solution)/shard_map/psum | solution.py:142
  377.9 32.7 %all-reduce.14.cloned.1.call-done = f32[256,768]{1,0:T(8,128)} async-done(((f32[256,768]{1,0:T(8,128)}), f32[256,768]{1,0:T(8,128)}) %all-reduce.14.cloned.1.call-update) | async-done | bytes 786448 | tf_op jit(solution)/shard_map/psum | solution.py:157
  410.6 2.3 multiply_reduce_fusion.1
  414.6 14.4 %while.46 = (s32[]{:T(128)}, bf16[3,32,256,64]{2,3,1,0:T(8,128)(2,1)}, s32[3,256,32]{1,2,0:T(8,128)}, bf16[3,256,64]{1,2,0:T(8,128)(2,1)}) while((s32[]{:T(128)}, bf16[3,32,256,64]{2,3,1,0:T(8,128)(2,1)}, s32[3,256,32]{1,2,0:T(8,128)}, bf16[3,256,64]{1,2,0:T(8,128)(2,1)}) %tuple.118), condition=%wide.region_19.20_spmd.clone, body=%wide.region_18.19_spmd.sunk.clone | while | flops 270532608 | bytes 2229305 | solution.py:53
  415.3 4.0 bitcast_dynamic-update-slice_fusion.7
  420.1 4.0 bitcast_dynamic-update-slice_fusion.7
  424.9 4.0 bitcast_dynamic-update-slice_fusion.7
  433.3 2.7 convolution_convert_fusion
  437.7 3.4 collective-permute-start.2
  443.7 4.4 collective-permute-done.3
  450.5 108.5 %all-reduce.16.cloned.1.call-done = bf16[3,32,256,64]{2,3,1,0:T(8,128)(2,1)} async-done(((bf16[3,32,256,64]{2,3,1,0:T(8,128)(2,1)}), bf16[3,32,256,64]{2,3,1,0:T(8,128)(2,1)}) %all-reduce.16.cloned.1.call-update) | async-done | bytes 3145744 | tf_op jit(solution)/shard_map/psum | solution.py:169
  559.0 13.2 %while.47 = (s32[]{:T(128)}, f32[3,256,64]{1,2,0:T(8,128)S(1)}, s32[3,256,32]{1,2,0:T(8,128)}, bf16[3,32,256,64]{2,3,1,0:T(8,128)(2,1)}) while((s32[]{:T(128)}, f32[3,256,64]{1,2,0:T(8,128)S(1)}, s32[3,256,32]{1,2,0:T(8,128)}, bf16[3,32,256,64]{2,3,1,0:T(8,128)(2,1)}) %tuple.120), condition=%wide.region_22.23_spmd.clone, body=%wide.region_21.22_spmd.sunk.clone | while | flops 270532608 | bytes 1213497 | solution.py:65
  559.9 3.6 fusion.102
  564.3 3.6 fusion.102
  568.6 3.6 fusion.102
  575.0 11.9 %fusion.58 = f32[65,1,192]{2,1,0:T(1,128)S(1)} fusion(bf16[1,320,192]{2,0,1:T(2,128)(2,1)S(1)} %copy-done.21, bf16[1,256,192]{2,0,1:T(2,128)(2,1)S(1)} %copy.48), kind=kOutput, calls=%fused_computation.126 | convolution fusion | flops 6389760 | bytes 271104 | tf_op jit(solution)/shard_map/transpose(jvp())/conv_general_dilated | solution.py:70
  587.1 18.1 %all-reduce.18.cloned.1.call-done = bf16[256,768]{1,0:T(8,128)(2,1)} async-done(((bf16[256,768]{1,0:T(8,128)(2,1)}), bf16[256,768]{1,0:T(8,128)(2,1)}) %all-reduce.18.cloned.1.call-update) | async-done | bytes 393232 | tf_op jit(solution)/shard_map/psum | solution.py:184
  607.3 38.8 %all-reduce = (bf16[192]{0:T(256)(128)(2,1)S(1)}, bf16[768]{0:T(1024)(128)(2,1)S(1)}, bf16[768]{0:T(1024)(128)(2,1)S(1)}, bf16[768]{0:T(1024)(128)(2,1)S(1)}, bf...) all-reduce(bf16[192]{0:T(256)(128)(2,1)S(1)} %reduce_sum.198, ...), channel_id=1, replica_groups=mesh['seq'=8,'tp'=4] {'seq'}, use_global_device_ids=true, to_apply=%region_26.27 | all-reduce | flops 5763 | bytes 23052 | tf_op jit(solution)/shard_map/psum | solution.py:193
  651.4 84.9 %all-reduce.20.cloned.1.call-done = (bf16[768,192]{0,1:T(8,128)(2,1)}, bf16[192,768]{1,0:T(8,128)(2,1)}, bf16[768,768]{1,0:T(8,128)(2,1)}, bf16[768,768]{1,0:T(8,128)(2,1)}) async-done(((bf16[768,192]{0,1:T(8,128)(2,1)}, bf16[192,768]{1,0:T(8,128)(2,1)}, bf16[768,768]{1,0:T(8,128)(2,1)}, bf16[768,768]{1,0:T(8,128)(2,1)}), (bf16[768,192]{0,1:T(8,128)(2,1)}, bf16[192,768]{1,0:T(8,128)(2,1)}, ...) | async-done | bytes 2949136 | tf_op jit(solution)/shard_map/psum | solution.py:192
  736.3 2.9 convert_element_type.194
  (198 shorter events, 57.7 us)
Async XLA Ops:
  7.2 322.7 %copy-start = (bf16[768,768]{1,0:T(8,128)(2,1)S(1)}, bf16[768,768]{1,0:T(8,128)(2,1)}, u32[]{:S(2)}) copy-start(bf16[768,768]{1,0:T(8,128)(2,1)} %param.33) | copy-start | bytes 3538948
  7.2 321.1 %all-reduce.10.cloned.1.call-start = ((), (), s32[]{:S(2)}) async-start(), calls=%async_computation | async-start | bytes 1572864 | tf_op jit(solution)/shard_map/psum | solution.py:132
  8.8 280.4 %collective-permute-start = (bf16[32,192]{0,1:T(8,128)(2,1)S(1)}, bf16[32,192]{0,1:T(8,128)(2,1)S(1)}, u32[]{:S(2)}, u32[]{:S(2)}) collective-permute-start(bf16[32,192]{0,1:T(8,128)(2,1)S(1)} %get-tuple-element.177), channel_id=1, source_target_pairs={{0,4},{4,8},{8,12},{12,16},{16,20},{20,24},{24,28},{1,5},{5,9},{9,... | collective-permute-start | bytes 36872 | tf_op jit(solution)/shard_map/ppermute | solution.py:17
  13.7 275.5 %collective-permute-start.1 = (bf16[32,192]{0,1:T(8,128)(2,1)S(1)}, bf16[32,192]{0,1:T(8,128)(2,1)S(1)}, u32[]{:S(2)}, u32[]{:S(2)}) collective-permute-start(bf16[32,192]{0,1:T(8,128)(2,1)S(1)} %get-tuple-element.178), channel_id=1, source_target_pairs={{4,0},{8,4},{12,8},{16,12},{20,16},{24,20},{28,24},{5,1},{9,5},{13... | collective-permute-start | bytes 36872 | tf_op jit(solution)/shard_map/ppermute | solution.py:20
  275.2 13.8 %copy-start.39 = (f32[3,65]{1,0:T(4,128)S(1)}, f32[3,65]{1,0:T(4,128)}, u32[]{:S(2)}) copy-start(f32[3,65]{1,0:T(4,128)} %param.39) | copy-start | bytes 2344
  292.2 36.1 %copy-start.3 = (bf16[256,768]{1,0:T(8,128)(2,1)S(1)}, bf16[256,768]{1,0:T(8,128)(2,1)}, u32[]{:S(2)}) copy-start(bf16[256,768]{1,0:T(8,128)(2,1)} %param.26) | copy-start | bytes 1179652
  292.2 36.1 %copy-start.43 = (f32[768]{0:T(1024)S(1)}, f32[768]{0:T(1024)}, u32[]{:S(2)}) copy-start(f32[768]{0:T(1024)} %param.30) | copy-start | bytes 9220
  293.0 36.8 %copy-start.25 = (f32[768]{0:T(1024)S(1)}, f32[768]{0:T(1024)}, u32[]{:S(2)}) copy-start(f32[768]{0:T(1024)} %param.31) | copy-start | bytes 9220
  293.0 36.8 %copy-start.27 = (f32[768]{0:T(1024)S(1)}, f32[768]{0:T(1024)}, u32[]{:S(2)}) copy-start(f32[768]{0:T(1024)} %param.32) | copy-start | bytes 9220
  293.0 36.8 %copy-start.47 = (f32[768]{0:T(1024)S(1)}, f32[768]{0:T(1024)}, u32[]{:S(2)}) copy-start(f32[768]{0:T(1024)} %param.34) | copy-start | bytes 9220
  294.2 73.6 %all-reduce.12.cloned.1.call-start = ((), (), s32[]{:S(2)}) async-start(), calls=%async_computation.1 | async-start | bytes 786432 | tf_op jit(solution)/shard_map/psum | solution.py:142
  333.1 34.8 %copy-start.44 = (f32[768]{0:T(1024)S(1)}, f32[768]{0:T(1024)}, u32[]{:S(2)}) copy-start(f32[768]{0:T(1024)} %param.36) | copy-start | bytes 9220
  333.8 35.7 %copy-start.8 = (f32[256,768]{1,0:T(8,128)S(1)}, f32[256,768]{1,0:T(8,128)}, u32[]{:S(2)}) copy-start(f32[256,768]{1,0:T(8,128)} %param.43) | copy-start | bytes 2359300
  333.8 35.7 %copy-start.26 = (f32[768]{0:T(1024)S(1)}, f32[768]{0:T(1024)}, u32[]{:S(2)}) copy-start(f32[768]{0:T(1024)} %param.37) | copy-start | bytes 9220
  335.1 75.5 %all-reduce.14.cloned.1.call-start = ((), (), s32[]{:S(2)}) async-start(), calls=%async_computation.2 | async-start | bytes 1572864 | tf_op jit(solution)/shard_map/psum | solution.py:157
  335.1 35.4 %copy-start.33 = (f32[256]{0:T(256)}, f32[256]{0:T(256)S(1)}, u32[]{:S(2)}) copy-start(f32[256]{0:T(256)S(1)} %convert_element_type.170) | copy-start | bytes 3076
  372.4 38.2 %copy-start.34 = (f32[256]{0:T(256)}, f32[256]{0:T(256)S(1)}, u32[]{:S(2)}) copy-start(f32[256]{0:T(256)S(1)} %negate_multiply_fusion.2) | copy-start | bytes 3076
  375.8 183.2 %all-reduce.16.cloned.1.call-start = ((), (), s32[]{:S(2)}) async-start(), calls=%async_computation.3 | async-start | bytes 6291456 | tf_op jit(solution)/shard_map/psum | solution.py:169
  377.9 34.9 %copy-start.36 = (f32[256]{0:T(256)S(1)}, f32[256]{0:T(256)}, u32[]{:S(2)}) copy-start(f32[256]{0:T(256)} %copy-done.35) | copy-start | bytes 3076
  429.0 176.2 %all-reduce.18.cloned.1.call-start = ((), (), s32[]{:S(2)}) async-start(), calls=%async_computation.4 | async-start | bytes 786432 | tf_op jit(solution)/shard_map/psum | solution.py:184
  437.7 6.0 collective-permute-start.2
  441.1 7.0 collective-permute-start.3
  559.0 13.4 %copy-start.13 = (bf16[768,192]{0,1:T(8,128)(2,1)S(1)}, bf16[768,192]{0,1:T(8,128)(2,1)}, u32[]{:S(2)}) copy-start(bf16[768,192]{0,1:T(8,128)(2,1)} %param.27) | copy-start | bytes 884740
  559.0 14.7 %copy-start.4 = (bf16[256,768]{1,0:T(8,128)(2,1)S(1)}, bf16[256,768]{1,0:T(8,128)(2,1)}, u32[]{:S(2)}) copy-start(bf16[256,768]{1,0:T(8,128)(2,1)} %param.26) | copy-start | bytes 1179652
  573.5 162.8 %all-reduce.20.cloned.1.call-start = ((), (), s32[]{:S(2)}) async-start(), calls=%async_computation.5 | async-start | bytes 5898240 | tf_op jit(solution)/shard_map/psum | solution.py:192
  574.9 30.3 %copy-start.32 = (f32[256]{0:T(256)S(1)}, f32[256]{0:T(256)}, u32[]{:S(2)}) copy-start(f32[256]{0:T(256)} %copy-done.30) | copy-start | bytes 3076
  574.9 32.3 %copy-start.37 = (bf16[768]{0:T(1024)(128)(2,1)S(1)}, bf16[768]{0:T(1024)(128)(2,1)}, u32[]{:S(2)}) copy-start(bf16[768]{0:T(1024)(128)(2,1)} %get-tuple-element.107) | copy-start | bytes 4612
  574.9 32.3 %copy-start.38 = (bf16[768]{0:T(1024)(128)(2,1)S(1)}, bf16[768]{0:T(1024)(128)(2,1)}, u32[]{:S(2)}) copy-start(bf16[768]{0:T(1024)(128)(2,1)} %get-tuple-element.111) | copy-start | bytes 4612
  574.9 32.3 %copy-start.40 = (bf16[768]{0:T(1024)(128)(2,1)S(1)}, bf16[768]{0:T(1024)(128)(2,1)}, u32[]{:S(2)}) copy-start(bf16[768]{0:T(1024)(128)(2,1)} %get-tuple-element.109) | copy-start | bytes 4612
  575.0 32.3 %copy-start.41 = (bf16[768]{0:T(1024)(128)(2,1)S(1)}, bf16[768]{0:T(1024)(128)(2,1)}, u32[]{:S(2)}) copy-start(bf16[768]{0:T(1024)(128)(2,1)} %get-tuple-element.112) | copy-start | bytes 4612
  575.0 32.3 %copy-start.42 = (bf16[768]{0:T(1024)(128)(2,1)S(1)}, bf16[768]{0:T(1024)(128)(2,1)}, u32[]{:S(2)}) copy-start(bf16[768]{0:T(1024)(128)(2,1)} %get-tuple-element.172) | copy-start | bytes 4612
  575.0 32.3 %copy-start.45 = (bf16[768]{0:T(1024)(128)(2,1)S(1)}, bf16[768]{0:T(1024)(128)(2,1)}, u32[]{:S(2)}) copy-start(bf16[768]{0:T(1024)(128)(2,1)} %get-tuple-element.182) | copy-start | bytes 4612
  (28 other events, 89.7 us)
Sparse Core Ops, SparseCore 0:
  294.4 33.8 all-reduce.9
  335.2 32.6 all-reduce.11
  376.0 34.6 all-reduce.13
  429.1 129.8 all-reduce.15
  573.6 31.5 all-reduce.17
  610.8 125.4 all-reduce.19
where the time goes:
time: 751 us; the launch traced here: 749 us
  waiting for transfers between devices  316 us (42%)
  blocking collectives  286 us (38%)
  matrix products  77.2 us (10%)
  other arithmetic  26 us (3%)
  local copies, waits for them, and re-layouts  18.1 us (2%)
  between operations  14.8 us (2%)
  starting transfers between devices  11.2 us (1%)
    psum x1, blocking collectives, per_device(): tables_low = lax.psum(tables, 'seq').astype(jnp.bfloat16)  248 us
    psum x1, waiting for transfers between devices, per_device(): lax.psum(shortened(grad_tables), 'seq')  108 us
    psum x1, waiting for transfers between devices, per_device(): lax.psum(grad_value_weight.astype(jnp.bfloat16), 'seq').astype(jnp.float32)  84.9 us
    psum x1, blocking collectives, per_device(): lax.psum(grad_value_bias.astype(jnp.bfloat16), 'seq').astype(jnp.float32)  38.8 us
    psum x1, waiting for transfers between devices, per_device(): lax.psum(jnp.dot(context_low, out_weight, preferred_element_type=jnp.floa...  34 us
    psum x1, waiting for transfers between devices, per_device(): lax.psum(jnp.dot(act_low, down_weight, preferred_element_type=jnp.float32...  32.7 us
    psum x1, waiting for transfers between devices, per_device(): grad_first = grad_second + lax.psum(times_trans(grad_pre, up_weight), 'tp')  32.7 us
    dot_general x6, matrix products, build_one_head(): jnp.einsum('rmb,rc->mbc', one_hot(operands[1]), operands[0], preferred_el...  22.5 us
  transfers between devices with their start and end apart: 10, of which 8 were waited for; matrix products, arithmetic and copies ran while one was open for 8% of the time, Pallas kernels for 0%

commit v1 on v0

v1 whole, which is shorter than its diff:
```python
from functools import partial

import jax
import jax.numpy as jnp
import numpy as np
from jax import lax
from jax.experimental import pallas as pl
from jax.experimental.pallas import tpu as pltpu
from jax.sharding import PartitionSpec as P

F32, BF16, I32 = jnp.float32, jnp.bfloat16, jnp.int32
MIB = 1 << 20


def dot(a, b, dims):
    return lax.dot_general(a, b, (dims, ((), ())), preferred_element_type=F32)


def nn(a, b):
    return dot(a, b, ((1,), (0,)))


def nt(a, b):
    return dot(a, b, ((1,), (1,)))


def tn(a, b):
    return dot(a, b, ((0,), (0,)))


def split2(x):
    high = x.astype(BF16)
    return high, (x - high.astype(F32)).astype(BF16)


def split3(x):
    high = x.astype(BF16)
    rest = x - high.astype(F32)
    middle = rest.astype(BF16)
    return high, middle, (rest - middle.astype(F32)).astype(BF16)


def iota(shape, dim):
    return lax.broadcasted_iota(I32, shape, dim)


def one_zero(condition):
    return jnp.where(condition, 1.0, 0.0).astype(BF16)


def call(body, outs, args, name, scratch=(), smem=0, vmem=40, flops=0, moved=0):
    specs = [pl.BlockSpec(memory_space=pltpu.SMEM)] * smem
    specs += [pl.BlockSpec(memory_space=pltpu.VMEM)] * (len(args) - smem)
    shapes = [outs] if isinstance(outs, tuple) else outs
    shapes = [jax.ShapeDtypeStruct(shape, dtype) for shape, dtype in shapes]
    return pl.pallas_call(
        body,
        out_shape=shapes,
        in_specs=specs,
        out_specs=[pl.BlockSpec(memory_space=pltpu.VMEM)] * len(shapes),
        scratch_shapes=list(scratch),
        compiler_params=pltpu.CompilerParams(vmem_limit_bytes=vmem * MIB),
        cost_estimate=pl.CostEstimate(flops=flops, bytes_accessed=moved, transcendentals=0),
        name=name,
    )(*args)


def norm_stats(rows):
    centre = rows - jnp.mean(rows, -1, keepdims=True)
    spread = jnp.mean(centre * centre, -1, keepdims=True)
    q = lax.rsqrt(spread + 1e-05)
    return centre * q, q


def cdf_of(u):
    return 0.5 * (1.0 + lax.erf(u * 0.7071067811865476))


def gelu_grad(u):
    return cdf_of(u) + u * jnp.exp(-0.5 * u * u) * 0.3989422804014327


def plane_weights(heads, hashes):
    lanes = 128
    rows = heads * hashes
    wide = np.zeros((8 * lanes, 2 * lanes), np.float32)
    tall = np.zeros((64, 8 * rows), np.float32)
    for b in range(8):
        for h in range(heads):
            for m in range(hashes):
                half, power = divmod(m, 16)
                wide[b * lanes + h * hashes + m, half * lanes + h * 8 + b] = 2.0**power
                tall[half * 32 + h * 8 + b, b * rows + h * hashes + m] = 2.0**power
    return jnp.asarray(wide, BF16), jnp.asarray(tall, BF16)


def query_words(codes, wide):
    whole = codes.astype(F32).astype(I32)
    bits = jnp.concatenate(
        [((whole >> b) & 1).astype(F32).astype(BF16) for b in range(8)], axis=1
    )
    both = nn(bits, wide)
    return both[:, :128].astype(I32) | (both[:, 128:].astype(I32) << 16)


def key_words(codes, tall):
    whole = codes.astype(F32).astype(I32)
    bits = jnp.concatenate(
        [((whole >> b) & 1).astype(F32).astype(BF16) for b in range(8)], axis=0
    )
    both = nn(tall, bits)
    return both[:32].astype(I32) | (both[32:].astype(I32) << 16)


def matches(query_block, key_block, head):
    apart = None
    for b in range(8):
        word = head * 8 + b
        unlike = query_block[:, word : word + 1] ^ key_block[word : word + 1, :]
        apart = unlike if apart is None else apart | unlike
    return (32 - lax.population_count(apart)).astype(F32).astype(BF16)


def per_device(
    inputs,
    value_weight,
    value_bias,
    out_weight,
    out_bias,
    first_gain,
    first_shift,
    up_weight,
    up_bias,
    down_weight,
    down_bias,
    second_gain,
    second_shift,
    conv_weight,
    query_codes,
    key_codes,
    masked,
    out_grad,
):
    n = lax.axis_size("seq")
    tp = lax.axis_size("tp")
    tokens, width = inputs.shape
    heads, hashes = query_codes.shape[1], query_codes.shape[2]
    taps = conv_weight.shape[1]
    half = (taps - 1) // 2
    local = value_weight.shape[1]
    dim = local // heads
    hidden_units = up_weight.shape[1]
    chosen = tokens // 4
    rest = tokens - chosen
    piece = rest // tp
    codes_rows = heads * hashes
    window = tokens + 128
    total = n * chosen
    seq_id, tp_id = lax.axis_index("seq"), lax.axis_index("tp")
    ids = jnp.stack([seq_id, tp_id]).astype(I32)
    wide, tall = plane_weights(heads, hashes)

    def swap(array, k):
        return lax.ppermute(array, "tp", [(i, i ^ k) for i in range(tp)])

    def others(array):
        return [swap(array, k) for k in range(1, tp)]

    def exchange(array):
        return lax.all_to_all(array, "seq", 0, 0)

    def row(vector):
        return vector.reshape(1, -1)

    query_t = jnp.transpose(query_codes, (1, 2, 0)).reshape(codes_rows, tokens)
    key_t = jnp.transpose(key_codes, (1, 2, 0)).reshape(codes_rows, tokens)
    value_t = value_weight.T

    def order_body(masked_ref, query_ref, chosen_ref, rest_ref, order_ref):
        flags = jnp.broadcast_to(masked_ref[...].astype(F32), (8, tokens))
        upto = one_zero(iota((tokens, tokens), 0) <= iota((tokens, tokens), 1))
        count = nn(flags.astype(BF16), upto)
        spot = iota((8, tokens), 1).astype(F32)
        target = jnp.where(flags > 0, count - 1.0, count[:, tokens - 1 :] + spot - count)
        order = one_zero(iota((tokens, tokens), 0) == target[:1].astype(I32))
        order_ref[...] = order
        where = jnp.where(
            iota((128 - codes_rows, tokens), 0) == 0, iota((128 - codes_rows, tokens), 1), 0
        )
        table = jnp.concatenate([query_ref[...], where], axis=0).astype(F32).astype(BF16)
        sorted_codes = nt(order, table).astype(BF16)
        for i in range(n):
            chosen_ref[i] = sorted_codes[:chosen]
        rest_ref[...] = sorted_codes[chosen:]

    chosen_codes, rest_codes, order = call(
        order_body,
        [((n, chosen, 128), BF16), ((rest, 128), BF16), ((tokens, tokens), BF16)],
        (row(masked), query_t),
        "order",
    )
    all_codes = exchange(chosen_codes)

    def value_body(inputs_ref, weight_ref, bias_ref, key_ref, value_ref, send_ref):
        values = (nt(inputs_ref[...], weight_ref[...]) + bias_ref[...]).astype(BF16)
        value_ref[...] = values
        same = one_zero(iota((local, local), 0) == iota((local, local), 1))
        send_ref[:codes_rows] = key_ref[...].astype(F32).astype(BF16)
        send_ref[codes_rows:] = nt(same, values).astype(BF16)

    values, value_send = call(
        value_body,
        [((tokens, local), BF16), ((codes_rows + local, tokens), BF16)],
        (inputs, value_t, row(value_bias), key_t),
        "values",
    )
    all_keys = lax.all_gather(value_send, "seq", axis=0)
    out_all = lax.all_gather(out_weight, "tp", axis=0)
    value_all = lax.all_gather(value_t, "tp", axis=0)

    def sort_body(order_ref, inputs_ref, grad_ref, masked_ref, sorted_ref, cot_ref):
        sorted_ref[...] = nn(order_ref[...], inputs_ref[...]).astype(BF16)
        pick = order_ref[:chosen]
        flags = jnp.broadcast_to(masked_ref[...].astype(F32), (8, tokens)).astype(BF16)
        valid = nt(pick, flags)[:, :1]
        parts = split3(grad_ref[...])
        cot_ref[...] = (nn(pick, parts[0]) + nn(pick, parts[1]) + nn(pick, parts[2])) * valid

    sorted_inputs, cot = call(
        sort_body,
        [((tokens, width), BF16), ((chosen, width), F32)],
        (order, inputs, out_grad, row(masked)),
        "sort",
    )

    def taps_body(order_ref, conv_ref, ahead_ref, back_ref, pad_ref):
        pad_ref[...] = jnp.zeros_like(pad_ref)
        pad_ref[:heads, :taps] = conv_ref[...]
        turn = one_zero(iota((128, 128), 0) + iota((128, 128), 1) == taps - 1)
        padded = pad_ref[:, :128]
        parts = split3(padded)
        turned = nn(parts[0], turn) + nn(parts[1], turn) + nn(parts[2], turn)
        blank = jnp.zeros((8, window - 128), F32)
        ahead = jnp.concatenate([padded, blank], axis=1)
        back = jnp.concatenate([turned, blank], axis=1)
        for h in range(heads):
            for source, ref in ((ahead, ahead_ref), (back, back_ref)):
                spread = jnp.broadcast_to(source[h : h + 1], (tokens, window))
                band = pltpu.roll(spread, 0, 1, stride=1, stride_axis=0)
                high, low = split2(band)
                if ref is ahead_ref:
                    high = nn(order_ref[...], high).astype(BF16)
                    low = nn(order_ref[...], low).astype(BF16)
                ref[h, :, :window] = high
                ref[h, :, window:] = low

    bands, back_bands = call(
        taps_body,
        [((heads, tokens, 2 * window), BF16)] * 2,
        (order, conv_weight),
        "taps",
        scratch=[pltpu.VMEM((8, 128), F32)],
    )

    def count_body(ids_ref, codes_ref, send_ref, value_ref, wide_ref, tall_ref, count_ref, out_ref):
        me = ids_ref[0]
        keys = key_words(send_ref[:codes_rows], tall_ref[...])
        queries = query_words(codes_ref[...].reshape(total, 128), wide_ref[...])
        for h in range(heads):
            turned = send_ref[codes_rows + h * dim : codes_rows + (h + 1) * dim]
            for r in range(0, total, tokens):
                for c in range(0, tokens, 128):
                    count_ref[h, r : r + tokens, c : c + 128] = matches(
                        queries[r : r + tokens], keys[:, c : c + 128], h
                    )
            read = nt(count_ref[h], turned).astype(BF16)
            for i in range(n):
                out_ref[i, :chosen, h * dim : (h + 1) * dim] = read[i * chosen : (i + 1) * chosen]
        for i in range(n):
            last, head_rows = value_ref[tokens - half :], value_ref[:half]
            rows = jnp.where(i == me + 1, last.astype(F32), head_rows.astype(F32))
            out_ref[i, chosen:] = rows.astype(BF16)

    counts, reads = call(
        count_body,
        [((heads, total, tokens), BF16), ((n, chosen + half, local), BF16)],
        (ids, all_codes, value_send, values, wide, tall),
        "count",
        smem=1,
    )
    reads = exchange(reads)

    def unit_rows(value_sum):
        return lax.rsqrt(jnp.mean(value_sum * value_sum, -1, keepdims=True) + 1e-05)

    def context_body(ids_ref, reads_ref, value_ref, band_ref, context_ref, sum_ref, near_ref):
        me = ids_ref[0]
        total_read = reads_ref[0, :chosen].astype(F32)
        for i in range(1, n):
            total_read += reads_ref[i, :chosen].astype(F32)
        total_read = total_read * (1.0 / hashes)
        sum_ref[...] = total_read
        before = reads_ref[jnp.maximum(me - 1, 0), chosen:].astype(F32)
        after = reads_ref[jnp.minimum(me + 1, n - 1), chosen:].astype(F32)
        near_ref[:half] = jnp.where(me > 0, before, 0.0).astype(BF16)
        near_ref[half : half + tokens] = value_ref[...]
        near_ref[half + tokens : 2 * half + tokens] = jnp.where(me < n - 1, after, 0.0).astype(BF16)
        near_ref[2 * half + tokens :] = jnp.zeros((window - tokens - 2 * half, local), BF16)
        near = near_ref[...]
        twice = jnp.concatenate([near, near], axis=0)
        for h in range(heads):
            cols = slice(h * dim, (h + 1) * dim)
            mine = total_read[:, cols]
            conv = nn(band_ref[h, :chosen], twice[:, cols])
            context_ref[:, cols] = (mine * unit_rows(mine) + conv).astype(BF16)

    context, value_sum, near = call(
        context_body,
        [((chosen, local), BF16), ((chosen, local), F32), ((window, local), BF16)],
        (ids, reads, values, bands),
        "context",
        smem=1,
    )
    contexts = [context] + others(context)

    def joined(ids_ref, context_refs, out_ref):
        mine = ids_ref[1]
        terms = [nn(ref[...], out_ref[mine ^ k]) for k, ref in enumerate(context_refs)]
        return paired(terms)

    def paired(terms):
        while len(terms) > 1:
            terms = [terms[i] + terms[i + 1] for i in range(0, len(terms), 2)]
        return terms[0]

    def feed(low, up_ref, up_bias_ref, down_ref):
        pre = nn(low, up_ref[...]) + up_bias_ref[...]
        act = (pre * cdf_of(pre)).astype(BF16)
        return pre, nn(act, down_ref[...]).astype(BF16)

    def first_body(ids_ref, *refs):
        context_refs, refs = refs[:tp], refs[tp:]
        (out_ref, inputs_ref, bias_ref, gain_ref, shift_ref, up_ref, up_bias_ref, down_ref, sum_ref,
         hidden_ref, first_ref, pre_ref, part_ref, keep_ref) = refs
        hidden = inputs_ref[:chosen].astype(F32) + joined(ids_ref, context_refs, out_ref) + bias_ref[...]
        hidden_ref[...] = hidden
        unit, _ = norm_stats(hidden)
        first = unit * gain_ref[...] + shift_ref[...]
        first_ref[...] = first
        low = first.astype(BF16)
        pre, part = feed(low, up_ref, up_bias_ref, down_ref)
        pre_ref[...] = pre
        part_ref[...] = part
        keep_ref[:, :width] = low
        keep_ref[:, width : width + local] = context_refs[0][...]
        keep_ref[:, width + local :] = sum_ref[...].astype(BF16)

    hidden, first, pre_act, part, keep = call(
        first_body,
        [((chosen, width), F32), ((chosen, width), F32), ((chosen, hidden_units), F32),
         ((chosen, width), BF16), ((chosen, width + 2 * local), BF16)],
        (ids, *contexts, out_all, sorted_inputs, row(out_bias), row(first_gain), row(first_shift),
         up_weight, row(up_bias), down_weight, value_sum),
        "first",
        smem=1,
    )
    parts = [part] + others(part)
    keeps = lax.all_gather(keep, "seq", axis=0)

    def slope_body(pre_ref, slope_ref):
        slope_ref[...] = gelu_grad(pre_ref[...])

    (slope,) = call(slope_body, ((chosen, hidden_units), F32), (pre_act,), "slope")

    def back_norm(grad, unit, q, gain):
        scaled = grad * gain
        return q * (
            scaled
            - jnp.mean(scaled, -1, keepdims=True)
            - unit * jnp.mean(scaled * unit, -1, keepdims=True)
        )

    def put_sums(ref, sums):
        for i, vector in enumerate(sums):
            ref[i : i + 1] = vector

    def column_sum(array):
        return jnp.sum(array, 0, keepdims=True)

    def second_body(*refs):
        part_refs, refs = refs[:tp], refs[tp:]
        (first_ref, bias_ref, gain_ref, shift_ref, cot_ref, slope_ref, down_ref, up_ref,
         output_ref, grad_ref, back_ref, sums_ref, send_ref) = refs
        second = first_ref[...] + paired([r[...].astype(F32) for r in part_refs]) + bias_ref[...]
        unit, q = norm_stats(second)
        output_ref[...] = (unit * gain_ref[...] + shift_ref[...]).astype(BF16)
        grad = back_norm(cot_ref[...], unit, q, gain_ref[...])
        grad_ref[...] = grad
        low = grad.astype(BF16)
        grad_pre = (nt(low, down_ref[...]) * slope_ref[...]).astype(BF16)
        back_ref[...] = nt(grad_pre, up_ref[...]).astype(BF16)
        put_sums(sums_ref, [column_sum(cot_ref[...] * unit), column_sum(cot_ref[...]), column_sum(grad)])
        send_ref[:, :width] = low
        send_ref[:, width:] = jnp.zeros((chosen, send_ref.shape[1] - width), BF16)

    out_chosen, grad_second, back, sums, down_send = call(
        second_body,
        [((chosen, width), BF16), ((chosen, width), F32), ((chosen, width), BF16), ((8, width), F32),
         ((chosen, width + 256), BF16)],
        (*parts, first, row(down_bias), row(second_gain), row(second_shift), cot, slope, down_weight,
         up_weight),
        "second",
    )
    backs = [back] + others(back)
    down_all = lax.all_gather(down_send, "seq", axis=0)
    part_width = width // 2

    def hidden_body(ids_ref, *refs):
        back_refs, refs = refs[:tp], refs[tp:]
        grad_ref, hidden_ref, gain_ref, sums_ref, out_ref, send_ref, attn_ref, sum_ref = refs
        side = ids_ref[1] % 2
        grad = grad_ref[...] + paired([r[...].astype(F32) for r in back_refs])
        unit, q = norm_stats(hidden_ref[...])
        grad_hidden = back_norm(grad, unit, q, gain_ref[...])
        out_ref[...] = grad_hidden
        attn_ref[...] = grad_hidden.astype(BF16)
        sum_ref[...] = jnp.zeros_like(sum_ref)
        sum_ref[:3] = sums_ref[:3]
        put_sums(sum_ref.at[3:6], [column_sum(grad * unit), column_sum(grad), column_sum(grad_hidden)])
        lanes = pl.ds(pl.multiple_of(side * part_width, part_width), part_width)
        mine, mine_sums = attn_ref[:, lanes], sum_ref[:, lanes].astype(BF16)
        for i in range(n):
            send_ref[i, :chosen] = mine
            send_ref[i, chosen:] = mine_sums

    grad_hidden, attn_send = call(
        hidden_body,
        [((chosen, width), F32), ((n, chosen + 16, part_width), BF16)],
        (ids, *backs, grad_second, hidden, row(first_gain), sums),
        "hidden",
        smem=1,
        scratch=[pltpu.VMEM((chosen, width), BF16), pltpu.VMEM((16, width), F32)],
    )
    attn_mine = exchange(attn_send)
    attn_other = swap(attn_mine, 1)

    def values_body(ids_ref, mine_ref, other_ref, out_ref, keep_ref, count_ref, band_ref, codes_ref,
                    grad_ref, dense_ref, attn_ref, sums_ref, y_ref, read_ref):
        me, side = ids_ref[0], ids_ref[1] % 2
        own = pl.ds(pl.multiple_of(side * part_width, part_width), part_width)
        far = pl.ds(pl.multiple_of((1 - side) * part_width, part_width), part_width)
        for ref, lanes in ((mine_ref, own), (other_ref, far)):
            for i in range(n):
                attn_ref[i * chosen : (i + 1) * chosen, lanes] = ref[i, :chosen]
            sum_all = ref[0, chosen:].astype(F32)
            for i in range(1, n):
                sum_all += ref[i, chosen:].astype(F32)
            sums_ref[:, lanes] = sum_all
        y = nt(attn_ref[...], out_ref[...]).astype(BF16)
        y_ref[...] = y
        for h in range(heads):
            cols = slice(h * dim, (h + 1) * dim)
            read = keep_ref[:, :, width + local + h * dim : width + local + (h + 1) * dim]
            read = read.reshape(total, dim).astype(F32)
            grad = y[:, cols].astype(F32)
            r = unit_rows(read)
            back = r * (grad - read * (r * r) * jnp.mean(grad * read, -1, keepdims=True))
            read_ref[:, cols] = (back * (1.0 / hashes)).astype(BF16)
        dense = jnp.zeros((window, local), F32)
        for step in (-1, 0, 1):
            source = jnp.clip(me + step, 0, n - 1)
            inside = jnp.logical_and(me + step >= 0, me + step < n)
            there = y_ref[pl.ds(pl.multiple_of(source * chosen, chosen), chosen)]
            spots = codes_ref[source][:, codes_rows : codes_rows + 1].astype(F32).astype(I32)
            spots = jnp.where(inside, spots + step * tokens + half, -1)
            place = one_zero(spots == iota((chosen, window), 1))
            dense += tn(place, there)
        dense_low = dense.astype(BF16)
        dense_ref[...] = dense_low
        twice = jnp.concatenate([dense_low, dense_low], axis=0)
        for h in range(heads):
            cols = slice(h * dim, (h + 1) * dim)
            grad = tn(count_ref[h], read_ref[:, cols]) + nn(band_ref[h], twice[:, cols])
            grad_ref[:, cols] = grad.astype(BF16)

    grad_values, dense, attn_all, vectors = call(
        values_body,
        [((tokens, local), BF16), ((window, local), BF16), ((total, width), BF16), ((16, width), F32)],
        (ids, attn_mine, attn_other, out_weight, keeps, counts, back_bands, all_codes),
        "values_back",
        smem=1,
        scratch=[pltpu.VMEM((total, local), BF16), pltpu.VMEM((total, local), BF16)],
    )
    grads = [grad_values] + others(grad_values)

    share = local // n
    extra = 8

    def value_grad_body(inputs_ref, grad_ref, dense_ref, near_ref, send_ref, row_ref):
        grad = grad_ref[...]
        weight = tn(grad, inputs_ref[...]).astype(BF16)
        row_ref[...] = jnp.zeros_like(row_ref)
        row_ref[:1, :local] = column_sum(grad.astype(F32))
        turn = one_zero(iota((tokens, tokens), 0) + iota((tokens, tokens), 1) == tokens - 1)
        turned = nn(turn, dense_ref[half : half + tokens]).astype(BF16)
        for h in range(heads):
            cols = slice(h * dim, (h + 1) * dim)
            both = nt(turned[:, cols], near_ref[:, cols])
            aligned = pltpu.roll(both, window - tokens + 1, 1, stride=1, stride_axis=0)
            row_ref[1 + h : 2 + h, :128] = column_sum(aligned)[:, :128]
        for i in range(n):
            send_ref[i, :share] = weight[i * share : (i + 1) * share]
            send_ref[i, share:] = row_ref[...].astype(BF16)

    (value_part,) = call(
        value_grad_body,
        ((n, share + extra, width), BF16),
        (inputs, grad_values, dense, near),
        "value_grad",
        scratch=[pltpu.VMEM((extra, width), F32)],
    )
    value_part = exchange(value_part)

    def value_sum_body(part_ref, send_ref, row_ref):
        whole = part_ref[0].astype(F32)
        for i in range(1, n):
            whole += part_ref[i].astype(F32)
        for i in range(n):
            send_ref[i] = whole[:share].astype(BF16)
        row_ref[...] = whole[share:]

    value_send_back, value_rows = call(
        value_sum_body,
        [((n, share, width), BF16), ((extra, width), F32)],
        (value_part,),
        "value_sums",
    )
    value_grad = exchange(value_send_back).reshape(local, width).astype(F32).T

    def input_body(ids_ref, *refs):
        grad_refs, refs = refs[:tp], refs[tp:]
        weight_ref, order_ref, hidden_ref, out_ref = refs
        mine = ids_ref[1]
        pick = order_ref[:chosen]
        parts = split3(hidden_ref[...])
        placed = tn(pick, parts[0]) + tn(pick, parts[1]) + tn(pick, parts[2])
        terms = [nn(ref[...], weight_ref[mine ^ k]) for k, ref in enumerate(grad_refs)]
        out_ref[...] = placed + paired(terms)

    (input_grad,) = call(
        input_body,
        ((tokens, width), F32),
        (ids, *grads, value_all, order, grad_hidden),
        "input_grad",
        smem=1,
    )

    step_rows = chosen

    def weights_body(keep_ref, down_ref, up_w_ref, up_bias_ref, down_w_ref,
                     up_ref, up_sum_ref, grad_ref, act_ref, pre_ref):
        up_sum_ref[...] = jnp.zeros_like(up_sum_ref)

        @pl.loop(0, n)
        def _(i):
            rows = pl.ds(pl.multiple_of(i * step_rows, step_rows), step_rows)
            pre = nn(keep_ref[i, :, :width], up_w_ref[...]) + up_bias_ref[...]
            cdf = cdf_of(pre)
            act_ref[rows] = (pre * cdf).astype(BF16)
            slope = cdf + pre * jnp.exp(-0.5 * pre * pre) * 0.3989422804014327
            grad_pre = (nt(down_ref[i, :, :width], down_w_ref[...]) * slope).astype(BF16)
            pre_ref[rows] = grad_pre
            up_sum_ref[:1] += column_sum(grad_pre.astype(F32))

        first_low = keep_ref[:, :, :width].reshape(total, width)
        up_ref[...] = tn(first_low, pre_ref[...])
        grad_ref[...] = tn(act_ref[...], down_ref[:, :, :width].reshape(total, width))

    grad_up, up_sum, grad_down = call(
        weights_body,
        [((width, hidden_units), F32), ((8, hidden_units), F32), ((hidden_units, width), F32)],
        (keeps, down_all, up_weight, row(up_bias), down_weight),
        "weights",
        scratch=[pltpu.VMEM((total, hidden_units), BF16), pltpu.VMEM((total, hidden_units), BF16)],
    )

    def out_grad_body(keep_ref, attn_ref, out_ref):
        context_all = keep_ref[:, :, width : width + local].reshape(total, local)
        out_ref[...] = tn(context_all, attn_ref[...])

    (grad_out,) = call(out_grad_body, ((local, width), F32), (keeps, attn_all), "out_grad")

    def rest_body(codes_ref, keys_ref, wide_ref, tall_ref, band_ref, near_ref, context_ref,
                  count_ref, sum_ref):
        queries = query_words(codes_ref[...], wide_ref[...])
        sum_ref[...] = jnp.zeros_like(sum_ref)

        @pl.loop(0, n)
        def _(i):
            block = keys_ref[i]
            keys = key_words(block[:codes_rows], tall_ref[...])
            for h in range(heads):
                for c in range(0, tokens, 128):
                    count_ref[:, c : c + 128] = matches(queries, keys[:, c : c + 128], h)
                turned = block[codes_rows + h * dim : codes_rows + (h + 1) * dim]
                sum_ref[:, h * dim : (h + 1) * dim] += nt(count_ref[...], turned)

        near = near_ref[...]
        twice = jnp.concatenate([near, near], axis=0)
        for h in range(heads):
            cols = slice(h * dim, (h + 1) * dim)
            mine = sum_ref[:, cols] * (1.0 / hashes)
            conv = nn(band_ref[h, chosen:], twice[:, cols])
            context_ref[:, cols] = (mine * unit_rows(mine) + conv).astype(BF16)

    (rest_context,) = call(
        rest_body,
        ((rest, local), BF16),
        (rest_codes, all_keys, wide, tall, bands, near),
        "rest_context",
        scratch=[pltpu.VMEM((rest, tokens), BF16), pltpu.VMEM((rest, local), F32)],
    )
    rest_contexts = [rest_context] + others(rest_context)

    def rest_first_body(ids_ref, *refs):
        context_refs, refs = refs[:tp], refs[tp:]
        (out_ref, inputs_ref, bias_ref, gain_ref, shift_ref, up_ref, up_bias_ref, down_ref), refs = (
            refs[:8], refs[8:])
        send_refs, (first_ref, all_ref, part_ref) = refs[:tp], refs[tp:]
        mine = ids_ref[1]
        hidden = inputs_ref[chosen:].astype(F32) + joined(ids_ref, context_refs, out_ref) + bias_ref[...]
        unit, _ = norm_stats(hidden)
        first = unit * gain_ref[...] + shift_ref[...]
        all_ref[...] = first
        part_ref[...] = feed(first.astype(BF16), up_ref, up_bias_ref, down_ref)[1]
        for k in range(tp):
            rows = pl.ds(pl.multiple_of((mine ^ k) * piece, piece), piece)
            send_refs[k][...] = part_ref[rows]
        first_ref[...] = all_ref[pl.ds(pl.multiple_of(mine * piece, piece), piece)]

    *rest_parts, rest_first = call(
        rest_first_body,
        [((piece, width), BF16)] * tp + [((piece, width), F32)],
        (ids, *rest_contexts, out_all, sorted_inputs, row(out_bias), row(first_gain), row(first_shift),
         up_weight, row(up_bias), down_weight),
        "rest_first",
        smem=1,
        scratch=[pltpu.VMEM((rest, width), F32), pltpu.VMEM((rest, width), BF16)],
    )
    rest_parts = [rest_parts[0]] + [swap(rest_parts[k], k) for k in range(1, tp)]

    def rest_second_body(*refs):
        part_refs, (first_ref, bias_ref, gain_ref, shift_ref, out_ref) = refs[:tp], refs[tp:]
        second = first_ref[...] + paired([r[...].astype(F32) for r in part_refs]) + bias_ref[...]
        unit, _ = norm_stats(second)
        out_ref[...] = (unit * gain_ref[...] + shift_ref[...]).astype(BF16)

    (rest_out,) = call(
        rest_second_body,
        ((piece, width), BF16),
        (*rest_parts, rest_first, row(down_bias), row(second_gain), row(second_shift)),
        "rest_second",
    )
    rest_outs = [rest_out] + others(rest_out)

    def output_body(ids_ref, *refs):
        out_refs, (chosen_ref, order_ref, out_ref, sorted_ref) = refs[:tp], refs[tp:]
        mine = ids_ref[1]
        sorted_ref[:chosen] = chosen_ref[...]
        for k in range(tp):
            rows = pl.ds(pl.multiple_of(chosen + (mine ^ k) * piece, 16), piece)
            sorted_ref[rows] = out_refs[k][...]
        out_ref[...] = tn(order_ref[...], sorted_ref[...]).astype(BF16)

    (output,) = call(
        output_body,
        ((tokens, width), BF16),
        (ids, *rest_outs, out_chosen, order),
        "output",
        smem=1,
        scratch=[pltpu.VMEM((tokens, width), BF16)],
    )
    return (
        output,
        input_grad,
        value_grad,
        value_rows[0, :local],
        grad_out,
        vectors[5],
        vectors[3],
        vectors[4],
        grad_up,
        up_sum[0],
        grad_down,
        vectors[2],
        vectors[0],
        vectors[1],
        value_rows[1 : 1 + heads, :taps],
    )


def solution(mesh):
    return jax.shard_map(
        per_device,
        mesh=mesh,
        in_specs=(
            P("seq", None),
            P(None, "tp"),
            P("tp"),
            P("tp", None),
            P(),
            P(),
            P(),
            P(None, "tp"),
            P("tp"),
            P("tp", None),
            P(),
            P(),
            P(),
            P("tp", None),
            P("seq", "tp", None),
            P("seq", "tp", None),
            P("seq"),
            P("seq", None),
        ),
        out_specs=(
            P("seq", None),
            P("seq", None),
            P(None, "tp"),
            P("tp"),
            P("tp", None),
            P(),
            P(),
            P(),
            P(None, "tp"),
            P("tp"),
            P("tp", None),
            P(),
            P(),
            P(),
            P("tp", None),
        ),
        check_vma=False,
    )
```

time: 751 us -> 243 us (0.32)
  blocking collectives: 286 us -> 23.6 us
  waiting for transfers between devices: 316 us -> 54.8 us
  matrix products: 77.2 us -> 0 us
  local copies, waits for them, and re-layouts: 18.1 us -> 68 us
  Pallas kernels: 0 us -> 44.7 us
  other arithmetic: 26 us -> 1.89 us
  starting transfers between devices: 11.2 us -> 33.2 us
    psum x6 -> x0, waiting for transfers between devices: 311 us -> none  [the longest x1 108 us: per_device(): lax.psum(shortened(grad_tables), 'seq')]
    psum x2 -> x0, blocking collectives: 286 us -> none  [the longest x1 248 us: per_device(): tables_low = lax.psum(tables, 'seq').astype(jnp.bfloat16)]
    dot_general x24 -> x0, matrix products: 61.5 us -> none  [the longest x6 22.5 us: build_one_head(): jnp.einsum('rmb,rc->mbc', one_hot(operands[1]), operands[0], preferred_el...]
    unnamed x100 -> x194, local copies, waits for them, and re-layouts: 3.2 us -> 58.6 us
    pallas_call x0 -> x20, Pallas kernels: none -> 44.7 us  [call(): pl.pallas_call(body, out_shape=shapes, in_specs=specs, out_specs=[pl.Bloc...]
    all_to_all x0 -> x4, waiting for transfers between devices: none -> 28.6 us  [exchange(): return lax.all_to_all(array, 'seq', 0, 0)]
    all_to_all x0 -> x1, blocking collectives: none -> 23.6 us  [exchange(): return lax.all_to_all(array, 'seq', 0, 0)]
    all_to_all x0 -> x4, starting transfers between devices: none -> 19.2 us  [exchange(): return lax.all_to_all(array, 'seq', 0, 0)]
  transfers between devices with their start and end apart: 10 -> 31, of which waited for: 8 -> 15; matrix products, arithmetic and copies ran while one was open for 8% -> 4% of each run, Pallas kernels for 0% -> 18%
where the time goes in v1:
time: 243 us; the launch traced here: 241 us
  local copies, waits for them, and re-layouts  68 us (28%)
  waiting for transfers between devices  54.8 us (23%)
  Pallas kernels  44.7 us (18%)
  starting transfers between devices  33.2 us (14%)
  blocking collectives  23.6 us (10%)
  between operations  14.3 us (6%)
    unnamed x194, local copies, waits for them, and re-layouts  58.6 us
    pallas_call x20, Pallas kernels, call(): pl.pallas_call(body, out_shape=shapes, in_specs=specs, out_specs=[pl.Bloc...  44.7 us
    all_to_all x4, waiting for transfers between devices, exchange(): return lax.all_to_all(array, 'seq', 0, 0)  28.6 us
    all_to_all x1, blocking collectives, exchange(): return lax.all_to_all(array, 'seq', 0, 0)  23.6 us
    ppermute x22, waiting for transfers between devices, swap(): return lax.ppermute(array, 'tp', [(i, i ^ k) for i in range(tp)])  23.2 us
    all_to_all x4, starting transfers between devices, exchange(): return lax.all_to_all(array, 'seq', 0, 0)  19.2 us
    ppermute x22, starting transfers between devices, swap(): return lax.ppermute(array, 'tp', [(i, i ^ k) for i in range(tp)])  13.8 us
  transfers between devices with their start and end apart: 31, of which 15 were waited for; matrix products, arithmetic and copies ran while one was open for 4% of the time, Pallas kernels for 18%

profile of v1, /device:TPU:0, one launch (start us, length us, event | category | flops | bytes accessed | tf_op | source)
XLA Modules:
  0.0 240.6 jit_solution(8588318782100187397)
XLA Ops:
  11.2 7.3 %all-to-all-start = ((bf16[8,64,128]{2,1,0:T(8,128)(2,1)}), bf16[8,64,128]{2,1,0:T(8,128)(2,1)S(1)}, u32[]{:S(2)}, u32[]{:S(2)}) async-start(bf16[8,64,128]{2,1,0:T(8,128)(2,1)} %get-tuple-element.59), calls=%async_computation | async-start | bytes 262144 | tf_op jit(solution)/shard_map/all_to_all | solution.py:170
  22.6 3.2 %all-to-all-done.codes_ref = bf16[8,64,128]{2,1,0:T(8,128)(2,1)S(1)} async-done(((bf16[8,64,128]{2,1,0:T(8,128)(2,1)}), bf16[8,64,128]{2,1,0:T(8,128)(2,1)S(1)}, u32[]{:S(2)}, u32[]{:S(2)}) %all-to-all-start) | async-done | bytes 131104 | tf_op jit(solution)/shard_map/all_to_all | solution.py:170
  25.8 4.3 %count.1 = (bf16[3,512,256]{2,1,0:T(8,128)(2,1)S(1)}, bf16[8,96,192]{2,1,0:T(8,128)(2,1)}) custom-call(s32[2]{0:T(128)S(1)} %pad_add_fusion.ids_ref, bf16[8,64,128]{2,1,0:T(8,128)(2,1)S(1)} %all-to-all-done.codes_ref, bf16[288,256]{1,0:T(8,128)(2,1)S(1)} %get-tuple-element.56.send_ref, bf16[256,192]{1,0:T(8,128)(2,1)S(1)} %get-tuple-element.60.value_ref, ...), custom_call_target="tpu_custom_call" | custom-call | tf_op jit(solution)/shard_map/count/pallas_call | solution.py:56
  31.0 3.6 %all-to-all-start.1 = ((bf16[8,96,192]{2,1,0:T(8,128)(2,1)}), bf16[8,96,192]{2,1,0:T(8,128)(2,1)S(1)}, u32[]{:S(2)}, u32[]{:S(2)}) async-start(bf16[8,96,192]{2,1,0:T(8,128)(2,1)} %get-tuple-element.61), calls=%async_computation.1 | async-start | bytes 786432 | tf_op jit(solution)/shard_map/all_to_all | solution.py:170
  36.4 8.7 %all-to-all-done.1.reads_ref = bf16[8,96,192]{2,1,0:T(8,128)(2,1)S(1)} async-done(((bf16[8,96,192]{2,1,0:T(8,128)(2,1)}), bf16[8,96,192]{2,1,0:T(8,128)(2,1)S(1)}, u32[]{:S(2)}, u32[]{:S(2)}) %all-to-all-start.1) | async-done | bytes 294944 | tf_op jit(solution)/shard_map/all_to_all | solution.py:170
  49.9 1.6 collective-permute-start.10
  68.7 1.7 first.1
  79.6 2.4 collective-permute-done.13.refs_2_
  91.1 3.4 %collective-permute-done.17.refs_3_ = bf16[64,768]{1,0:T(8,128)(2,1)S(1)} collective-permute-done((bf16[64,768]{1,0:T(8,128)(2,1)}, bf16[64,768]{1,0:T(8,128)(2,1)S(1)}, u32[]{:S(2)}, u32[]{:S(2)}) %collective-permute-start.17) | collective-permute-done | bytes 98336 | tf_op jit(solution)/shard_map/ppermute | solution.py:164
  94.4 2.2 collective-permute-done.16.refs_2_
  102.5 4.1 %all-to-all-start.2 = ((bf16[8,80,384]{2,1,0:T(8,128)(2,1)}), bf16[8,80,384]{2,1,0:T(8,128)(2,1)}, u32[]{:S(2)}, u32[]{:S(2)}) async-start(bf16[8,80,384]{2,1,0:T(8,128)(2,1)} %copy-done.40), calls=%async_computation.2 | async-start | bytes 983040 | tf_op jit(solution)/shard_map/all_to_all | solution.py:170
  107.2 16.8 %all-to-all-done.2.mine_ref = bf16[8,80,384]{2,1,0:T(8,128)(2,1)} async-done(((bf16[8,80,384]{2,1,0:T(8,128)(2,1)}), bf16[8,80,384]{2,1,0:T(8,128)(2,1)}, u32[]{:S(2)}, u32[]{:S(2)}) %all-to-all-start.2) | async-done | bytes 491552 | tf_op jit(solution)/shard_map/all_to_all | solution.py:170
  124.0 2.1 collective-permute-done.18.other_ref
  133.5 4.4 %values_back.1 = (bf16[256,192]{1,0:T(8,128)(2,1)}, bf16[384,192]{1,0:T(8,128)(2,1)S(1)}, bf16[512,768]{1,0:T(8,128)(2,1)S(1)}, f32[16,768]{1,0:T(8,128)S(1)}) custom-call(s32[2]{0:T(128)S(1)} %pad_add_fusion.ids_ref, bf16[8,80,384]{2,1,0:T(8,128)(2,1)} %all-to-all-done.2.mine_ref, bf16[8,80,384]{2,1,0:T(8,128)(2,1)S(1)} %copy-done.42, ...), custom_call_target="tpu_custom_call" | custom-call | tf_op jit(solution)/shard_map/values_back/pallas_call | solution.py:56
  137.9 1.7 value_grad.1
  139.6 23.6 %all_to_all.25.part_ref = bf16[8,32,768]{2,1,0:T(8,128)(2,1)S(1)} all-to-all(bf16[8,32,768]{2,1,0:T(8,128)(2,1)S(1)} %value_grad.1), channel_id=1, replica_groups=mesh['seq'=8,'tp'=4] {'seq'}, dimensions={0} | all-to-all | bytes 786432 | tf_op jit(solution)/shard_map/all_to_all | solution.py:170
  164.5 4.2 %all-to-all-start.4 = ((bf16[8,24,768]{2,1,0:T(8,128)(2,1)}), bf16[8,24,768]{2,1,0:T(8,128)(2,1)}, u32[]{:S(2)}, u32[]{:S(2)}) async-start(bf16[8,24,768]{2,1,0:T(8,128)(2,1)} %copy-done.45), calls=%async_computation.4 | async-start | bytes 589824 | tf_op jit(solution)/shard_map/all_to_all | solution.py:170
  173.8 10.2 %rest_context.1.refs_0_ = bf16[192,192]{1,0:T(8,128)(2,1)S(1)} custom-call(bf16[192,128]{1,0:T(8,128)(2,1)S(1)} %copy-done.71, bf16[8,288,256]{2,1,0:T(8,128)(2,1)S(1)} %bitcast.27, bf16[1024,256]{1,0:T(8,128)(2,1)S(1)} %copy-done.10, bf16[64,768]{1,0:T(8,128)(2,1)S(1)} %copy-done.44, bf16[3,256,768]{2,1,0:T(8,128)(2,1)S(1)} %get-tuple-element.58.band_ref, ...), custom_call_target="tpu_custom_call" | custom-call | tf_op jit(solution)/shard_map/rest_context/pallas_call | solution.py:56
  184.1 1.6 collective-permute-start.1
  185.9 3.2 %collective-permute-done.2.refs_3_ = bf16[192,192]{1,0:T(8,128)(2,1)S(1)} collective-permute-done((bf16[192,192]{1,0:T(8,128)(2,1)S(1)}, bf16[192,192]{1,0:T(8,128)(2,1)S(1)}, u32[]{:S(2)}, u32[]{:S(2)}) %collective-permute-start.2) | collective-permute-done | bytes 73760 | tf_op jit(solution)/shard_map/ppermute | solution.py:164
  189.1 2.1 collective-permute-done.1.refs_2_
  191.3 2.2 rest_first.1
  194.0 1.5 collective-permute-start.5
  195.5 3.3 %collective-permute-done.4.refs_2_ = bf16[48,768]{1,0:T(8,128)(2,1)S(1)} collective-permute-done((bf16[48,768]{1,0:T(8,128)(2,1)S(1)}, bf16[48,768]{1,0:T(8,128)(2,1)S(1)}, u32[]{:S(2)}, u32[]{:S(2)}) %collective-permute-start.4) | collective-permute-done | bytes 73760 | tf_op jit(solution)/shard_map/ppermute | solution.py:164
  200.2 1.8 collective-permute-start.7
  202.0 1.5 collective-permute-done.8.refs_3_
  203.5 2.4 collective-permute-done.7.refs_2_
  205.9 1.6 output.1
  211.8 8.7 %weights.1 = (f32[768,768]{1,0:T(8,128)}, f32[8,768]{1,0:T(8,128)S(1)}, f32[768,768]{1,0:T(8,128)}) custom-call(bf16[8,64,1152]{2,1,0:T(8,128)(2,1)S(1)} %bitcast.24, bf16[8,64,1024]{2,1,0:T(8,128)(2,1)S(1)} %bitcast.31, bf16[768,768]{1,0:T(8,128)(2,1)S(1)} %copy-done, f32[1,768]{1,0:T(1,128)S(1)} %reshape.83.refs_10_.up_bias_ref, bf16[768,768]{1,0:T(8,128)(2,1)S(1)} %copy-done.1), custom_call_target="tpu_custom_call" | custom-call | tf_op jit(solution)/shard_map/weights/pallas_call | solution.py:56
  220.5 1.6 slice_reduce_fusion
  226.8 2.9 %input_grad.1 = f32[256,768]{1,0:T(8,128)} custom-call(s32[2]{0:T(128)S(1)} %pad_add_fusion.ids_ref, bf16[256,192]{1,0:T(8,128)(2,1)} %get-tuple-element.84.refs_0_.grad_ref, bf16[256,192]{1,0:T(8,128)(2,1)} %collective-permute-done.19.refs_1_, bf16[256,192]{1,0:T(8,128)(2,1)} %collective-permute-done.20.refs_2_, ...), custom_call_target="tpu_custom_call" | custom-call | tf_op jit(solution)/shard_map/input_grad/pallas_call | solution.py:56
  232.2 1.8 convert_bitcast_fusion
  (263 shorter events, 84.9 us)
Async XLA Ops:
  7.2 54.6 %all-gather.13.cloned.1.call-start = ((), (), s32[]{:S(2)}) async-start(), calls=%async_computation.6 | async-start | bytes 1474560 | tf_op jit(solution)/shard_map/all_gather | solution.py:218
  11.2 14.6 %all-to-all-start = ((bf16[8,64,128]{2,1,0:T(8,128)(2,1)}), bf16[8,64,128]{2,1,0:T(8,128)(2,1)S(1)}, u32[]{:S(2)}, u32[]{:S(2)}) async-start(bf16[8,64,128]{2,1,0:T(8,128)(2,1)} %get-tuple-element.59), calls=%async_computation | async-start | bytes 262144 | tf_op jit(solution)/shard_map/all_to_all | solution.py:170
  31.0 14.1 %all-to-all-start.1 = ((bf16[8,96,192]{2,1,0:T(8,128)(2,1)}), bf16[8,96,192]{2,1,0:T(8,128)(2,1)S(1)}, u32[]{:S(2)}, u32[]{:S(2)}) async-start(bf16[8,96,192]{2,1,0:T(8,128)(2,1)} %get-tuple-element.61), calls=%async_computation.1 | async-start | bytes 786432 | tf_op jit(solution)/shard_map/all_to_all | solution.py:170
  34.6 92.3 %all-gather.15.cloned.1.call-start = ((), (), s32[]{:S(2)}) async-start(), calls=%async_computation.7 | async-start | bytes 1327104 | tf_op jit(solution)/shard_map/all_gather | solution.py:368
  49.9 10.1 %collective-permute-start.11 = (bf16[64,192]{1,0:T(8,128)(2,1)S(1)}, bf16[64,192]{1,0:T(8,128)(2,1)S(1)}, u32[]{:S(2)}, u32[]{:S(2)}) collective-permute-start(bf16[64,192]{1,0:T(8,128)(2,1)S(1)} %get-tuple-element.69.refs_0_), channel_id=1, source_target_pairs={{0,3},{1,2},{2,1},{3,0},{4,7},{5,6},{6,5},{7,4},{8,11},{9,10},{10,... | collective-permute-start | bytes 73736 | tf_op jit(solution)/shard_map/ppermute | solution.py:164
  49.9 10.8 %collective-permute-start.10 = (bf16[64,192]{1,0:T(8,128)(2,1)S(1)}, bf16[64,192]{1,0:T(8,128)(2,1)S(1)}, u32[]{:S(2)}, u32[]{:S(2)}) collective-permute-start(bf16[64,192]{1,0:T(8,128)(2,1)S(1)} %get-tuple-element.69.refs_0_), channel_id=1, source_target_pairs={{0,2},{1,3},{2,0},{3,1},{4,6},{5,7},{6,4},{7,5},{8,10},{9,11},{10,... | collective-permute-start | bytes 73736 | tf_op jit(solution)/shard_map/ppermute | solution.py:164
  51.4 9.8 %collective-permute-start.9 = (bf16[64,192]{1,0:T(8,128)(2,1)S(1)}, bf16[64,192]{1,0:T(8,128)(2,1)S(1)}, u32[]{:S(2)}, u32[]{:S(2)}) collective-permute-start(bf16[64,192]{1,0:T(8,128)(2,1)S(1)} %get-tuple-element.69.refs_0_), channel_id=1, source_target_pairs={{0,1},{1,0},{2,3},{3,2},{4,5},{5,4},{6,7},{7,6},{8,9},{9,8},{10,11... | collective-permute-start | bytes 73736 | tf_op jit(solution)/shard_map/ppermute | solution.py:164
  73.7 95.1 %all-gather.11.cloned.1.call-start = ((), (), s32[]{:S(2)}) async-start(), calls=%async_computation.5 | async-start | bytes 1327104 | tf_op jit(solution)/shard_map/all_gather | solution.py:217
  74.5 136.1 %all-gather.19.cloned.1.call-start = ((), (), s32[]{:S(2)}) async-start(), calls=%async_computation.9 | async-start | bytes 1179648 | tf_op jit(solution)/shard_map/all_gather | solution.py:415
  74.5 5.1 %collective-permute-start.14 = (bf16[64,768]{1,0:T(8,128)(2,1)}, bf16[64,768]{1,0:T(8,128)(2,1)S(1)}, u32[]{:S(2)}, u32[]{:S(2)}) collective-permute-start(bf16[64,768]{1,0:T(8,128)(2,1)} %copy-done.60), channel_id=1, source_target_pairs={{0,3},{1,2},{2,1},{3,0},{4,7},{5,6},{6,5},{7,4},{8,11},{9,10},{10,... | collective-permute-start | bytes 294920 | tf_op jit(solution)/shard_map/ppermute | solution.py:164
  75.7 6.3 %collective-permute-start.13 = (bf16[64,768]{1,0:T(8,128)(2,1)}, bf16[64,768]{1,0:T(8,128)(2,1)S(1)}, u32[]{:S(2)}, u32[]{:S(2)}) collective-permute-start(bf16[64,768]{1,0:T(8,128)(2,1)} %copy-done.60), channel_id=1, source_target_pairs={{0,2},{1,3},{2,0},{3,1},{4,6},{5,7},{6,4},{7,5},{8,10},{9,11},{10,... | collective-permute-start | bytes 294920 | tf_op jit(solution)/shard_map/ppermute | solution.py:164
  76.4 5.6 %collective-permute-start.12 = (bf16[64,768]{1,0:T(8,128)(2,1)}, bf16[64,768]{1,0:T(8,128)(2,1)S(1)}, u32[]{:S(2)}, u32[]{:S(2)}) collective-permute-start(bf16[64,768]{1,0:T(8,128)(2,1)} %copy-done.60), channel_id=1, source_target_pairs={{0,1},{1,0},{2,3},{3,2},{4,5},{5,4},{6,7},{7,6},{8,9},{9,8},{10,11... | collective-permute-start | bytes 294920 | tf_op jit(solution)/shard_map/ppermute | solution.py:164
  89.2 5.3 %collective-permute-start.17 = (bf16[64,768]{1,0:T(8,128)(2,1)}, bf16[64,768]{1,0:T(8,128)(2,1)S(1)}, u32[]{:S(2)}, u32[]{:S(2)}) collective-permute-start(bf16[64,768]{1,0:T(8,128)(2,1)} %copy-done.66), channel_id=1, source_target_pairs={{0,3},{1,2},{2,1},{3,0},{4,7},{5,6},{6,5},{7,4},{8,11},{9,10},{10,... | collective-permute-start | bytes 294920 | tf_op jit(solution)/shard_map/ppermute | solution.py:164
  90.3 6.4 %collective-permute-start.16 = (bf16[64,768]{1,0:T(8,128)(2,1)}, bf16[64,768]{1,0:T(8,128)(2,1)S(1)}, u32[]{:S(2)}, u32[]{:S(2)}) collective-permute-start(bf16[64,768]{1,0:T(8,128)(2,1)} %copy-done.66), channel_id=1, source_target_pairs={{0,2},{1,3},{2,0},{3,1},{4,6},{5,7},{6,4},{7,5},{8,10},{9,11},{10,... | collective-permute-start | bytes 294920 | tf_op jit(solution)/shard_map/ppermute | solution.py:164
  90.8 5.8 %collective-permute-start.15 = (bf16[64,768]{1,0:T(8,128)(2,1)}, bf16[64,768]{1,0:T(8,128)(2,1)S(1)}, u32[]{:S(2)}, u32[]{:S(2)}) collective-permute-start(bf16[64,768]{1,0:T(8,128)(2,1)} %copy-done.66), channel_id=1, source_target_pairs={{0,1},{1,0},{2,3},{3,2},{4,5},{5,4},{6,7},{7,6},{8,9},{9,8},{10,11... | collective-permute-start | bytes 294920 | tf_op jit(solution)/shard_map/ppermute | solution.py:164
  102.5 21.5 %all-to-all-start.2 = ((bf16[8,80,384]{2,1,0:T(8,128)(2,1)}), bf16[8,80,384]{2,1,0:T(8,128)(2,1)}, u32[]{:S(2)}, u32[]{:S(2)}) async-start(bf16[8,80,384]{2,1,0:T(8,128)(2,1)} %copy-done.40), calls=%async_computation.2 | async-start | bytes 983040 | tf_op jit(solution)/shard_map/all_to_all | solution.py:170
  106.7 117.1 %all-gather.17.cloned.1.call-start = ((), (), s32[]{:S(2)}) async-start(), calls=%async_computation.8 | async-start | bytes 1474560 | tf_op jit(solution)/shard_map/all_gather | solution.py:219
  124.0 2.1 collective-permute-start.18
  137.8 25.4 %copy-start.90 = (f32[16,768]{1,0:T(8,128)}, f32[16,768]{1,0:T(8,128)S(1)}, u32[]{:S(2)}) copy-start(f32[16,768]{1,0:T(8,128)S(1)} %get-tuple-element.90) | copy-start | bytes 147460
  164.5 67.7 %all-to-all-start.4 = ((bf16[8,24,768]{2,1,0:T(8,128)(2,1)}), bf16[8,24,768]{2,1,0:T(8,128)(2,1)}, u32[]{:S(2)}, u32[]{:S(2)}) async-start(bf16[8,24,768]{2,1,0:T(8,128)(2,1)} %copy-done.45), calls=%async_computation.4 | async-start | bytes 589824 | tf_op jit(solution)/shard_map/all_to_all | solution.py:170
  184.0 5.1 %collective-permute-start.2 = (bf16[192,192]{1,0:T(8,128)(2,1)S(1)}, bf16[192,192]{1,0:T(8,128)(2,1)S(1)}, u32[]{:S(2)}, u32[]{:S(2)}) collective-permute-start(bf16[192,192]{1,0:T(8,128)(2,1)S(1)} %rest_context.1.refs_0_), channel_id=1, source_target_pairs={{0,3},{1,2},{2,1},{3,0},{4,7},{5,6},{6,5},{7,4},{8,11},{9,10},{10,... | collective-permute-start | bytes 221192 | tf_op jit(solution)/shard_map/ppermute | solution.py:164
  184.1 7.2 %collective-permute-start.1 = (bf16[192,192]{1,0:T(8,128)(2,1)S(1)}, bf16[192,192]{1,0:T(8,128)(2,1)S(1)}, u32[]{:S(2)}, u32[]{:S(2)}) collective-permute-start(bf16[192,192]{1,0:T(8,128)(2,1)S(1)} %rest_context.1.refs_0_), channel_id=1, source_target_pairs={{0,2},{1,3},{2,0},{3,1},{4,6},{5,7},{6,4},{7,5},{8,10},{9,11},{10,... | collective-permute-start | bytes 221192 | tf_op jit(solution)/shard_map/ppermute | solution.py:164
  185.6 5.6 %collective-permute-start = (bf16[192,192]{1,0:T(8,128)(2,1)S(1)}, bf16[192,192]{1,0:T(8,128)(2,1)S(1)}, u32[]{:S(2)}, u32[]{:S(2)}) collective-permute-start(bf16[192,192]{1,0:T(8,128)(2,1)S(1)} %rest_context.1.refs_0_), channel_id=1, source_target_pairs={{0,1},{1,0},{2,3},{3,2},{4,5},{5,4},{6,7},{7,6},{8,9},{9,8},{10,11... | collective-permute-start | bytes 221192 | tf_op jit(solution)/shard_map/ppermute | solution.py:164
  193.5 1.9 collective-permute-start.3
  193.7 5.1 %collective-permute-start.4 = (bf16[48,768]{1,0:T(8,128)(2,1)S(1)}, bf16[48,768]{1,0:T(8,128)(2,1)S(1)}, u32[]{:S(2)}, u32[]{:S(2)}) collective-permute-start(bf16[48,768]{1,0:T(8,128)(2,1)S(1)} %get-tuple-element.66), channel_id=1, source_target_pairs={{0,2},{1,3},{2,0},{3,1},{4,6},{5,7},{6,4},{7,5},{8,10},{9,11},{10,... | collective-permute-start | bytes 221192 | tf_op jit(solution)/shard_map/ppermute | solution.py:164
  194.0 5.4 %collective-permute-start.5 = (bf16[48,768]{1,0:T(8,128)(2,1)S(1)}, bf16[48,768]{1,0:T(8,128)(2,1)S(1)}, u32[]{:S(2)}, u32[]{:S(2)}) collective-permute-start(bf16[48,768]{1,0:T(8,128)(2,1)S(1)} %get-tuple-element.67), channel_id=1, source_target_pairs={{0,3},{1,2},{2,1},{3,0},{4,7},{5,6},{6,5},{7,4},{8,11},{9,10},{10,... | collective-permute-start | bytes 221192 | tf_op jit(solution)/shard_map/ppermute | solution.py:164
  199.7 3.8 %collective-permute-start.8 = (bf16[48,768]{1,0:T(8,128)(2,1)S(1)}, bf16[48,768]{1,0:T(8,128)(2,1)S(1)}, u32[]{:S(2)}, u32[]{:S(2)}) collective-permute-start(bf16[48,768]{1,0:T(8,128)(2,1)S(1)} %rest_second.1.refs_0_), channel_id=1, source_target_pairs={{0,3},{1,2},{2,1},{3,0},{4,7},{5,6},{6,5},{7,4},{8,11},{9,10},{10,... | collective-permute-start | bytes 221192 | tf_op jit(solution)/shard_map/ppermute | solution.py:164
  200.2 5.7 %collective-permute-start.7 = (bf16[48,768]{1,0:T(8,128)(2,1)S(1)}, bf16[48,768]{1,0:T(8,128)(2,1)S(1)}, u32[]{:S(2)}, u32[]{:S(2)}) collective-permute-start(bf16[48,768]{1,0:T(8,128)(2,1)S(1)} %rest_second.1.refs_0_), channel_id=1, source_target_pairs={{0,2},{1,3},{2,0},{3,1},{4,6},{5,7},{6,4},{7,5},{8,10},{9,11},{10,... | collective-permute-start | bytes 221192 | tf_op jit(solution)/shard_map/ppermute | solution.py:164
  202.0 3.8 %collective-permute-start.6 = (bf16[48,768]{1,0:T(8,128)(2,1)S(1)}, bf16[48,768]{1,0:T(8,128)(2,1)S(1)}, u32[]{:S(2)}, u32[]{:S(2)}) collective-permute-start(bf16[48,768]{1,0:T(8,128)(2,1)S(1)} %rest_second.1.refs_0_), channel_id=1, source_target_pairs={{0,1},{1,0},{2,3},{3,2},{4,5},{5,4},{6,7},{7,6},{8,9},{9,8},{10,11... | collective-permute-start | bytes 221192 | tf_op jit(solution)/shard_map/ppermute | solution.py:164
  207.5 16.3 %collective-permute-start.21 = (bf16[256,192]{1,0:T(8,128)(2,1)}, bf16[256,192]{1,0:T(8,128)(2,1)}, u32[]{:S(2)}, u32[]{:S(2)}) collective-permute-start(bf16[256,192]{1,0:T(8,128)(2,1)} %get-tuple-element.84.refs_0_.grad_ref), channel_id=1, source_target_pairs={{0,3},{1,2},{2,1},{3,0},{4,7},{5,6},{6,5},{7,4},{8,11},{9,10},{10,... | collective-permute-start | bytes 294920 | tf_op jit(solution)/shard_map/ppermute | solution.py:164
  207.5 16.3 %collective-permute-start.20 = (bf16[256,192]{1,0:T(8,128)(2,1)}, bf16[256,192]{1,0:T(8,128)(2,1)}, u32[]{:S(2)}, u32[]{:S(2)}) collective-permute-start(bf16[256,192]{1,0:T(8,128)(2,1)} %get-tuple-element.84.refs_0_.grad_ref), channel_id=1, source_target_pairs={{0,2},{1,3},{2,0},{3,1},{4,6},{5,7},{6,4},{7,5},{8,10},{9,11},{10,... | collective-permute-start | bytes 294920 | tf_op jit(solution)/shard_map/ppermute | solution.py:164
  208.5 15.2 %collective-permute-start.19 = (bf16[256,192]{1,0:T(8,128)(2,1)}, bf16[256,192]{1,0:T(8,128)(2,1)}, u32[]{:S(2)}, u32[]{:S(2)}) collective-permute-start(bf16[256,192]{1,0:T(8,128)(2,1)} %get-tuple-element.84.refs_0_.grad_ref), channel_id=1, source_target_pairs={{0,1},{1,0},{2,3},{3,2},{4,5},{5,4},{6,7},{7,6},{8,9},{9,8},{10,11... | collective-permute-start | bytes 294920 | tf_op jit(solution)/shard_map/ppermute | solution.py:164
  (96 other events, 468.3 us)
Sparse Core Ops, SparseCore 0:
  9.6 20.1 all-gather.12
  73.9 42.5 all-gather.14
  118.6 45.4 all-gather.10
  166.2 39.3 all-gather.18
  207.0 16.7 all-gather.16

commit v2 on v1

v2 whole, which is shorter than its diff:
```python
from functools import partial

import jax
import jax.numpy as jnp
import numpy as np
from jax import lax
from jax.experimental import pallas as pl
from jax.experimental.pallas import tpu as pltpu
from jax.sharding import PartitionSpec as P

F32, BF16, I32 = jnp.float32, jnp.bfloat16, jnp.int32
MIB = 1 << 20
VMEM_MIB = 20


def dot(a, b, dims):
    return lax.dot_general(a, b, (dims, ((), ())), preferred_element_type=F32)


def nn(a, b):
    return dot(a, b, ((1,), (0,)))


def nt(a, b):
    return dot(a, b, ((1,), (1,)))


def tn(a, b):
    return dot(a, b, ((0,), (0,)))


def split2(x):
    high = x.astype(BF16)
    return high, (x - high.astype(F32)).astype(BF16)


def split3(x):
    high = x.astype(BF16)
    rest = x - high.astype(F32)
    middle = rest.astype(BF16)
    return high, middle, (rest - middle.astype(F32)).astype(BF16)


def iota(shape, dim):
    return lax.broadcasted_iota(I32, shape, dim)


def one_zero(condition):
    return jnp.where(condition, 1.0, 0.0).astype(BF16)


def call(body, outs, args, name, scratch=(), smem=0, far=(), far_out=(), late=(), early=(),
         after=(), us=1.0):
    shapes = [outs] if isinstance(outs, tuple) else outs
    count = len(args)
    arrays = [*args, *(jax.ShapeDtypeStruct(shape, dtype) for shape, dtype in shapes)]
    moved = [*far, *(count + i for i in far_out)]
    spaces = [
        pltpu.SMEM if i < smem else pltpu.HBM if i in moved else pltpu.VMEM for i in range(len(arrays))
    ]
    inner = [pltpu.VMEM(arrays[i].shape, arrays[i].dtype) for i in moved]
    extra = len(after)

    held = sum(
        int(np.prod(ref.shape)) * jnp.dtype(ref.dtype).itemsize for ref in (*inner, *scratch)
    )
    limit = max(VMEM_MIB * MIB, held + 12 * MIB)

    def kernel(*refs):
        refs = list(refs[:count] + refs[count + extra :])
        given, here, rest = refs[: len(arrays)], refs[len(arrays) :][: len(inner)], refs[len(arrays) + len(inner) :]
        copies = []
        for slot, i in enumerate(moved):
            pair = (refs[i], here[slot]) if i < count else (here[slot], refs[i])
            copies.append(pltpu.make_async_copy(*pair, rest[-1].at[slot]))
            given[i] = here[slot]
        for copy in copies[: len(far)]:
            copy.start()
        for i, copy in zip(far, copies):
            if i not in late:
                copy.wait()

        def ready():
            for i, copy in zip(far, copies):
                if i in late:
                    copy.wait()

        sends = dict(zip(far_out, copies[len(far) :]))

        def finish(i):
            sends[i].start()

        options = {"ready": ready} if late else {}
        if early:
            options["finish"] = finish
        body(*given, *(rest[:-1] if moved else rest), **options)
        for i in sends:
            if i not in early:
                finish(i)
        for copy in sends.values():
            copy.wait()

    placed = [
        a if i < smem else pltpu.with_memory_space_constraint(a, spaces[i]) for i, a in enumerate(args)
    ]
    return pl.pallas_call(
        kernel,
        out_shape=[spaces[i](arrays[i].shape, arrays[i].dtype) for i in range(count, len(arrays))],
        in_specs=[pl.BlockSpec(memory_space=space) for space in spaces[:count]]
        + [pl.BlockSpec(memory_space=space) for _, space in after],
        out_specs=[pl.BlockSpec(memory_space=space) for space in spaces[count:]],
        scratch_shapes=[*inner, *scratch, *([pltpu.SemaphoreType.DMA((len(inner),))] if moved else [])],
        compiler_params=pltpu.CompilerParams(vmem_limit_bytes=limit),
        cost_estimate=pl.CostEstimate(
            flops=int(us * 1.1e9), bytes_accessed=0, transcendentals=0
        ),
        name=name,
    )(*placed, *(pltpu.with_memory_space_constraint(*pair) for pair in after))


def line(ref):
    return ref[...].reshape(1, ref.shape[0])


def norm_stats(rows):
    centre = rows - jnp.mean(rows, -1, keepdims=True)
    spread = jnp.mean(centre * centre, -1, keepdims=True)
    q = lax.rsqrt(spread + 1e-05)
    return centre * q, q


def cdf_of(u):
    return 0.5 * (1.0 + lax.erf(u * 0.7071067811865476))


def gelu_grad(u):
    return cdf_of(u) + u * jnp.exp(-0.5 * u * u) * 0.3989422804014327


def plane_weights(heads, hashes):
    lanes = 128
    rows = heads * hashes
    wide = np.zeros((8 * lanes, 2 * lanes), np.float32)
    tall = np.zeros((64, 8 * rows), np.float32)
    for b in range(8):
        for h in range(heads):
            for m in range(hashes):
                half, power = divmod(m, 16)
                wide[b * lanes + h * hashes + m, half * lanes + h * 8 + b] = 2.0**power
                tall[half * 32 + h * 8 + b, b * rows + h * hashes + m] = 2.0**power
    return jnp.asarray(wide, BF16), jnp.asarray(tall, BF16)


def query_words(codes, wide):
    whole = codes.astype(F32).astype(I32)
    bits = jnp.concatenate(
        [((whole >> b) & 1).astype(F32).astype(BF16) for b in range(8)], axis=1
    )
    both = nn(bits, wide)
    return both[:, :128].astype(I32) | (both[:, 128:].astype(I32) << 16)


def key_words(codes, tall):
    whole = codes.astype(F32).astype(I32)
    bits = jnp.concatenate(
        [((whole >> b) & 1).astype(F32).astype(BF16) for b in range(8)], axis=0
    )
    both = nn(tall, bits)
    return both[:32].astype(I32) | (both[32:].astype(I32) << 16)


def matches(query_block, key_block, head):
    apart = None
    for b in range(8):
        word = head * 8 + b
        unlike = query_block[:, word : word + 1] ^ key_block[word : word + 1, :]
        apart = unlike if apart is None else apart | unlike
    return (32 - lax.population_count(apart)).astype(F32).astype(BF16)


def per_device(
    inputs,
    value_weight,
    value_bias,
    out_weight,
    out_bias,
    first_gain,
    first_shift,
    up_weight,
    up_bias,
    down_weight,
    down_bias,
    second_gain,
    second_shift,
    conv_weight,
    query_codes,
    key_codes,
    masked,
    out_grad,
):
    n = lax.axis_size("seq")
    tp = lax.axis_size("tp")
    tokens, width = inputs.shape
    heads, hashes = query_codes.shape[1], query_codes.shape[2]
    taps = conv_weight.shape[1]
    half = (taps - 1) // 2
    local = value_weight.shape[1]
    dim = local // heads
    units = up_weight.shape[1]
    chosen = tokens // 4
    rest = tokens - chosen
    piece = rest // tp
    part_rows = chosen // tp
    part_width = width // 2
    codes_rows = heads * hashes
    window = tokens + 128
    total = n * chosen
    ids = jnp.stack([lax.axis_index("seq"), lax.axis_index("tp")]).astype(I32)
    wide, tall = plane_weights(heads, hashes)

    previous = []

    def run(*args, also=(), **options):
        results = call(*args, after=(*previous, *also), **options)
        previous[:] = [(results[0], pltpu.HBM if 0 in options.get("far_out", ()) else pltpu.VMEM)]
        return results

    def swap(array, k):
        return lax.ppermute(array, "tp", [(i, i ^ k) for i in range(tp)])

    def others(array):
        return [swap(array, k) for k in range(1, tp)]

    def exchange(array):
        return lax.all_to_all(array, "seq", 0, 0)

    query_t = jnp.transpose(query_codes, (1, 2, 0)).reshape(codes_rows, tokens)
    key_t = jnp.transpose(key_codes, (1, 2, 0)).reshape(codes_rows, tokens)
    value_t = value_weight.T
    out_all = [out_weight] + others(out_weight)
    value_all = [value_t] + others(value_t)

    def order_body(masked_ref, query_ref, chosen_ref, rest_ref, order_ref):
        flags = jnp.broadcast_to(line(masked_ref).astype(F32), (8, tokens))
        upto = one_zero(iota((tokens, tokens), 0) <= iota((tokens, tokens), 1))
        count = nn(flags.astype(BF16), upto)
        spot = iota((8, tokens), 1).astype(F32)
        target = jnp.where(flags > 0, count - 1.0, count[:, tokens - 1 :] + spot - count)
        order = one_zero(iota((tokens, tokens), 0) == target[:1].astype(I32))
        order_ref[...] = order
        where = jnp.where(
            iota((128 - codes_rows, tokens), 0) == 0, iota((128 - codes_rows, tokens), 1), 0
        )
        table = jnp.concatenate([query_ref[...], where], axis=0).astype(F32).astype(BF16)
        sorted_codes = nt(order, table).astype(BF16)
        for i in range(n):
            chosen_ref[i] = sorted_codes[:chosen]
        rest_ref[...] = sorted_codes[chosen:]

    chosen_codes, rest_codes, order = run(
        order_body,
        [((n, chosen, 128), BF16), ((rest, 128), BF16), ((tokens, tokens), BF16)],
        (masked, query_t),
        "order",
        far=(0, 1),
        far_out=(1, 2),
        us=2,
    )
    all_codes = exchange(chosen_codes)

    def prepare_body(inputs_ref, weight_ref, bias_ref, key_ref, order_ref, grad_ref, masked_ref, conv_ref,
                     value_ref, send_ref, top_ref, low_ref, cot_ref, band_ref, low_band_ref, back_ref,
                     pad_ref):
        values = (nt(inputs_ref[...], weight_ref[...]) + line(bias_ref)).astype(BF16)
        value_ref[...] = values
        same = one_zero(iota((local, local), 0) == iota((local, local), 1))
        send_ref[:codes_rows] = key_ref[...].astype(F32).astype(BF16)
        send_ref[codes_rows:] = nt(same, values).astype(BF16)
        order = order_ref[...]
        moved = nn(order, inputs_ref[...]).astype(BF16)
        top_ref[...] = moved[:chosen]
        low_ref[...] = moved[chosen:]
        pick = order_ref[:chosen]
        flags = jnp.broadcast_to(line(masked_ref).astype(F32), (8, tokens)).astype(BF16)
        valid = nt(pick, flags)[:, :1]
        parts = split3(grad_ref[...])
        cot_ref[...] = (nn(pick, parts[0]) + nn(pick, parts[1]) + nn(pick, parts[2])) * valid
        pad_ref[...] = jnp.zeros_like(pad_ref)
        pad_ref[:heads, :taps] = conv_ref[...]
        turn = one_zero(iota((128, 128), 0) + iota((128, 128), 1) == taps - 1)
        padded = pad_ref[...]
        parts = split3(padded)
        turned = nn(parts[0], turn) + nn(parts[1], turn) + nn(parts[2], turn)
        blank = jnp.zeros((8, window - 128), F32)
        for h in range(heads):
            for ahead, source in ((True, padded), (False, turned)):
                long = jnp.concatenate([source, blank], axis=1)
                spread = jnp.broadcast_to(long[h : h + 1], (tokens, window))
                band = pltpu.roll(spread, 0, 1, stride=1, stride_axis=0)
                for at, level in zip((0, window), split2(band)):
                    if ahead:
                        moved = nn(order, level).astype(BF16)
                        band_ref[h, :, at : at + window] = moved[:chosen]
                        low_band_ref[h, :, at : at + window] = moved[chosen:]
                    else:
                        back_ref[h, :, at : at + window] = level

    values, value_send, top_inputs, low_inputs, cot, bands, low_bands, back_bands = run(
        prepare_body,
        [((tokens, local), BF16), ((codes_rows + local, tokens), BF16), ((chosen, width), BF16),
         ((rest, width), BF16), ((chosen, width), F32), ((heads, chosen, 2 * window), BF16),
         ((heads, rest, 2 * window), BF16), ((heads, tokens, 2 * window), BF16)],
        (inputs, value_t, value_bias, key_t, order, out_grad, masked, conv_weight),
        "prepare",
        far=tuple(range(8)),
        far_out=(0, 2, 3, 4, 5, 6, 7),
        scratch=[pltpu.VMEM((8, 128), F32)],
        us=4,
    )
    all_keys = lax.all_gather(value_send, "seq", axis=0)

    def count_body(ids_ref, codes_ref, send_ref, value_ref, wide_ref, tall_ref, count_ref, out_ref, finish):
        me = ids_ref[0]
        keys = key_words(send_ref[:codes_rows], tall_ref[...])
        queries = query_words(codes_ref[...].reshape(total, 128), wide_ref[...])
        for h in range(heads):
            for r in range(0, total, tokens):
                for c in range(0, tokens, 128):
                    count_ref[h, r : r + tokens, c : c + 128] = matches(
                        queries[r : r + tokens], keys[:, c : c + 128], h
                    )
        finish(0)
        for h in range(heads):
            turned = send_ref[codes_rows + h * dim : codes_rows + (h + 1) * dim]
            read = nt(count_ref[h], turned).astype(BF16)
            for i in range(n):
                out_ref[i, :chosen, h * dim : (h + 1) * dim] = read[i * chosen : (i + 1) * chosen]
        for i in range(n):
            last, head_rows = value_ref[tokens - half :], value_ref[:half]
            rows = jnp.where(i == me + 1, last.astype(F32), head_rows.astype(F32))
            out_ref[i, chosen:] = rows.astype(BF16)

    counts, reads = run(
        count_body,
        [((heads, total, tokens), BF16), ((n, chosen + half, local), BF16)],
        (ids, all_codes, value_send, values, wide, tall),
        "count",
        far=(3, 4, 5),
        far_out=(0,),
        early=(0,),
        smem=1,
        us=5,
    )
    reads = exchange(reads)

    def unit_rows(value_sum):
        return lax.rsqrt(jnp.mean(value_sum * value_sum, -1, keepdims=True) + 1e-05)

    def context_body(ids_ref, reads_ref, value_ref, band_ref, context_ref, sum_ref, near_ref):
        me = ids_ref[0]
        total_read = reads_ref[0, :chosen].astype(F32)
        for i in range(1, n):
            total_read += reads_ref[i, :chosen].astype(F32)
        total_read = total_read * (1.0 / hashes)
        sum_ref[...] = total_read
        before = reads_ref[jnp.maximum(me - 1, 0), chosen:].astype(F32)
        after = reads_ref[jnp.minimum(me + 1, n - 1), chosen:].astype(F32)
        near_ref[:half] = jnp.where(me > 0, before, 0.0).astype(BF16)
        near_ref[half : half + tokens] = value_ref[...]
        near_ref[half + tokens : 2 * half + tokens] = jnp.where(me < n - 1, after, 0.0).astype(BF16)
        near_ref[2 * half + tokens :] = jnp.zeros((window - tokens - 2 * half, local), BF16)
        near = near_ref[...]
        twice = jnp.concatenate([near, near], axis=0)
        for h in range(heads):
            cols = slice(h * dim, (h + 1) * dim)
            mine = total_read[:, cols]
            conv = nn(band_ref[h], twice[:, cols])
            context_ref[:, cols] = (mine * unit_rows(mine) + conv).astype(BF16)

    context, value_sum, near = run(
        context_body,
        [((chosen, local), BF16), ((chosen, local), F32), ((window, local), BF16)],
        (ids, reads, values, bands),
        "context",
        far=(2, 3),
        far_out=(2,),
        smem=1,
        us=2,
    )
    contexts = [context] + others(context)

    def paired(terms):
        while len(terms) > 1:
            terms = [terms[i] + terms[i + 1] for i in range(0, len(terms), 2)]
        return terms[0]

    def joined(context_refs, out_refs):
        return paired([nn(a[...], b[...]) for a, b in zip(context_refs, out_refs)])

    def feed(low, up_ref, up_bias_ref, down_ref):
        pre = nn(low, up_ref[...]) + line(up_bias_ref)
        act = (pre * cdf_of(pre)).astype(BF16)
        return pre, nn(act, down_ref[...]).astype(BF16)

    def first_body(*refs, ready, finish):
        context_refs, out_refs, refs = refs[:tp], refs[tp : 2 * tp], refs[2 * tp :]
        (inputs_ref, bias_ref, gain_ref, shift_ref, up_ref, up_bias_ref, down_ref,
         part_ref, hidden_ref, first_ref, pre_ref) = refs
        hidden = joined(context_refs, out_refs)
        ready()
        hidden = inputs_ref[...].astype(F32) + hidden + line(bias_ref)
        hidden_ref[...] = hidden
        finish(1)
        unit, _ = norm_stats(hidden)
        first = unit * line(gain_ref) + line(shift_ref)
        first_ref[...] = first
        finish(2)
        pre, part = feed(first.astype(BF16), up_ref, up_bias_ref, down_ref)
        pre_ref[...] = pre
        part_ref[...] = part

    part, hidden, first, pre_act = run(
        first_body,
        [((chosen, width), BF16), ((chosen, width), F32), ((chosen, width), F32), ((chosen, units), F32)],
        (*contexts, *out_all, top_inputs, out_bias, first_gain, first_shift, up_weight, up_bias, down_weight),
        "first",
        far=tuple(range(tp, 2 * tp + 4)) + (2 * tp + 5,),
        far_out=(1, 2, 3),
        early=(1, 2),
        late=tuple(range(2 * tp, 2 * tp + 4)) + (2 * tp + 5,),
        us=3,
    )
    parts = [part] + others(part)

    def slope_body(pre_ref, slope_ref):
        slope_ref[...] = gelu_grad(pre_ref[...])

    (slope,) = run(slope_body, ((chosen, units), F32), (pre_act,), "slope", far=(0,), us=1.5)

    def back_norm(grad, unit, q, gain):
        scaled = grad * gain
        return q * (
            scaled
            - jnp.mean(scaled, -1, keepdims=True)
            - unit * jnp.mean(scaled * unit, -1, keepdims=True)
        )

    def put_sums(ref, sums):
        for i, vector in enumerate(sums):
            ref[i : i + 1] = vector

    def column_sum(array):
        return jnp.sum(array, 0, keepdims=True)

    def second_body(*refs, ready, finish):
        part_refs, refs = refs[:tp], refs[tp:]
        (first_ref, bias_ref, gain_ref, shift_ref, cot_ref, slope_ref, down_ref, up_ref,
         context_ref, output_ref, grad_ref, back_ref, sums_ref, keep_ref) = refs
        second = paired([r[...].astype(F32) for r in part_refs])
        ready()
        second = first_ref[...] + second + line(bias_ref)
        unit, q = norm_stats(second)
        output_ref[...] = (unit * line(gain_ref) + line(shift_ref)).astype(BF16)
        finish(0)
        grad = back_norm(cot_ref[...], unit, q, line(gain_ref))
        grad_ref[...] = grad
        low = grad.astype(BF16)
        grad_pre = (nt(low, down_ref[...]) * slope_ref[...]).astype(BF16)
        back_ref[...] = nt(grad_pre, up_ref[...]).astype(BF16)
        put_sums(sums_ref, [column_sum(cot_ref[...] * unit), column_sum(cot_ref[...]), column_sum(grad)])
        keep_ref[:, :width] = first_ref[...].astype(BF16)
        keep_ref[:, width : 2 * width] = low
        keep_ref[:, 2 * width :] = context_ref[...]

    out_chosen, grad_second, back, sums, keep = run(
        second_body,
        [((chosen, width), BF16), ((chosen, width), F32), ((chosen, width), BF16), ((8, width), F32),
         ((chosen, 2 * width + local), BF16)],
        (*parts, first, down_bias, second_gain, second_shift, cot, slope, down_weight, up_weight, context),
        "second",
        far=tuple(range(tp, tp + 5)),
        late=tuple(range(tp, tp + 5)),
        far_out=(0, 4),
        early=(0,),
        us=3,
    )
    backs = [back] + others(back)
    keeps = lax.all_gather(keep, "seq", axis=0)

    def hidden_body(ids_ref, *refs, ready):
        back_refs, refs = refs[:tp], refs[tp:]
        grad_ref, hidden_ref, gain_ref, sums_ref, read_ref, out_ref, send_ref, attn_ref, sum_ref = refs
        side = ids_ref[1] % 2
        grad = grad_ref[...] + paired([r[...].astype(F32) for r in back_refs])
        ready()
        unit, q = norm_stats(hidden_ref[...])
        grad_hidden = back_norm(grad, unit, q, line(gain_ref))
        out_ref[...] = grad_hidden
        attn_ref[...] = grad_hidden.astype(BF16)
        sum_ref[...] = jnp.zeros_like(sum_ref)
        sum_ref[:3] = sums_ref[:3]
        put_sums(sum_ref.at[3:6], [column_sum(grad * unit), column_sum(grad), column_sum(grad_hidden)])
        lanes = pl.ds(pl.multiple_of(side * part_width, part_width), part_width)
        mine, mine_sums = attn_ref[:, lanes], sum_ref[:, lanes].astype(BF16)
        read = read_ref[...].astype(BF16)
        for i in range(n):
            send_ref[i, :chosen] = mine
            send_ref[i, chosen : chosen + 16] = mine_sums
            send_ref[i, chosen + 16 :, :local] = read[: chosen // 2]
            send_ref[i, chosen + 16 :, local:] = read[chosen // 2 :]

    grad_hidden, attn_send = run(
        hidden_body,
        [((chosen, width), F32), ((n, chosen + 16 + chosen // 2, part_width), BF16)],
        (ids, *backs, grad_second, hidden, first_gain, sums, value_sum),
        "hidden",
        also=((all_keys, pltpu.HBM),),
        far=(tp + 2, tp + 3),
        late=(tp + 2, tp + 3),
        far_out=(0,),
        smem=1,
        scratch=[pltpu.VMEM((chosen, width), BF16), pltpu.VMEM((16, width), F32)],
        us=2,
    )
    attn_mine = exchange(attn_send)

    def rest_body(codes_ref, keys_ref, wide_ref, tall_ref, band_ref, near_ref, context_ref,
                  key_ref, turned_ref, word_ref, count_ref, ready):
        queries = query_words(codes_ref[...], wide_ref[...])
        ready()
        for i in range(n):
            key_ref[:, i * tokens : (i + 1) * tokens] = keys_ref[i, :codes_rows]
            turned_ref[:, i * tokens : (i + 1) * tokens] = keys_ref[i, codes_rows:]
        word_ref[...] = key_words(key_ref[...], tall_ref[...])
        near = near_ref[...]
        twice = jnp.concatenate([near, near], axis=0)
        for h in range(heads):
            @pl.loop(0, n * tokens // 256)
            def _(i):
                for c in range(2):
                    lanes = pl.ds(pl.multiple_of(i * 256 + c * 128, 128), 128)
                    count_ref[:, lanes] = matches(queries, word_ref[:, lanes], h)

            cols = slice(h * dim, (h + 1) * dim)
            mine = nt(count_ref[...], turned_ref[cols]) * (1.0 / hashes)
            conv = nn(band_ref[h], twice[:, cols])
            context_ref[:, cols] = (mine * unit_rows(mine) + conv).astype(BF16)

    (rest_context,) = run(
        rest_body,
        ((rest, local), BF16),
        (rest_codes, all_keys, wide, tall, low_bands, near),
        "rest_context",
        far=(0, 1, 2, 3, 4, 5),
        late=(1, 4, 5),
        scratch=[pltpu.VMEM((codes_rows, n * tokens), BF16), pltpu.VMEM((local, n * tokens), BF16),
                 pltpu.VMEM((32, n * tokens), I32), pltpu.VMEM((rest, n * tokens), BF16)],
        us=12,
    )
    rest_contexts = [rest_context] + others(rest_context)

    def values_body(ids_ref, mine_ref, other_ref, out_ref, count_ref, band_ref, codes_ref,
                    grad_ref, dense_ref, attn_ref, *refs, ready):
        vector_refs, (y_ref, read_ref, reads_ref, sums_ref) = refs[:6], refs[6:]
        me, side = ids_ref[0], ids_ref[1] % 2
        own = pl.ds(pl.multiple_of(side * part_width, part_width), part_width)
        far = pl.ds(pl.multiple_of((1 - side) * part_width, part_width), part_width)
        for ref, lanes in ((mine_ref, own), (other_ref, far)):
            for i in range(n):
                attn_ref[i * chosen : (i + 1) * chosen, lanes] = ref[i, :chosen]
            sum_all = ref[0, chosen : chosen + 16].astype(F32)
            for i in range(1, n):
                sum_all += ref[i, chosen : chosen + 16].astype(F32)
            sums_ref[:, lanes] = sum_all
        for i, ref in enumerate(vector_refs):
            ref[...] = sums_ref[i : i + 1].reshape(width)
        for i in range(n):
            for at in range(2):
                reads_ref[i * chosen + at * (chosen // 2) : i * chosen + (at + 1) * (chosen // 2)] = mine_ref[
                    i, chosen + 16 :, at * local : (at + 1) * local
                ]
        y = nt(attn_ref[...], out_ref[...]).astype(BF16)
        y_ref[...] = y
        ready()
        for h in range(heads):
            cols = slice(h * dim, (h + 1) * dim)
            read = reads_ref[:, cols].astype(F32)
            grad = y[:, cols].astype(F32)
            r = unit_rows(read)
            back = r * (grad - read * (r * r) * jnp.mean(grad * read, -1, keepdims=True))
            read_ref[:, cols] = (back * (1.0 / hashes)).astype(BF16)
        dense = jnp.zeros((window, local), F32)
        for step in (-1, 0, 1):
            source = jnp.clip(me + step, 0, n - 1)
            inside = jnp.logical_and(me + step >= 0, me + step < n)
            there = y_ref[pl.ds(pl.multiple_of(source * chosen, chosen), chosen)]
            spots = codes_ref[source][:, codes_rows : codes_rows + 1].astype(F32).astype(I32)
            spots = jnp.where(inside, spots + step * tokens + half, -1)
            place = one_zero(spots == iota((chosen, window), 1))
            dense += tn(place, there)
        dense_low = dense.astype(BF16)
        dense_ref[...] = dense_low
        twice = jnp.concatenate([dense_low, dense_low], axis=0)
        for h in range(heads):
            cols = slice(h * dim, (h + 1) * dim)
            grad = tn(count_ref[h], read_ref[:, cols]) + nn(band_ref[h], twice[:, cols])
            grad_ref[:, cols] = grad.astype(BF16)

    attn_other = swap(lax.optimization_barrier((attn_mine, rest_context))[0], 1)
    grad_values, dense, attn_all, *vectors = run(
        values_body,
        [((tokens, local), BF16), ((window, local), BF16), ((total, width), BF16)] + [((width,), F32)] * 6,
        (ids, attn_mine, attn_other, out_weight, counts, back_bands, all_codes),
        "values_back",
        far=(3, 4, 5, 6),
        late=(4, 5, 6),
        far_out=(2, 3, 4, 5, 6, 7, 8),
        smem=1,
        scratch=[pltpu.VMEM((total, local), BF16)] * 3 + [
                 pltpu.VMEM((16, width), F32)],
        us=6,
    )
    grads = [grad_values] + others(grad_values)

    share = local // n
    extra = 8

    def value_grad_body(inputs_ref, grad_ref, dense_ref, near_ref, send_ref, row_ref):
        grad = grad_ref[...]
        weight = tn(grad, inputs_ref[...]).astype(BF16)
        row_ref[...] = jnp.zeros_like(row_ref)
        row_ref[:1, :local] = column_sum(grad.astype(F32))
        turn = one_zero(iota((tokens, tokens), 0) + iota((tokens, tokens), 1) == tokens - 1)
        turned = nn(turn, dense_ref[half : half + tokens]).astype(BF16)
        for h in range(heads):
            cols = slice(h * dim, (h + 1) * dim)
            both = nt(turned[:, cols], near_ref[:, cols])
            aligned = pltpu.roll(both, window - tokens + 1, 1, stride=1, stride_axis=0)
            row_ref[1 + h : 2 + h, :128] = column_sum(aligned)[:, :128]
        for i in range(n):
            send_ref[i, :share] = weight[i * share : (i + 1) * share]
            send_ref[i, share:] = row_ref[...].astype(BF16)

    (value_part,) = run(
        value_grad_body,
        ((n, share + extra, width), BF16),
        (inputs, grad_values, dense, near),
        "value_grad",
        far=(0, 3),
        scratch=[pltpu.VMEM((extra, width), F32)],
        us=2.5,
    )
    value_part = exchange(value_part)

    def rest_first_body(*refs, ready):
        context_refs, out_refs, refs = refs[:tp], refs[tp : 2 * tp], refs[2 * tp :]
        (inputs_ref, bias_ref, gain_ref, shift_ref, up_ref, up_bias_ref, down_ref, part_ref, first_ref) = refs
        hidden = joined(context_refs, out_refs)
        ready()
        hidden = inputs_ref[...].astype(F32) + hidden + line(bias_ref)
        unit, _ = norm_stats(hidden)
        first = unit * line(gain_ref) + line(shift_ref)
        first_ref[...] = first
        part_ref[...] = feed(first.astype(BF16), up_ref, up_bias_ref, down_ref)[1]

    rest_part, rest_first = run(
        rest_first_body,
        [((rest, width), BF16), ((rest, width), F32)],
        (*rest_contexts, *out_all, low_inputs, out_bias, first_gain, first_shift, up_weight, up_bias,
         down_weight),
        "rest_first",
        far=tuple(range(tp, 2 * tp + 4)) + (2 * tp + 5,),
        late=tuple(range(2 * tp, 2 * tp + 4)) + (2 * tp + 5,),
        far_out=(1,),
        us=4,
    )
    rest_parts = [rest_part] + others(rest_part)

    def input_body(*refs):
        grad_refs, weight_refs, (order_ref, hidden_ref, out_ref) = (
            refs[:tp], refs[tp : 2 * tp], refs[2 * tp :])
        pick = order_ref[:chosen]
        parts = split3(hidden_ref[...])
        placed = tn(pick, parts[0]) + tn(pick, parts[1]) + tn(pick, parts[2])
        out_ref[...] = placed + joined(grad_refs, weight_refs)

    (input_grad,) = run(
        input_body,
        ((tokens, width), F32),
        (*grads, *value_all, order, grad_hidden),
        "input_grad",
        far=tuple(range(tp, 2 * tp + 2)),
        far_out=(0,),
        us=4,
    )

    def value_sum_body(part_ref, send_ref, bias_ref, taps_ref):
        whole = part_ref[0].astype(F32)
        for i in range(1, n):
            whole += part_ref[i].astype(F32)
        for i in range(n):
            send_ref[i] = whole[:share].astype(BF16)
        bias_ref[...] = whole[share : share + 1, :local].reshape(local)
        taps_ref[...] = whole[share + 1 : share + 1 + heads, :taps]

    value_send_back, grad_value_bias, grad_taps = run(
        value_sum_body,
        [((n, share, width), BF16), ((local,), F32), ((heads, taps), F32)],
        (value_part,),
        "value_sums",
        far_out=(1, 2),
        us=1.5,
    )
    value_grad = exchange(value_send_back).reshape(local, width).astype(F32).T

    def output_body(*refs):
        part_refs, refs = refs[:tp], refs[tp:]
        first_ref, bias_ref, gain_ref, shift_ref, chosen_ref, order_ref, out_ref, sorted_ref = refs
        second = first_ref[...] + paired([r[...].astype(F32) for r in part_refs]) + line(bias_ref)
        unit, _ = norm_stats(second)
        sorted_ref[:chosen] = chosen_ref[...]
        sorted_ref[chosen:] = (unit * line(gain_ref) + line(shift_ref)).astype(BF16)
        out_ref[...] = tn(order_ref[...], sorted_ref[...]).astype(BF16)

    (output,) = run(
        output_body,
        ((tokens, width), BF16),
        (*rest_parts, rest_first, down_bias, second_gain, second_shift, out_chosen, order),
        "output",
        far=tuple(range(tp, tp + 6)),
        far_out=(0,),
        scratch=[pltpu.VMEM((tokens, width), BF16)],
        us=3,
    )

    def weights_body(keep_ref, attn_ref, up_w_ref, up_bias_ref, down_w_ref,
                     up_ref, up_sum_ref, grad_ref, out_ref, act_ref, pre_ref, finish):
        up_sum = jnp.zeros((1, units), F32)
        for i in range(n):
            rows = slice(i * chosen, (i + 1) * chosen)
            pre = nn(keep_ref[i, :, :width], up_w_ref[...]) + line(up_bias_ref)
            cdf = cdf_of(pre)
            act_ref[rows] = (pre * cdf).astype(BF16)
            slope = cdf + pre * jnp.exp(-0.5 * pre * pre) * 0.3989422804014327
            grad_pre = (nt(keep_ref[i, :, width : 2 * width], down_w_ref[...]) * slope).astype(BF16)
            pre_ref[rows] = grad_pre
            up_sum += column_sum(grad_pre.astype(F32))
        up_sum_ref[...] = up_sum.reshape(units)
        up_ref[...] = tn(keep_ref[:, :, :width].reshape(total, width), pre_ref[...])
        finish(0)
        grad_ref[...] = tn(act_ref[...], keep_ref[:, :, width : 2 * width].reshape(total, width))
        finish(2)
        out_ref[...] = tn(keep_ref[:, :, 2 * width :].reshape(total, local), attn_ref[...])

    grad_up, up_sum, grad_down, grad_out = run(
        weights_body,
        [((width, units), F32), ((units,), F32), ((units, width), F32), ((local, width), F32)],
        (keeps, attn_all, up_weight, up_bias, down_weight),
        "weights",
        far=(0, 1, 3),
        far_out=(0, 1, 2, 3),
        early=(0, 2),
        scratch=[pltpu.VMEM((total, units), BF16)] * 2,
        us=9,
    )

    return (
        output,
        input_grad,
        value_grad,
        grad_value_bias,
        grad_out,
        vectors[5],
        vectors[3],
        vectors[4],
        grad_up,
        up_sum,
        grad_down,
        vectors[2],
        vectors[0],
        vectors[1],
        grad_taps,
    )


def solution(mesh):
    return jax.shard_map(
        per_device,
        mesh=mesh,
        in_specs=(
            P("seq", None),
            P(None, "tp"),
            P("tp"),
            P("tp", None),
            P(),
            P(),
            P(),
            P(None, "tp"),
            P("tp"),
            P("tp", None),
            P(),
            P(),
            P(),
            P("tp", None),
            P("seq", "tp", None),
            P("seq", "tp", None),
            P("seq"),
            P("seq", None),
        ),
        out_specs=(
            P("seq", None),
            P("seq", None),
            P(None, "tp"),
            P("tp"),
            P("tp", None),
            P(),
            P(),
            P(),
            P(None, "tp"),
            P("tp"),
            P("tp", None),
            P(),
            P(),
            P(),
            P("tp", None),
        ),
        check_vma=False,
    )
```

time: 243 us -> 170 us (0.70)
  local copies, waits for them, and re-layouts: 68 us -> 0.02 us
  blocking collectives: 23.6 us -> 0 us
  Pallas kernels: 44.7 us -> 68.2 us
  waiting for transfers between devices: 54.8 us -> 43.2 us
  starting transfers between devices: 33.2 us -> 42.4 us
    unnamed x194 -> x10, local copies, waits for them, and re-layouts: 58.6 us -> 0.02 us
    all_to_all x1 -> x0, blocking collectives: 23.6 us -> none  [exchange(): return lax.all_to_all(array, 'seq', 0, 0)]
    pallas_call x20 -> x16, Pallas kernels: 44.7 us -> 68.2 us  [call(): pl.pallas_call(kernel, out_shape=[spaces[i](arrays[i].shape, arrays[i].dt...]
    all_to_all x4 -> x5, starting transfers between devices: 19.2 us -> 25.5 us  [exchange(): return lax.all_to_all(array, 'seq', 0, 0)]
    all_to_all x4 -> x5, waiting for transfers between devices: 28.6 us -> 23.5 us  [exchange(): return lax.all_to_all(array, 'seq', 0, 0)]
    slice x4 -> x0, local copies, waits for them, and re-layouts: 4.74 us -> none  [the longest x1 1.62 us: per_device(): vectors[1]]
    reshape x7 -> x0, local copies, waits for them, and re-layouts: 4.72 us -> none  [row(): return vector.reshape(1, -1)]
    ppermute x22 -> x25, waiting for transfers between devices: 23.2 us -> 19.6 us  [swap(): return lax.ppermute(array, 'tp', [(i, i ^ k) for i in range(tp)])]
  transfers between devices with their start and end apart: 31 -> 32, of which waited for: 15 -> 13; matrix products, arithmetic and copies ran while one was open for 4% -> 0% of each run, Pallas kernels for 18% -> 39%
where the time goes in v2:
time: 170 us; the launch traced here: 169 us
  Pallas kernels  68.2 us (40%)
  waiting for transfers between devices  43.2 us (25%)
  starting transfers between devices  42.4 us (25%)
  between operations  14.3 us (8%)
    pallas_call x16, Pallas kernels, call(): pl.pallas_call(kernel, out_shape=[spaces[i](arrays[i].shape, arrays[i].dt...  68.2 us
    all_to_all x5, starting transfers between devices, exchange(): return lax.all_to_all(array, 'seq', 0, 0)  25.5 us
    all_to_all x5, waiting for transfers between devices, exchange(): return lax.all_to_all(array, 'seq', 0, 0)  23.5 us
    ppermute x25, waiting for transfers between devices, swap(): return lax.ppermute(array, 'tp', [(i, i ^ k) for i in range(tp)])  19.6 us
    ppermute x25, starting transfers between devices, swap(): return lax.ppermute(array, 'tp', [(i, i ^ k) for i in range(tp)])  16.8 us
  transfers between devices with their start and end apart: 32, of which 13 were waited for; matrix products, arithmetic and copies ran while one was open for 0% of the time, Pallas kernels for 39%

profile of v2, /device:TPU:0, one launch (start us, length us, event | category | flops | bytes accessed | tf_op | source)
XLA Modules:
  0.0 169.1 jit_solution(2470982871606990693)
XLA Ops:
  7.2 2.7 %order.1 = (bf16[8,64,128]{2,1,0:T(8,128)(2,1)}, bf16[192,128]{1,0:T(8,128)(2,1)}, bf16[256,256]{1,0:T(8,128)(2,1)}) custom-call(s32[256]{0:T(256)} %refs_6_.3, s32[96,256]{1,0:T(8,128)} %bitcast.19), custom_call_target="tpu_custom_call" | custom-call | flops 2200000000 | tf_op jit(solution)/shard_map/order/pallas_call | solution.py:106
  9.9 7.3 %all-to-all-start = ((bf16[8,64,128]{2,1,0:T(8,128)(2,1)}), bf16[8,64,128]{2,1,0:T(8,128)(2,1)S(1)}, u32[]{:S(2)}, u32[]{:S(2)}) async-start(bf16[8,64,128]{2,1,0:T(8,128)(2,1)} %get-tuple-element.63.refs_8_), calls=%async_computation | async-start | bytes 262144 | tf_op jit(solution)/shard_map/all_to_all | solution.py:235
  17.2 5.9 %prepare.1 = (bf16[256,192]{1,0:T(8,128)(2,1)}, bf16[288,256]{1,0:T(8,128)(2,1)}, bf16[64,768]{1,0:T(8,128)(2,1)}, bf16[192,768]{1,0:T(8,128)(2,1)}, f32[64,768]...) custom-call(bf16[256,768]{1,0:T(8,128)(2,1)} %refs_0_.5, ...), custom_call_target="tpu_custom_call" | custom-call | flops 4400000000 | tf_op jit(solution)/shard_map/prepare/pallas_call | solution.py:106
  24.5 6.4 %count.1 = (bf16[3,512,256]{2,1,0:T(8,128)(2,1)}, bf16[8,96,192]{2,1,0:T(8,128)(2,1)}) custom-call(s32[2]{0:T(128)S(1)} %pad_add_fusion.refs_0_, bf16[8,64,128]{2,1,0:T(8,128)(2,1)S(1)} %all-to-all-done.refs_1_.refs_6_, bf16[288,256]{1,0:T(8,128)(2,1)} %get-tuple-element.64.refs_2_, bf16[256,192]{1,0:T(8,128)(2,1)} %get-tuple-element.66.refs_3_.refs_6_.refs_2_, ...), custom_call_target="tpu_custom_call" | custom-call | flops 5500000256 | tf_op jit(solution)/shard_map/count/pallas_call | solution.py:106
  30.9 4.7 %all-to-all-start.1 = ((bf16[8,96,192]{2,1,0:T(8,128)(2,1)}), bf16[8,96,192]{2,1,0:T(8,128)(2,1)S(1)}, u32[]{:S(2)}, u32[]{:S(2)}) async-start(bf16[8,96,192]{2,1,0:T(8,128)(2,1)} %get-tuple-element.67), calls=%async_computation.1 | async-start | bytes 786432 | tf_op jit(solution)/shard_map/all_to_all | solution.py:235
  35.8 1.6 collective-permute-start.4
  37.6 12.5 %all-to-all-done.1.refs_1_ = bf16[8,96,192]{2,1,0:T(8,128)(2,1)S(1)} async-done(((bf16[8,96,192]{2,1,0:T(8,128)(2,1)}), bf16[8,96,192]{2,1,0:T(8,128)(2,1)S(1)}, u32[]{:S(2)}, u32[]{:S(2)}) %all-to-all-start.1) | async-done | bytes 294944 | tf_op jit(solution)/shard_map/all_to_all | solution.py:235
  50.1 2.6 %context.1 = (bf16[64,192]{1,0:T(8,128)(2,1)S(1)}, f32[64,192]{1,0:T(8,128)S(1)}, bf16[384,192]{1,0:T(8,128)(2,1)}) custom-call(s32[2]{0:T(128)S(1)} %pad_add_fusion.refs_0_, bf16[8,96,192]{2,1,0:T(8,128)(2,1)S(1)} %all-to-all-done.1.refs_1_, bf16[256,192]{1,0:T(8,128)(2,1)} %get-tuple-element.66.refs_3_.refs_6_.refs_2_, ...), custom_call_target="tpu_custom_call" | custom-call | flops 2200000000 | tf_op jit(solution)/shard_map/context/pallas_call | solution.py:106
  52.8 1.5 collective-permute-start.1
  54.7 2.1 %collective-permute-done.1.refs_2_ = bf16[64,192]{1,0:T(8,128)(2,1)S(1)} collective-permute-done((bf16[64,192]{1,0:T(8,128)(2,1)S(1)}, bf16[64,192]{1,0:T(8,128)(2,1)S(1)}, u32[]{:S(2)}, u32[]{:S(2)}) %collective-permute-start.1) | collective-permute-done | bytes 24608 | tf_op jit(solution)/shard_map/ppermute | solution.py:229
  57.7 3.0 %first.1 = (bf16[64,768]{1,0:T(8,128)(2,1)S(1)}, f32[64,768]{1,0:T(8,128)}, f32[64,768]{1,0:T(8,128)}, f32[64,768]{1,0:T(8,128)}) custom-call(bf16[64,192]{1,0:T(8,128)(2,1)S(1)} %get-tuple-element.71.refs_0_.refs_15_.refs_12_, bf16[64,192]{1,0:T(8,128)(2,1)S(1)} %collective-permute-done.refs_1_, bf16[64,192]{1,0:T(8,128)(2,1)S(1)} %collective-permute-done.1.refs_2_, ...), custom_call_target="tpu_custom_call" | custom-call | flops 3300000000 | tf_op jit(solution)/shard_map/first/pallas_call | solution.py:106
  63.8 3.2 %collective-permute-done.7.refs_2_ = bf16[64,768]{1,0:T(8,128)(2,1)S(1)} collective-permute-done((bf16[64,768]{1,0:T(8,128)(2,1)S(1)}, bf16[64,768]{1,0:T(8,128)(2,1)S(1)}, u32[]{:S(2)}, u32[]{:S(2)}) %collective-permute-start.7) | collective-permute-done | bytes 98336 | tf_op jit(solution)/shard_map/ppermute | solution.py:229
  67.3 2.9 %second.1 = (bf16[64,768]{1,0:T(8,128)(2,1)}, f32[64,768]{1,0:T(8,128)S(1)}, bf16[64,768]{1,0:T(8,128)(2,1)S(1)}, f32[8,768]{1,0:T(8,128)S(1)}, bf16[64,1728]{1,0:T(8,128)(2,1)}) custom-call(bf16[64,768]{1,0:T(8,128)(2,1)S(1)} %get-tuple-element.73.refs_1_.refs_0_, bf16[64,768]{1,0:T(8,128)(2,1)S(1)} %collective-permute-done.6.refs_1_, ...), custom_call_target="tpu_custom_call" | custom-call | flops 3300000000 | tf_op jit(solution)/shard_map/second/pallas_call | solution.py:106
  72.5 3.5 %collective-permute-done.10.refs_3_ = bf16[64,768]{1,0:T(8,128)(2,1)S(1)} collective-permute-done((bf16[64,768]{1,0:T(8,128)(2,1)S(1)}, bf16[64,768]{1,0:T(8,128)(2,1)S(1)}, u32[]{:S(2)}, u32[]{:S(2)}) %collective-permute-start.10) | collective-permute-done | bytes 98336 | tf_op jit(solution)/shard_map/ppermute | solution.py:229
  75.9 1.6 collective-permute-done.11.refs_4_
  77.5 3.3 %hidden.1 = (f32[64,768]{1,0:T(8,128)}, bf16[8,112,384]{2,1,0:T(8,128)(2,1)}) custom-call(s32[2]{0:T(128)S(1)} %pad_add_fusion.refs_0_, bf16[64,768]{1,0:T(8,128)(2,1)S(1)} %get-tuple-element.77.refs_1_, bf16[64,768]{1,0:T(8,128)(2,1)S(1)} %collective-permute-done.9.refs_2_, bf16[64,768]{1,0:T(8,128)(2,1)S(1)} %collective-permute-done.10.refs_3_, ...), custom_call_target="tpu_custom_call" | custom-call | flops 2200000000 | tf_op jit(solution)/shard_map/hidden/pallas_call | solution.py:106
  80.9 3.7 %all-to-all-start.2 = ((bf16[8,112,384]{2,1,0:T(8,128)(2,1)}), bf16[8,112,384]{2,1,0:T(8,128)(2,1)S(1)}, u32[]{:S(2)}, u32[]{:S(2)}) async-start(bf16[8,112,384]{2,1,0:T(8,128)(2,1)} %get-tuple-element.85), calls=%async_computation.2 | async-start | bytes 1376256 | tf_op jit(solution)/shard_map/all_to_all | solution.py:235
  84.6 12.1 %rest_context.1.refs_7_.refs_0_ = bf16[192,192]{1,0:T(8,128)(2,1)S(1)} custom-call(bf16[192,128]{1,0:T(8,128)(2,1)} %get-tuple-element.61.refs_0_, bf16[8,288,256]{2,1,0:T(8,128)(2,1)} %bitcast.18, bf16[1024,256]{1,0:T(8,128)(2,1)} %constant.13.clone.refs_4_.refs_2_, bf16[64,768]{1,0:T(8,128)(2,1)} %constant.14.clone.refs_5_.refs_3_, ...), custom_call_target="tpu_custom_call" | custom-call | flops 13200000000 | tf_op jit(solution)/shard_map/rest_context/pallas_call | solution.py:106
  96.7 9.8 %all-to-all-done.2.refs_1_ = bf16[8,112,384]{2,1,0:T(8,128)(2,1)S(1)} async-done(((bf16[8,112,384]{2,1,0:T(8,128)(2,1)}), bf16[8,112,384]{2,1,0:T(8,128)(2,1)S(1)}, u32[]{:S(2)}, u32[]{:S(2)}) %all-to-all-start.2) | async-done | bytes 688160 | tf_op jit(solution)/shard_map/all_to_all | solution.py:235
  107.0 1.5 collective-permute-start.23
  110.4 4.1 %values_back.1 = (bf16[256,192]{1,0:T(8,128)(2,1)S(1)}, bf16[384,192]{1,0:T(8,128)(2,1)S(1)}, bf16[512,768]{1,0:T(8,128)(2,1)}, f32[768]{0:T(1024)}, f32[768]{0:...) custom-call(s32[2]{0:T(128)S(1)} %pad_add_fusion.refs_0_, ...), custom_call_target="tpu_custom_call" | custom-call | flops 6600000000 | tf_op jit(solution)/shard_map/values_back/pallas_call | solution.py:106
  114.4 2.5 %value_grad.1.refs_15_ = bf16[8,32,768]{2,1,0:T(8,128)(2,1)} custom-call(bf16[256,768]{1,0:T(8,128)(2,1)} %refs_0_.5, bf16[256,192]{1,0:T(8,128)(2,1)S(1)} %get-tuple-element.88.refs_1_.refs_4_.refs_0_, bf16[384,192]{1,0:T(8,128)(2,1)S(1)} %get-tuple-element.89.refs_2_, bf16[384,192]{1,0:T(8,128)(2,1)} %get-tuple-element.70.refs_5_.refs_3_, ...), custom_call_target="tpu_custom_call" | custom-call | flops 2750000128 | tf_op jit(solution)/shard_map/value_grad/pallas_call | solution.py:106
  116.9 3.6 %all-to-all-start.3 = ((bf16[8,32,768]{2,1,0:T(8,128)(2,1)}), bf16[8,32,768]{2,1,0:T(8,128)(2,1)S(1)}, u32[]{:S(2)}, u32[]{:S(2)}) async-start(bf16[8,32,768]{2,1,0:T(8,128)(2,1)} %value_grad.1.refs_15_), calls=%async_computation.3 | async-start | bytes 786432 | tf_op jit(solution)/shard_map/all_to_all | solution.py:235
  121.2 1.5 collective-permute-start.20
  122.8 4.1 %rest_first.1 = (bf16[192,768]{1,0:T(8,128)(2,1)S(1)}, f32[192,768]{1,0:T(8,128)}) custom-call(bf16[192,192]{1,0:T(8,128)(2,1)S(1)} %rest_context.1.refs_7_.refs_0_, bf16[192,192]{1,0:T(8,128)(2,1)S(1)} %collective-permute-done.12.refs_1_, bf16[192,192]{1,0:T(8,128)(2,1)S(1)} %collective-permute-done.13.refs_2_, ...), custom_call_target="tpu_custom_call" | custom-call | flops 4400000000 | tf_op jit(solution)/shard_map/rest_first/pallas_call | solution.py:106
  127.5 2.3 %collective-permute-done.24.refs_7_ = bf16[192,768]{1,0:T(8,128)(2,1)S(1)} collective-permute-done((bf16[192,768]{1,0:T(8,128)(2,1)}, bf16[192,768]{1,0:T(8,128)(2,1)S(1)}, u32[]{:S(2)}, u32[]{:S(2)}) %collective-permute-start.24) | collective-permute-done | bytes 294944 | tf_op jit(solution)/shard_map/ppermute | solution.py:229
  133.2 2.2 %collective-permute-done.21.refs_3_ = bf16[256,192]{1,0:T(8,128)(2,1)S(1)} collective-permute-done((bf16[256,192]{1,0:T(8,128)(2,1)S(1)}, bf16[256,192]{1,0:T(8,128)(2,1)S(1)}, u32[]{:S(2)}, u32[]{:S(2)}) %collective-permute-start.21) | collective-permute-done | bytes 98336 | tf_op jit(solution)/shard_map/ppermute | solution.py:229
  135.4 3.2 %input_grad.1.refs_1_ = f32[256,768]{1,0:T(8,128)} custom-call(bf16[256,192]{1,0:T(8,128)(2,1)S(1)} %get-tuple-element.88.refs_1_.refs_4_.refs_0_, bf16[256,192]{1,0:T(8,128)(2,1)S(1)} %collective-permute-done.19.refs_1_, bf16[256,192]{1,0:T(8,128)(2,1)S(1)} %collective-permute-done.20.refs_2_, bf16[256,192]{1,0:T(8,128)(2,1)S(1)} %collective-permute-done.21.refs_3_, ...), custom_call_target="tpu_custom_call" | custom-call | flops 4400000000 | tf_op jit(solution)/shard_map/input_grad/pallas_call | solution.py:106
  139.9 6.2 %all-to-all-start.4 = ((bf16[8,24,768]{2,1,0:T(8,128)(2,1)}), bf16[8,24,768]{2,1,0:T(8,128)(2,1)S(1)}, u32[]{:S(2)}, u32[]{:S(2)}) async-start(bf16[8,24,768]{2,1,0:T(8,128)(2,1)} %get-tuple-element.92.refs_10_), calls=%async_computation.4 | async-start | bytes 589824 | tf_op jit(solution)/shard_map/all_to_all | solution.py:235
  146.1 2.0 %collective-permute-done.18.refs_3_ = bf16[192,768]{1,0:T(8,128)(2,1)} collective-permute-done((bf16[192,768]{1,0:T(8,128)(2,1)S(1)}, bf16[192,768]{1,0:T(8,128)(2,1)}, u32[]{:S(2)}, u32[]{:S(2)}) %collective-permute-start.18) | collective-permute-done | bytes 294944 | tf_op jit(solution)/shard_map/ppermute | solution.py:229
  148.1 3.7 %output.1.refs_5_ = bf16[256,768]{1,0:T(8,128)(2,1)} custom-call(bf16[192,768]{1,0:T(8,128)(2,1)S(1)} %get-tuple-element.90.refs_10_.refs_0_, bf16[192,768]{1,0:T(8,128)(2,1)S(1)} %collective-permute-done.16.refs_1_, bf16[192,768]{1,0:T(8,128)(2,1)} %collective-permute-done.17.refs_2_, bf16[192,768]{1,0:T(8,128)(2,1)} %collective-permute-done.18.refs_3_, ...), custom_call_target="tpu_custom_call" | custom-call | flops 3300000000 | tf_op jit(solution)/shard_map/output/pallas_call | solution.py:106
  151.9 9.4 %weights.1 = (f32[768,768]{1,0:T(8,128)}, f32[768]{0:T(1024)}, f32[768,768]{1,0:T(8,128)}, f32[192,768]{1,0:T(8,128)}) custom-call(bf16[8,64,1728]{2,1,0:T(8,128)(2,1)} %bitcast.16, bf16[512,768]{1,0:T(8,128)(2,1)} %get-tuple-element.95.refs_1_, bf16[768,768]{1,0:T(8,128)(2,1)S(1)} %copy-done.1, f32[768]{0:T(1024)} %refs_3_.4, ...), custom_call_target="tpu_custom_call" | custom-call | flops 9900000256 | tf_op jit(solution)/shard_map/weights/pallas_call | solution.py:106
  (62 shorter events, 18.2 us)
Async XLA Ops:
  9.9 14.6 %all-to-all-start = ((bf16[8,64,128]{2,1,0:T(8,128)(2,1)}), bf16[8,64,128]{2,1,0:T(8,128)(2,1)S(1)}, u32[]{:S(2)}, u32[]{:S(2)}) async-start(bf16[8,64,128]{2,1,0:T(8,128)(2,1)} %get-tuple-element.63.refs_8_), calls=%async_computation | async-start | bytes 262144 | tf_op jit(solution)/shard_map/all_to_all | solution.py:235
  17.1 60.4 %all-gather.5.cloned.1.call-start = ((), (), s32[]{:S(2)}) async-start(), calls=%async_computation.5 | async-start | bytes 1327104 | tf_op jit(solution)/shard_map/all_gather | solution.py:320
  30.9 19.2 %all-to-all-start.1 = ((bf16[8,96,192]{2,1,0:T(8,128)(2,1)}), bf16[8,96,192]{2,1,0:T(8,128)(2,1)S(1)}, u32[]{:S(2)}, u32[]{:S(2)}) async-start(bf16[8,96,192]{2,1,0:T(8,128)(2,1)} %get-tuple-element.67), calls=%async_computation.1 | async-start | bytes 786432 | tf_op jit(solution)/shard_map/all_to_all | solution.py:235
  35.6 116.3 %all-gather.7.cloned.1.call-start = ((), (), s32[]{:S(2)}) async-start(), calls=%async_computation.6 | async-start | bytes 2064384 | tf_op jit(solution)/shard_map/all_gather | solution.py:488
  35.7 18.7 %collective-permute-start.3 = (bf16[192,768]{1,0:T(8,128)(2,1)S(1)}, bf16[192,768]{1,0:T(8,128)(2,1)}, u32[]{:S(2)}, u32[]{:S(2)}) collective-permute-start(bf16[192,768]{1,0:T(8,128)(2,1)S(1)} %copy-done.3), channel_id=1, source_target_pairs={{0,1},{1,0},{2,3},{3,2},{4,5},{5,4},{6,7},{7,6},{8,9},{9,8},{10,11... | collective-permute-start | bytes 884744 | tf_op jit(solution)/shard_map/ppermute | solution.py:229
  35.8 18.9 %collective-permute-start.4 = (bf16[192,768]{1,0:T(8,128)(2,1)S(1)}, bf16[192,768]{1,0:T(8,128)(2,1)}, u32[]{:S(2)}, u32[]{:S(2)}) collective-permute-start(bf16[192,768]{1,0:T(8,128)(2,1)S(1)} %copy-done.3), channel_id=1, source_target_pairs={{0,2},{1,3},{2,0},{3,1},{4,6},{5,7},{6,4},{7,5},{8,10},{9,11},{10,... | collective-permute-start | bytes 884744 | tf_op jit(solution)/shard_map/ppermute | solution.py:229
  37.4 17.3 %collective-permute-start.5 = (bf16[192,768]{1,0:T(8,128)(2,1)S(1)}, bf16[192,768]{1,0:T(8,128)(2,1)}, u32[]{:S(2)}, u32[]{:S(2)}) collective-permute-start(bf16[192,768]{1,0:T(8,128)(2,1)S(1)} %copy-done.3), channel_id=1, source_target_pairs={{0,3},{1,2},{2,1},{3,0},{4,7},{5,6},{6,5},{7,4},{8,11},{9,10},{10,... | collective-permute-start | bytes 884744 | tf_op jit(solution)/shard_map/ppermute | solution.py:229
  52.7 2.0 %collective-permute-start = (bf16[64,192]{1,0:T(8,128)(2,1)S(1)}, bf16[64,192]{1,0:T(8,128)(2,1)S(1)}, u32[]{:S(2)}, u32[]{:S(2)}) collective-permute-start(bf16[64,192]{1,0:T(8,128)(2,1)S(1)} %get-tuple-element.71.refs_0_.refs_15_.refs_12_), channel_id=1, source_target_pairs={{0,1},{1,0},{2,3},{3,2},{4,5},{5,4},{6,7},{7,6},{8,9},{9,8},{10,11... | collective-permute-start | bytes 73736 | tf_op jit(solution)/shard_map/ppermute | solution.py:229
  52.8 4.0 %collective-permute-start.1 = (bf16[64,192]{1,0:T(8,128)(2,1)S(1)}, bf16[64,192]{1,0:T(8,128)(2,1)S(1)}, u32[]{:S(2)}, u32[]{:S(2)}) collective-permute-start(bf16[64,192]{1,0:T(8,128)(2,1)S(1)} %get-tuple-element.71.refs_0_.refs_15_.refs_12_), channel_id=1, source_target_pairs={{0,2},{1,3},{2,0},{3,1},{4,6},{5,7},{6,4},{7,5},{8,10},{9,11},{10,... | collective-permute-start | bytes 73736 | tf_op jit(solution)/shard_map/ppermute | solution.py:229
  54.4 3.3 %collective-permute-start.2 = (bf16[64,192]{1,0:T(8,128)(2,1)S(1)}, bf16[64,192]{1,0:T(8,128)(2,1)S(1)}, u32[]{:S(2)}, u32[]{:S(2)}) collective-permute-start(bf16[64,192]{1,0:T(8,128)(2,1)S(1)} %get-tuple-element.71.refs_0_.refs_15_.refs_12_), channel_id=1, source_target_pairs={{0,3},{1,2},{2,1},{3,0},{4,7},{5,6},{6,5},{7,4},{8,11},{9,10},{10,... | collective-permute-start | bytes 73736 | tf_op jit(solution)/shard_map/ppermute | solution.py:229
  60.7 3.1 %collective-permute-start.6 = (bf16[64,768]{1,0:T(8,128)(2,1)S(1)}, bf16[64,768]{1,0:T(8,128)(2,1)S(1)}, u32[]{:S(2)}, u32[]{:S(2)}) collective-permute-start(bf16[64,768]{1,0:T(8,128)(2,1)S(1)} %get-tuple-element.73.refs_1_.refs_0_), channel_id=1, source_target_pairs={{0,1},{1,0},{2,3},{3,2},{4,5},{5,4},{6,7},{7,6},{8,9},{9,8},{10,11... | collective-permute-start | bytes 294920 | tf_op jit(solution)/shard_map/ppermute | solution.py:229
  61.3 5.7 %collective-permute-start.7 = (bf16[64,768]{1,0:T(8,128)(2,1)S(1)}, bf16[64,768]{1,0:T(8,128)(2,1)S(1)}, u32[]{:S(2)}, u32[]{:S(2)}) collective-permute-start(bf16[64,768]{1,0:T(8,128)(2,1)S(1)} %get-tuple-element.73.refs_1_.refs_0_), channel_id=1, source_target_pairs={{0,2},{1,3},{2,0},{3,1},{4,6},{5,7},{6,4},{7,5},{8,10},{9,11},{10,... | collective-permute-start | bytes 294920 | tf_op jit(solution)/shard_map/ppermute | solution.py:229
  62.2 5.1 %collective-permute-start.8 = (bf16[64,768]{1,0:T(8,128)(2,1)S(1)}, bf16[64,768]{1,0:T(8,128)(2,1)S(1)}, u32[]{:S(2)}, u32[]{:S(2)}) collective-permute-start(bf16[64,768]{1,0:T(8,128)(2,1)S(1)} %get-tuple-element.73.refs_1_.refs_0_), channel_id=1, source_target_pairs={{0,3},{1,2},{2,1},{3,0},{4,7},{5,6},{6,5},{7,4},{8,11},{9,10},{10,... | collective-permute-start | bytes 294920 | tf_op jit(solution)/shard_map/ppermute | solution.py:229
  70.2 5.7 %collective-permute-start.10 = (bf16[64,768]{1,0:T(8,128)(2,1)S(1)}, bf16[64,768]{1,0:T(8,128)(2,1)S(1)}, u32[]{:S(2)}, u32[]{:S(2)}) collective-permute-start(bf16[64,768]{1,0:T(8,128)(2,1)S(1)} %get-tuple-element.77.refs_1_), channel_id=1, source_target_pairs={{0,2},{1,3},{2,0},{3,1},{4,6},{5,7},{6,4},{7,5},{8,10},{9,11},{10,... | collective-permute-start | bytes 294920 | tf_op jit(solution)/shard_map/ppermute | solution.py:229
  71.3 6.2 %collective-permute-start.11 = (bf16[64,768]{1,0:T(8,128)(2,1)S(1)}, bf16[64,768]{1,0:T(8,128)(2,1)S(1)}, u32[]{:S(2)}, u32[]{:S(2)}) collective-permute-start(bf16[64,768]{1,0:T(8,128)(2,1)S(1)} %get-tuple-element.77.refs_1_), channel_id=1, source_target_pairs={{0,3},{1,2},{2,1},{3,0},{4,7},{5,6},{6,5},{7,4},{8,11},{9,10},{10,... | collective-permute-start | bytes 294920 | tf_op jit(solution)/shard_map/ppermute | solution.py:229
  72.4 5.2 %collective-permute-start.9 = (bf16[64,768]{1,0:T(8,128)(2,1)S(1)}, bf16[64,768]{1,0:T(8,128)(2,1)S(1)}, u32[]{:S(2)}, u32[]{:S(2)}) collective-permute-start(bf16[64,768]{1,0:T(8,128)(2,1)S(1)} %get-tuple-element.77.refs_1_), channel_id=1, source_target_pairs={{0,1},{1,0},{2,3},{3,2},{4,5},{5,4},{6,7},{7,6},{8,9},{9,8},{10,11... | collective-permute-start | bytes 294920 | tf_op jit(solution)/shard_map/ppermute | solution.py:229
  80.9 25.7 %all-to-all-start.2 = ((bf16[8,112,384]{2,1,0:T(8,128)(2,1)}), bf16[8,112,384]{2,1,0:T(8,128)(2,1)S(1)}, u32[]{:S(2)}, u32[]{:S(2)}) async-start(bf16[8,112,384]{2,1,0:T(8,128)(2,1)} %get-tuple-element.85), calls=%async_computation.2 | async-start | bytes 1376256 | tf_op jit(solution)/shard_map/all_to_all | solution.py:235
  106.5 2.5 %collective-permute-start.15 = (bf16[8,112,384]{2,1,0:T(8,128)(2,1)S(1)}, bf16[8,112,384]{2,1,0:T(8,128)(2,1)S(1)}, u32[]{:S(2)}, u32[]{:S(2)}) collective-permute-start(bf16[8,112,384]{2,1,0:T(8,128)(2,1)S(1)} %all-to-all-done.2.refs_1_), channel_id=1, source_target_pairs={{0,1},{1,0},{2,3},{3,2},{4,5},{5,4},{6,7},{7,6},{8,9},{9,8},{10,11... | collective-permute-start | bytes 2064392 | tf_op jit(solution)/shard_map/ppermute | solution.py:229
  106.6 13.9 %collective-permute-start.22 = (bf16[192,768]{1,0:T(8,128)(2,1)}, bf16[192,768]{1,0:T(8,128)(2,1)}, u32[]{:S(2)}, u32[]{:S(2)}) collective-permute-start(bf16[192,768]{1,0:T(8,128)(2,1)} %bitcast.2.refs_1_.refs_4_), channel_id=1, source_target_pairs={{0,1},{1,0},{2,3},{3,2},{4,5},{5,4},{6,7},{7,6},{8,9},{9,8},{10,11... | collective-permute-start | bytes 884744 | tf_op jit(solution)/shard_map/ppermute | solution.py:229
  107.0 19.8 %collective-permute-start.23 = (bf16[192,768]{1,0:T(8,128)(2,1)}, bf16[192,768]{1,0:T(8,128)(2,1)}, u32[]{:S(2)}, u32[]{:S(2)}) collective-permute-start(bf16[192,768]{1,0:T(8,128)(2,1)} %bitcast.2.refs_1_.refs_4_), channel_id=1, source_target_pairs={{0,2},{1,3},{2,0},{3,1},{4,6},{5,7},{6,4},{7,5},{8,10},{9,11},{10,... | collective-permute-start | bytes 884744 | tf_op jit(solution)/shard_map/ppermute | solution.py:229
  108.5 12.4 %collective-permute-start.12 = (bf16[192,192]{1,0:T(8,128)(2,1)S(1)}, bf16[192,192]{1,0:T(8,128)(2,1)S(1)}, u32[]{:S(2)}, u32[]{:S(2)}) collective-permute-start(bf16[192,192]{1,0:T(8,128)(2,1)S(1)} %rest_context.1.refs_7_.refs_0_), channel_id=1, source_target_pairs={{0,1},{1,0},{2,3},{3,2},{4,5},{5,4},{6,7},{7,6},{8,9},{9,8},{10,11... | collective-permute-start | bytes 221192 | tf_op jit(solution)/shard_map/ppermute | solution.py:229
  108.5 12.7 %collective-permute-start.13 = (bf16[192,192]{1,0:T(8,128)(2,1)S(1)}, bf16[192,192]{1,0:T(8,128)(2,1)S(1)}, u32[]{:S(2)}, u32[]{:S(2)}) collective-permute-start(bf16[192,192]{1,0:T(8,128)(2,1)S(1)} %rest_context.1.refs_7_.refs_0_), channel_id=1, source_target_pairs={{0,2},{1,3},{2,0},{3,1},{4,6},{5,7},{6,4},{7,5},{8,10},{9,11},{10,... | collective-permute-start | bytes 221192 | tf_op jit(solution)/shard_map/ppermute | solution.py:229
  109.1 13.7 %collective-permute-start.14 = (bf16[192,192]{1,0:T(8,128)(2,1)S(1)}, bf16[192,192]{1,0:T(8,128)(2,1)}, u32[]{:S(2)}, u32[]{:S(2)}) collective-permute-start(bf16[192,192]{1,0:T(8,128)(2,1)S(1)} %rest_context.1.refs_7_.refs_0_), channel_id=1, source_target_pairs={{0,3},{1,2},{2,1},{3,0},{4,7},{5,6},{6,5},{7,4},{8,11},{9,10},{10,... | collective-permute-start | bytes 221192 | tf_op jit(solution)/shard_map/ppermute | solution.py:229
  116.9 21.7 %all-to-all-start.3 = ((bf16[8,32,768]{2,1,0:T(8,128)(2,1)}), bf16[8,32,768]{2,1,0:T(8,128)(2,1)S(1)}, u32[]{:S(2)}, u32[]{:S(2)}) async-start(bf16[8,32,768]{2,1,0:T(8,128)(2,1)} %value_grad.1.refs_15_), calls=%async_computation.3 | async-start | bytes 786432 | tf_op jit(solution)/shard_map/all_to_all | solution.py:235
  120.5 9.3 %collective-permute-start.24 = (bf16[192,768]{1,0:T(8,128)(2,1)}, bf16[192,768]{1,0:T(8,128)(2,1)S(1)}, u32[]{:S(2)}, u32[]{:S(2)}) collective-permute-start(bf16[192,768]{1,0:T(8,128)(2,1)} %bitcast.2.refs_1_.refs_4_), channel_id=1, source_target_pairs={{0,3},{1,2},{2,1},{3,0},{4,7},{5,6},{6,5},{7,4},{8,11},{9,10},{10,... | collective-permute-start | bytes 884744 | tf_op jit(solution)/shard_map/ppermute | solution.py:229
  120.9 9.4 %collective-permute-start.19 = (bf16[256,192]{1,0:T(8,128)(2,1)S(1)}, bf16[256,192]{1,0:T(8,128)(2,1)S(1)}, u32[]{:S(2)}, u32[]{:S(2)}) collective-permute-start(bf16[256,192]{1,0:T(8,128)(2,1)S(1)} %get-tuple-element.88.refs_1_.refs_4_.refs_0_), channel_id=1, source_target_pairs={{0,1},{1,0},{2,3},{3,2},{4,5},{5,4},{6,7},{7,6},{8,9},{9,8},{10,11... | collective-permute-start | bytes 294920 | tf_op jit(solution)/shard_map/ppermute | solution.py:229
  121.2 12.0 %collective-permute-start.20 = (bf16[256,192]{1,0:T(8,128)(2,1)S(1)}, bf16[256,192]{1,0:T(8,128)(2,1)S(1)}, u32[]{:S(2)}, u32[]{:S(2)}) collective-permute-start(bf16[256,192]{1,0:T(8,128)(2,1)S(1)} %get-tuple-element.88.refs_1_.refs_4_.refs_0_), channel_id=1, source_target_pairs={{0,2},{1,3},{2,0},{3,1},{4,6},{5,7},{6,4},{7,5},{8,10},{9,11},{10,... | collective-permute-start | bytes 294920 | tf_op jit(solution)/shard_map/ppermute | solution.py:229
  122.7 12.7 %collective-permute-start.21 = (bf16[256,192]{1,0:T(8,128)(2,1)S(1)}, bf16[256,192]{1,0:T(8,128)(2,1)S(1)}, u32[]{:S(2)}, u32[]{:S(2)}) collective-permute-start(bf16[256,192]{1,0:T(8,128)(2,1)S(1)} %get-tuple-element.88.refs_1_.refs_4_.refs_0_), channel_id=1, source_target_pairs={{0,3},{1,2},{2,1},{3,0},{4,7},{5,6},{6,5},{7,4},{8,11},{9,10},{10,... | collective-permute-start | bytes 294920 | tf_op jit(solution)/shard_map/ppermute | solution.py:229
  126.9 19.2 %collective-permute-start.16 = (bf16[192,768]{1,0:T(8,128)(2,1)S(1)}, bf16[192,768]{1,0:T(8,128)(2,1)S(1)}, u32[]{:S(2)}, u32[]{:S(2)}) collective-permute-start(bf16[192,768]{1,0:T(8,128)(2,1)S(1)} %get-tuple-element.90.refs_10_.refs_0_), channel_id=1, source_target_pairs={{0,1},{1,0},{2,3},{3,2},{4,5},{5,4},{6,7},{7,6},{8,9},{9,8},{10,11... | collective-permute-start | bytes 884744 | tf_op jit(solution)/shard_map/ppermute | solution.py:229
  129.8 16.3 %collective-permute-start.17 = (bf16[192,768]{1,0:T(8,128)(2,1)S(1)}, bf16[192,768]{1,0:T(8,128)(2,1)}, u32[]{:S(2)}, u32[]{:S(2)}) collective-permute-start(bf16[192,768]{1,0:T(8,128)(2,1)S(1)} %get-tuple-element.90.refs_10_.refs_0_), channel_id=1, source_target_pairs={{0,2},{1,3},{2,0},{3,1},{4,6},{5,7},{6,4},{7,5},{8,10},{9,11},{10,... | collective-permute-start | bytes 884744 | tf_op jit(solution)/shard_map/ppermute | solution.py:229
  130.3 17.8 %collective-permute-start.18 = (bf16[192,768]{1,0:T(8,128)(2,1)S(1)}, bf16[192,768]{1,0:T(8,128)(2,1)}, u32[]{:S(2)}, u32[]{:S(2)}) collective-permute-start(bf16[192,768]{1,0:T(8,128)(2,1)S(1)} %get-tuple-element.90.refs_10_.refs_0_), channel_id=1, source_target_pairs={{0,3},{1,2},{2,1},{3,0},{4,7},{5,6},{6,5},{7,4},{8,11},{9,10},{10,... | collective-permute-start | bytes 884744 | tf_op jit(solution)/shard_map/ppermute | solution.py:229
  139.9 21.4 %all-to-all-start.4 = ((bf16[8,24,768]{2,1,0:T(8,128)(2,1)}), bf16[8,24,768]{2,1,0:T(8,128)(2,1)S(1)}, u32[]{:S(2)}, u32[]{:S(2)}) async-start(bf16[8,24,768]{2,1,0:T(8,128)(2,1)} %get-tuple-element.92.refs_10_), calls=%async_computation.4 | async-start | bytes 589824 | tf_op jit(solution)/shard_map/all_to_all | solution.py:235
  (5 other events, 38.5 us)
Sparse Core Ops, SparseCore 0:
  23.2 44.7 all-gather.4
  72.6 51.5 all-gather.6

commit v3 on v2

--- a/solution.py
+++ b/solution.py
@@ -211,7 +211,6 @@
     rest = tokens - chosen
     piece = rest // tp
     part_rows = chosen // tp
-    part_width = width // 2
     codes_rows = heads * hashes
     window = tokens + 128
     total = n * chosen
@@ -231,46 +230,53 @@
     def others(array):
         return [swap(array, k) for k in range(1, tp)]
 
+    def others_by_steps(array):
+        far = swap(array, 2)
+        return [swap(array, 1), far, swap(far, 1)]
+
     def exchange(array):
         return lax.all_to_all(array, "seq", 0, 0)
 
     query_t = jnp.transpose(query_codes, (1, 2, 0)).reshape(codes_rows, tokens)
     key_t = jnp.transpose(key_codes, (1, 2, 0)).reshape(codes_rows, tokens)
     value_t = value_weight.T
-    out_all = [out_weight] + others(out_weight)
-    value_all = [value_t] + others(value_t)
-
-    def order_body(masked_ref, query_ref, chosen_ref, rest_ref, order_ref):
+    out_all = [out_weight] + others_by_steps(out_weight)
+    value_all = [value_t] + others_by_steps(value_t)
+
+    def order_of(masked_ref):
         flags = jnp.broadcast_to(line(masked_ref).astype(F32), (8, tokens))
         upto = one_zero(iota((tokens, tokens), 0) <= iota((tokens, tokens), 1))
         count = nn(flags.astype(BF16), upto)
         spot = iota((8, tokens), 1).astype(F32)
         target = jnp.where(flags > 0, count - 1.0, count[:, tokens - 1 :] + spot - count)
-        order = one_zero(iota((tokens, tokens), 0) == target[:1].astype(I32))
-        order_ref[...] = order
+        return one_zero(iota((tokens, tokens), 0) == target[:1].astype(I32))
+
+    def placed_codes(query_ref):
         where = jnp.where(
             iota((128 - codes_rows, tokens), 0) == 0, iota((128 - codes_rows, tokens), 1), 0
         )
-        table = jnp.concatenate([query_ref[...], where], axis=0).astype(F32).astype(BF16)
-        sorted_codes = nt(order, table).astype(BF16)
+        return jnp.concatenate([query_ref[...], where], axis=0).astype(F32).astype(BF16)
+
+    def order_body(masked_ref, query_ref, chosen_ref):
+        top = nt(order_of(masked_ref)[:chosen], placed_codes(query_ref)).astype(BF16)
         for i in range(n):
-            chosen_ref[i] = sorted_codes[:chosen]
-        rest_ref[...] = sorted_codes[chosen:]
-
-    chosen_codes, rest_codes, order = run(
+            chosen_ref[i] = top
+
+    (chosen_codes,) = run(
         order_body,
-        [((n, chosen, 128), BF16), ((rest, 128), BF16), ((tokens, tokens), BF16)],
+        ((n, chosen, 128), BF16),
         (masked, query_t),
         "order",
         far=(0, 1),
-        far_out=(1, 2),
         us=2,
     )
     all_codes = exchange(chosen_codes)
 
-    def prepare_body(inputs_ref, weight_ref, bias_ref, key_ref, order_ref, grad_ref, masked_ref, conv_ref,
+    def prepare_body(inputs_ref, weight_ref, bias_ref, key_ref, query_ref, grad_ref, masked_ref, conv_ref,
                      value_ref, send_ref, top_ref, low_ref, cot_ref, band_ref, low_band_ref, back_ref,
-                     pad_ref):
+                     codes_ref, order_ref, pad_ref):
+        order_ref[...] = order_of(masked_ref)
+        codes_ref[...] = nt(order_ref[chosen:], placed_codes(query_ref)).astype(BF16)
         values = (nt(inputs_ref[...], weight_ref[...]) + line(bias_ref)).astype(BF16)
         value_ref[...] = values
         same = one_zero(iota((local, local), 0) == iota((local, local), 1))
@@ -305,21 +311,23 @@
                     else:
                         back_ref[h, :, at : at + window] = level
 
-    values, value_send, top_inputs, low_inputs, cot, bands, low_bands, back_bands = run(
+    (values, value_send, top_inputs, low_inputs, cot, bands, low_bands, back_bands, rest_codes,
+     order) = run(
         prepare_body,
         [((tokens, local), BF16), ((codes_rows + local, tokens), BF16), ((chosen, width), BF16),
          ((rest, width), BF16), ((chosen, width), F32), ((heads, chosen, 2 * window), BF16),
-         ((heads, rest, 2 * window), BF16), ((heads, tokens, 2 * window), BF16)],
-        (inputs, value_t, value_bias, key_t, order, out_grad, masked, conv_weight),
+         ((heads, rest, 2 * window), BF16), ((heads, tokens, 2 * window), BF16), ((rest, 128), BF16),
+         ((tokens, tokens), BF16)],
+        (inputs, value_t, value_bias, key_t, query_t, out_grad, masked, conv_weight),
         "prepare",
         far=tuple(range(8)),
-        far_out=(0, 2, 3, 4, 5, 6, 7),
+        far_out=(0, 2, 3, 4, 5, 6, 7, 8, 9),
         scratch=[pltpu.VMEM((8, 128), F32)],
         us=4,
     )
     all_keys = lax.all_gather(value_send, "seq", axis=0)
 
-    def count_body(ids_ref, codes_ref, send_ref, value_ref, wide_ref, tall_ref, count_ref, out_ref, finish):
+    def count_body(ids_ref, codes_ref, send_ref, value_ref, wide_ref, tall_ref, count_ref, out_ref, ready, finish):
         me = ids_ref[0]
         keys = key_words(send_ref[:codes_rows], tall_ref[...])
         queries = query_words(codes_ref[...].reshape(total, 128), wide_ref[...])
@@ -335,6 +343,7 @@
             read = nt(count_ref[h], turned).astype(BF16)
             for i in range(n):
                 out_ref[i, :chosen, h * dim : (h + 1) * dim] = read[i * chosen : (i + 1) * chosen]
+        ready()
         for i in range(n):
             last, head_rows = value_ref[tokens - half :], value_ref[:half]
             rows = jnp.where(i == me + 1, last.astype(F32), head_rows.astype(F32))
@@ -345,7 +354,8 @@
         [((heads, total, tokens), BF16), ((n, chosen + half, local), BF16)],
         (ids, all_codes, value_send, values, wide, tall),
         "count",
-        far=(3, 4, 5),
+        far=(3,),
+        late=(3,),
         far_out=(0,),
         early=(0,),
         smem=1,
@@ -356,7 +366,7 @@
     def unit_rows(value_sum):
         return lax.rsqrt(jnp.mean(value_sum * value_sum, -1, keepdims=True) + 1e-05)
 
-    def context_body(ids_ref, reads_ref, value_ref, band_ref, context_ref, sum_ref, near_ref):
+    def context_body(ids_ref, reads_ref, value_ref, band_ref, context_ref, sum_ref, near_ref, ready, finish):
         me = ids_ref[0]
         total_read = reads_ref[0, :chosen].astype(F32)
         for i in range(1, n):
@@ -366,9 +376,11 @@
         before = reads_ref[jnp.maximum(me - 1, 0), chosen:].astype(F32)
         after = reads_ref[jnp.minimum(me + 1, n - 1), chosen:].astype(F32)
         near_ref[:half] = jnp.where(me > 0, before, 0.0).astype(BF16)
+        ready()
         near_ref[half : half + tokens] = value_ref[...]
         near_ref[half + tokens : 2 * half + tokens] = jnp.where(me < n - 1, after, 0.0).astype(BF16)
         near_ref[2 * half + tokens :] = jnp.zeros((window - tokens - 2 * half, local), BF16)
+        finish(2)
         near = near_ref[...]
         twice = jnp.concatenate([near, near], axis=0)
         for h in range(heads):
@@ -383,7 +395,9 @@
         (ids, reads, values, bands),
         "context",
         far=(2, 3),
+        late=(2, 3),
         far_out=(2,),
+        early=(2,),
         smem=1,
         us=2,
     )
@@ -452,10 +466,10 @@
     def column_sum(array):
         return jnp.sum(array, 0, keepdims=True)
 
-    def second_body(*refs, ready, finish):
+    def second_body(ids_ref, *refs, ready, finish):
         part_refs, refs = refs[:tp], refs[tp:]
         (first_ref, bias_ref, gain_ref, shift_ref, cot_ref, slope_ref, down_ref, up_ref,
-         context_ref, output_ref, grad_ref, back_ref, sums_ref, keep_ref) = refs
+         context_ref, output_ref, grad_ref, back_ref, sums_ref, keep_ref, low_ref) = refs
         second = paired([r[...].astype(F32) for r in part_refs])
         ready()
         second = first_ref[...] + second + line(bias_ref)
@@ -468,132 +482,147 @@
         grad_pre = (nt(low, down_ref[...]) * slope_ref[...]).astype(BF16)
         back_ref[...] = nt(grad_pre, up_ref[...]).astype(BF16)
         put_sums(sums_ref, [column_sum(cot_ref[...] * unit), column_sum(cot_ref[...]), column_sum(grad)])
-        keep_ref[:, :width] = first_ref[...].astype(BF16)
-        keep_ref[:, width : 2 * width] = low
-        keep_ref[:, 2 * width :] = context_ref[...]
-
+        low_ref[:, :width] = first_ref[...].astype(BF16)
+        low_ref[:, width:] = low
+        keep_ref[:, : 2 * width] = low_ref[pl.ds(pl.multiple_of(ids_ref[1] % 2 * mid, mid), mid)]
+        keep_ref[:, 2 * width : 2 * width + local] = context_ref[:mid]
+        keep_ref[:, 2 * width + local : 2 * width + 2 * local] = context_ref[mid:]
+        keep_ref[:, 2 * width + 2 * local :] = jnp.zeros((mid, kept - 2 * width - 2 * local), BF16)
+
+    mid = chosen // 2
+    kept = -(-2 * (width + local) // 1024) * 1024
     out_chosen, grad_second, back, sums, keep = run(
         second_body,
         [((chosen, width), BF16), ((chosen, width), F32), ((chosen, width), BF16), ((8, width), F32),
-         ((chosen, 2 * width + local), BF16)],
-        (*parts, first, down_bias, second_gain, second_shift, cot, slope, down_weight, up_weight, context),
+         ((mid, kept), BF16)],
+        (ids, *parts, first, down_bias, second_gain, second_shift, cot, slope, down_weight, up_weight, context),
         "second",
-        far=tuple(range(tp, tp + 5)),
-        late=tuple(range(tp, tp + 5)),
+        also=tuple((weight, pltpu.HBM) for weight in value_all[1:]),
+        far=tuple(range(tp + 1, tp + 6)),
+        late=tuple(range(tp + 1, tp + 6)),
         far_out=(0, 4),
         early=(0,),
+        smem=1,
+        scratch=[pltpu.VMEM((chosen, 2 * width), BF16)],
         us=3,
     )
     backs = [back] + others(back)
     keeps = lax.all_gather(keep, "seq", axis=0)
 
-    def hidden_body(ids_ref, *refs, ready):
+    def rest_counts(count_ref, queries, word_ref, head):
+        @pl.loop(0, n * tokens // 256)
+        def _(i):
+            for c in range(2):
+                lanes = pl.ds(pl.multiple_of(i * 256 + c * 128, 128), 128)
+                count_ref[:, lanes] = matches(queries, word_ref[:, lanes], head)
+
+    def rest_read(count_ref, keys_ref, head):
+        start = codes_rows + head * dim
+        turned = jnp.concatenate([keys_ref[i, start : start + dim] for i in range(n)], axis=1)
+        return nt(count_ref[...], turned) * (1.0 / hashes)
+
+    def rest_words_body(codes_ref, keys_ref, wide_ref, tall_ref, query_ref, word_ref, first_ref,
+                        key_ref, count_ref, ready):
+        queries = query_words(codes_ref[...], wide_ref[...])
+        query_ref[...] = queries
+        ready()
+        for i in range(n):
+            key_ref[:, i * tokens : (i + 1) * tokens] = keys_ref[i, :codes_rows]
+        word_ref[...] = key_words(key_ref[...], tall_ref[...])
+        rest_counts(count_ref, queries, word_ref, 0)
+        first_ref[...] = rest_read(count_ref, keys_ref, 0)
+
+    rest_queries, key_bits, rest_sum = run(
+        rest_words_body,
+        [((rest, 128), I32), ((32, n * tokens), I32), ((rest, dim), F32)],
+        (rest_codes, all_keys, wide, tall),
+        "rest_words",
+        far=(0, 1, 2, 3),
+        late=(1,),
+        scratch=[pltpu.VMEM((codes_rows, n * tokens), BF16), pltpu.VMEM((rest, n * tokens), BF16)],
+        us=5,
+    )
+
+    def hidden_body(ids_ref, *refs, ready, finish):
         back_refs, refs = refs[:tp], refs[tp:]
-        grad_ref, hidden_ref, gain_ref, sums_ref, read_ref, out_ref, send_ref, attn_ref, sum_ref = refs
-        side = ids_ref[1] % 2
+        grad_ref, hidden_ref, gain_ref, sums_ref, read_ref, weight_ref, out_ref, send_ref, share_ref, all_ref, attn_ref = refs
         grad = grad_ref[...] + paired([r[...].astype(F32) for r in back_refs])
         ready()
         unit, q = norm_stats(hidden_ref[...])
         grad_hidden = back_norm(grad, unit, q, line(gain_ref))
         out_ref[...] = grad_hidden
-        attn_ref[...] = grad_hidden.astype(BF16)
-        sum_ref[...] = jnp.zeros_like(sum_ref)
-        sum_ref[:3] = sums_ref[:3]
-        put_sums(sum_ref.at[3:6], [column_sum(grad * unit), column_sum(grad), column_sum(grad_hidden)])
-        lanes = pl.ds(pl.multiple_of(side * part_width, part_width), part_width)
-        mine, mine_sums = attn_ref[:, lanes], sum_ref[:, lanes].astype(BF16)
-        read = read_ref[...].astype(BF16)
-        for i in range(n):
-            send_ref[i, :chosen] = mine
-            send_ref[i, chosen : chosen + 16] = mine_sums
-            send_ref[i, chosen + 16 :, :local] = read[: chosen // 2]
-            send_ref[i, chosen + 16 :, local:] = read[chosen // 2 :]
-
-    grad_hidden, attn_send = run(
+        finish(0)
+        low = grad_hidden.astype(BF16)
+        y = nt(low, weight_ref[...]).astype(BF16)
+        for h in range(heads):
+            cols = slice(h * dim, (h + 1) * dim)
+            read, at = read_ref[:, cols], y[:, cols].astype(F32)
+            r = unit_rows(read)
+            back = r * (at - read * (r * r) * jnp.mean(at * read, -1, keepdims=True))
+            send_ref[0, :, cols] = (back * (1.0 / hashes)).astype(BF16)
+        send_ref[0, :, local:] = y
+        for i in range(1, n):
+            send_ref[i] = send_ref[0]
+        attn_ref[...] = low
+        share_ref[...] = attn_ref[pl.ds(pl.multiple_of(ids_ref[1] * part_rows, part_rows), part_rows)]
+        all_ref[:3] = sums_ref[:3]
+        put_sums(all_ref.at[3:6], [column_sum(grad * unit), column_sum(grad), column_sum(grad_hidden)])
+        all_ref[6:] = jnp.zeros((2, width), F32)
+
+    grad_hidden, read_send, share, sums = run(
         hidden_body,
-        [((chosen, width), F32), ((n, chosen + 16 + chosen // 2, part_width), BF16)],
-        (ids, *backs, grad_second, hidden, first_gain, sums, value_sum),
+        [((chosen, width), F32), ((n, chosen, 2 * local), BF16), ((part_rows, width), BF16), ((8, width), F32)],
+        (ids, *backs, grad_second, hidden, first_gain, sums, value_sum, out_weight),
         "hidden",
         also=((all_keys, pltpu.HBM),),
         far=(tp + 2, tp + 3),
         late=(tp + 2, tp + 3),
-        far_out=(0,),
+        far_out=(0, 2, 3),
+        early=(0,),
         smem=1,
-        scratch=[pltpu.VMEM((chosen, width), BF16), pltpu.VMEM((16, width), F32)],
+        scratch=[pltpu.VMEM((chosen, width), BF16)],
         us=2,
     )
-    attn_mine = exchange(attn_send)
-
-    def rest_body(codes_ref, keys_ref, wide_ref, tall_ref, band_ref, near_ref, context_ref,
-                  key_ref, turned_ref, word_ref, count_ref, ready):
-        queries = query_words(codes_ref[...], wide_ref[...])
-        ready()
-        for i in range(n):
-            key_ref[:, i * tokens : (i + 1) * tokens] = keys_ref[i, :codes_rows]
-            turned_ref[:, i * tokens : (i + 1) * tokens] = keys_ref[i, codes_rows:]
-        word_ref[...] = key_words(key_ref[...], tall_ref[...])
-        near = near_ref[...]
-        twice = jnp.concatenate([near, near], axis=0)
-        for h in range(heads):
-            @pl.loop(0, n * tokens // 256)
-            def _(i):
-                for c in range(2):
-                    lanes = pl.ds(pl.multiple_of(i * 256 + c * 128, 128), 128)
-                    count_ref[:, lanes] = matches(queries, word_ref[:, lanes], h)
-
+    read_all = exchange(read_send)
+
+    def rest_body(query_ref, word_ref, first_ref, keys_ref, band_ref, near_ref, context_ref, count_ref, ready):
+        queries = query_ref[...]
+        for h in range(heads):
+            if h:
+                rest_counts(count_ref, queries, word_ref, h)
+                if h == 1:
+                    ready()
+                    near = near_ref[...]
+                    twice = jnp.concatenate([near, near], axis=0)
             cols = slice(h * dim, (h + 1) * dim)
-            mine = nt(count_ref[...], turned_ref[cols]) * (1.0 / hashes)
-            conv = nn(band_ref[h], twice[:, cols])
-            context_ref[:, cols] = (mine * unit_rows(mine) + conv).astype(BF16)
+            if h:
+                mine = rest_read(count_ref, keys_ref, h)
+                conv = nn(band_ref[h], twice[:, cols])
+                context_ref[:, cols] = (mine * unit_rows(mine) + conv).astype(BF16)
+        mine = first_ref[...]
+        conv = nn(band_ref[0], twice[:, :dim])
+        context_ref[:, :dim] = (mine * unit_rows(mine) + conv).astype(BF16)
 
     (rest_context,) = run(
         rest_body,
         ((rest, local), BF16),
-        (rest_codes, all_keys, wide, tall, low_bands, near),
+        (rest_queries, key_bits, rest_sum, all_keys, low_bands, near),
         "rest_context",
-        far=(0, 1, 2, 3, 4, 5),
-        late=(1, 4, 5),
-        scratch=[pltpu.VMEM((codes_rows, n * tokens), BF16), pltpu.VMEM((local, n * tokens), BF16),
-                 pltpu.VMEM((32, n * tokens), I32), pltpu.VMEM((rest, n * tokens), BF16)],
-        us=12,
+        far=(3, 4, 5),
+        late=(3, 4, 5),
+        scratch=[pltpu.VMEM((rest, n * tokens), BF16)],
+        us=6,
     )
     rest_contexts = [rest_context] + others(rest_context)
 
-    def values_body(ids_ref, mine_ref, other_ref, out_ref, count_ref, band_ref, codes_ref,
-                    grad_ref, dense_ref, attn_ref, *refs, ready):
-        vector_refs, (y_ref, read_ref, reads_ref, sums_ref) = refs[:6], refs[6:]
-        me, side = ids_ref[0], ids_ref[1] % 2
-        own = pl.ds(pl.multiple_of(side * part_width, part_width), part_width)
-        far = pl.ds(pl.multiple_of((1 - side) * part_width, part_width), part_width)
-        for ref, lanes in ((mine_ref, own), (other_ref, far)):
-            for i in range(n):
-                attn_ref[i * chosen : (i + 1) * chosen, lanes] = ref[i, :chosen]
-            sum_all = ref[0, chosen : chosen + 16].astype(F32)
-            for i in range(1, n):
-                sum_all += ref[i, chosen : chosen + 16].astype(F32)
-            sums_ref[:, lanes] = sum_all
-        for i, ref in enumerate(vector_refs):
-            ref[...] = sums_ref[i : i + 1].reshape(width)
-        for i in range(n):
-            for at in range(2):
-                reads_ref[i * chosen + at * (chosen // 2) : i * chosen + (at + 1) * (chosen // 2)] = mine_ref[
-                    i, chosen + 16 :, at * local : (at + 1) * local
-                ]
-        y = nt(attn_ref[...], out_ref[...]).astype(BF16)
-        y_ref[...] = y
+    def values_body(ids_ref, read_ref, count_ref, band_ref, codes_ref, grad_ref, dense_ref, ready):
+        me = ids_ref[0]
         ready()
-        for h in range(heads):
-            cols = slice(h * dim, (h + 1) * dim)
-            read = reads_ref[:, cols].astype(F32)
-            grad = y[:, cols].astype(F32)
-            r = unit_rows(read)
-            back = r * (grad - read * (r * r) * jnp.mean(grad * read, -1, keepdims=True))
-            read_ref[:, cols] = (back * (1.0 / hashes)).astype(BF16)
         dense = jnp.zeros((window, local), F32)
         for step in (-1, 0, 1):
             source = jnp.clip(me + step, 0, n - 1)
             inside = jnp.logical_and(me + step >= 0, me + step < n)
-            there = y_ref[pl.ds(pl.multiple_of(source * chosen, chosen), chosen)]
+            there = read_ref[source][:, local:]
             spots = codes_ref[source][:, codes_rows : codes_rows + 1].astype(F32).astype(I32)
             spots = jnp.where(inside, spots + step * tokens + half, -1)
             place = one_zero(spots == iota((chosen, window), 1))
@@ -603,50 +632,50 @@
         twice = jnp.concatenate([dense_low, dense_low], axis=0)
         for h in range(heads):
             cols = slice(h * dim, (h + 1) * dim)
-            grad = tn(count_ref[h], read_ref[:, cols]) + nn(band_ref[h], twice[:, cols])
+            read = read_ref[:, :, cols].reshape(total, dim)
+            grad = tn(count_ref[h], read) + nn(band_ref[h], twice[:, cols])
             grad_ref[:, cols] = grad.astype(BF16)
 
-    attn_other = swap(lax.optimization_barrier((attn_mine, rest_context))[0], 1)
-    grad_values, dense, attn_all, *vectors = run(
+    grad_values, dense = run(
         values_body,
-        [((tokens, local), BF16), ((window, local), BF16), ((total, width), BF16)] + [((width,), F32)] * 6,
-        (ids, attn_mine, attn_other, out_weight, counts, back_bands, all_codes),
+        [((tokens, local), BF16), ((window, local), BF16)],
+        (ids, read_all, counts, back_bands, all_codes),
         "values_back",
-        far=(3, 4, 5, 6),
-        late=(4, 5, 6),
-        far_out=(2, 3, 4, 5, 6, 7, 8),
         smem=1,
-        scratch=[pltpu.VMEM((total, local), BF16)] * 3 + [
-                 pltpu.VMEM((16, width), F32)],
-        us=6,
+        far=(2, 3, 4),
+        late=(2, 3, 4),
+        us=4,
     )
     grads = [grad_values] + others(grad_values)
 
-    share = local // n
+    piece_rows = local // n
     extra = 8
 
-    def value_grad_body(inputs_ref, grad_ref, dense_ref, near_ref, send_ref, row_ref):
+    def value_grad_body(inputs_ref, grad_ref, dense_ref, near_ref, sums_ref, share_ref, send_ref, row_ref):
         grad = grad_ref[...]
         weight = tn(grad, inputs_ref[...]).astype(BF16)
         row_ref[...] = jnp.zeros_like(row_ref)
         row_ref[:1, :local] = column_sum(grad.astype(F32))
+        row_ref[1:7] = sums_ref[:6]
         turn = one_zero(iota((tokens, tokens), 0) + iota((tokens, tokens), 1) == tokens - 1)
         turned = nn(turn, dense_ref[half : half + tokens]).astype(BF16)
         for h in range(heads):
             cols = slice(h * dim, (h + 1) * dim)
             both = nt(turned[:, cols], near_ref[:, cols])
             aligned = pltpu.roll(both, window - tokens + 1, 1, stride=1, stride_axis=0)
-            row_ref[1 + h : 2 + h, :128] = column_sum(aligned)[:, :128]
+            row_ref[:1, 256 + 128 * h : 384 + 128 * h] = column_sum(aligned)[:, :128]
         for i in range(n):
-            send_ref[i, :share] = weight[i * share : (i + 1) * share]
-            send_ref[i, share:] = row_ref[...].astype(BF16)
+            send_ref[i, :piece_rows] = weight[i * piece_rows : (i + 1) * piece_rows]
+            send_ref[i, piece_rows : piece_rows + extra] = row_ref[...].astype(BF16)
+            send_ref[i, piece_rows + extra :] = share_ref[...]
 
     (value_part,) = run(
         value_grad_body,
-        ((n, share + extra, width), BF16),
-        (inputs, grad_values, dense, near),
+        ((n, piece_rows + extra + part_rows, width), BF16),
+        (inputs, grad_values, dense, near, sums, share),
         "value_grad",
-        far=(0, 3),
+        also=tuple((array, pltpu.HBM) for array in rest_contexts[1:]),
+        far=(0, 3, 4, 5),
         scratch=[pltpu.VMEM((extra, width), F32)],
         us=2.5,
     )
@@ -669,12 +698,13 @@
         (*rest_contexts, *out_all, low_inputs, out_bias, first_gain, first_shift, up_weight, up_bias,
          down_weight),
         "rest_first",
-        far=tuple(range(tp, 2 * tp + 4)) + (2 * tp + 5,),
+        far=tuple(range(2 * tp + 4)) + (2 * tp + 5,),
         late=tuple(range(2 * tp, 2 * tp + 4)) + (2 * tp + 5,),
         far_out=(1,),
         us=4,
     )
     rest_parts = [rest_part] + others(rest_part)
+    keeps = [keeps, swap(lax.optimization_barrier((keeps, rest_part))[0], 1)]
 
     def input_body(*refs):
         grad_refs, weight_refs, (order_ref, hidden_ref, out_ref) = (
@@ -689,85 +719,119 @@
         ((tokens, width), F32),
         (*grads, *value_all, order, grad_hidden),
         "input_grad",
-        far=tuple(range(tp, 2 * tp + 2)),
+        far=tuple(range(2 * tp + 2)),
         far_out=(0,),
-        us=4,
-    )
-
-    def value_sum_body(part_ref, send_ref, bias_ref, taps_ref):
-        whole = part_ref[0].astype(F32)
+        us=0.05,
+    )
+
+    def value_sum_body(part_ref, send_ref, attn_ref, bias_ref, taps_ref, *vector_refs):
+        rows = piece_rows + extra
+        whole = part_ref[0, :rows].astype(F32)
         for i in range(1, n):
-            whole += part_ref[i].astype(F32)
+            whole += part_ref[i, :rows].astype(F32)
         for i in range(n):
-            send_ref[i] = whole[:share].astype(BF16)
-        bias_ref[...] = whole[share : share + 1, :local].reshape(local)
-        taps_ref[...] = whole[share + 1 : share + 1 + heads, :taps]
-
-    value_send_back, grad_value_bias, grad_taps = run(
+            send_ref[i] = whole[:piece_rows].astype(BF16)
+            attn_ref[i] = part_ref[i, rows:]
+        bias_ref[...] = whole[piece_rows : piece_rows + 1, :local].reshape(local)
+        for h in range(heads):
+            taps_ref[h : h + 1] = whole[piece_rows : piece_rows + 1, 256 + 128 * h : 256 + 128 * h + taps]
+        for i, ref in enumerate(vector_refs):
+            ref[...] = whole[piece_rows + 1 + i : piece_rows + 2 + i].reshape(width)
+
+    value_send_back, attn_share, grad_value_bias, grad_taps, *vectors = run(
         value_sum_body,
-        [((n, share, width), BF16), ((local,), F32), ((heads, taps), F32)],
+        [((n, piece_rows, width), BF16), ((n, part_rows, width), BF16), ((local,), F32), ((heads, taps), F32)]
+        + [((width,), F32)] * 6,
         (value_part,),
         "value_sums",
-        far_out=(1, 2),
-        us=1.5,
-    )
-    value_grad = exchange(value_send_back).reshape(local, width).astype(F32).T
-
-    def output_body(*refs):
-        part_refs, refs = refs[:tp], refs[tp:]
-        first_ref, bias_ref, gain_ref, shift_ref, chosen_ref, order_ref, out_ref, sorted_ref = refs
-        second = first_ref[...] + paired([r[...].astype(F32) for r in part_refs]) + line(bias_ref)
+        far_out=tuple(range(2, 10)),
+        us=0.05,
+    )
+    attn_shares = [attn_share] + others(attn_share)
+    value_back = exchange(value_send_back)
+
+    def weights_body(keep_ref, far_ref, up_w_ref, up_bias_ref, down_w_ref,
+                     up_ref, up_sum_ref, grad_ref, act_ref, pre_ref, raw_ref, back_ref, finish):
+        sides = (keep_ref, far_ref)
+        low = jnp.concatenate([ref[:, :, :width].reshape(total // 2, width) for ref in sides], axis=0)
+        down = jnp.concatenate(
+            [ref[:, :, width : 2 * width].reshape(total // 2, width) for ref in sides], axis=0
+        )
+        raw_ref[...] = nn(low, up_w_ref[...])
+        back_ref[...] = nt(down, down_w_ref[...])
+        up_sum = jnp.zeros((1, units), F32)
+        for i in range(n):
+            rows = slice(i * chosen, (i + 1) * chosen)
+            pre = raw_ref[rows] + line(up_bias_ref)
+            cdf = cdf_of(pre)
+            act_ref[rows] = (pre * cdf).astype(BF16)
+            slope = cdf + pre * jnp.exp(-0.5 * pre * pre) * 0.3989422804014327
+            grad_pre = (back_ref[rows] * slope).astype(BF16)
+            pre_ref[rows] = grad_pre
+            up_sum += column_sum(grad_pre.astype(F32))
+        up_sum_ref[...] = up_sum.reshape(units)
+        up_ref[...] = tn(low, pre_ref[...])
+        finish(0)
+        grad_ref[...] = tn(act_ref[...], down)
+
+    grad_up, up_sum, grad_down = run(
+        weights_body,
+        [((width, units), F32), ((units,), F32), ((units, width), F32)],
+        (*keeps, up_weight, up_bias, down_weight),
+        "weights",
+        also=tuple((array, pltpu.VMEM) for array in rest_parts[1:]),
+        far=(0, 1, 3),
+        far_out=(0, 1, 2),
+        early=(0,),
+        scratch=[pltpu.VMEM((total, units), BF16)] * 2 + [pltpu.VMEM((total, units), F32)] * 2,
+        us=3,
+    )
+
+    def last_body(ids_ref, *refs, ready, finish):
+        part_refs, attn_refs, refs = refs[:tp], refs[tp : 2 * tp], refs[2 * tp :]
+        (back_ref, first_ref, bias_ref, gain_ref, shift_ref, chosen_ref, order_ref, keep_ref,
+         out_ref, grad_out_ref, grad_value_ref, sorted_ref, all_ref, context_ref) = refs
+        for i in range(n):
+            grad_value_ref[i * piece_rows : (i + 1) * piece_rows] = back_ref[i].astype(F32)
+        finish(2)
+        for k, ref in enumerate(attn_refs):
+            for i in range(n):
+                start = i * chosen + (ids_ref[1] ^ k) * part_rows
+                all_ref[pl.ds(pl.multiple_of(start, part_rows), part_rows)] = ref[i]
+        second = paired([r[...].astype(F32) for r in part_refs])
+        ready()
+        second = first_ref[...] + second + line(bias_ref)
         unit, _ = norm_stats(second)
         sorted_ref[:chosen] = chosen_ref[...]
         sorted_ref[chosen:] = (unit * line(gain_ref) + line(shift_ref)).astype(BF16)
         out_ref[...] = tn(order_ref[...], sorted_ref[...]).astype(BF16)
-
-    (output,) = run(
-        output_body,
-        ((tokens, width), BF16),
-        (*rest_parts, rest_first, down_bias, second_gain, second_shift, out_chosen, order),
-        "output",
-        far=tuple(range(tp, tp + 6)),
-        far_out=(0,),
-        scratch=[pltpu.VMEM((tokens, width), BF16)],
-        us=3,
-    )
-
-    def weights_body(keep_ref, attn_ref, up_w_ref, up_bias_ref, down_w_ref,
-                     up_ref, up_sum_ref, grad_ref, out_ref, act_ref, pre_ref, finish):
-        up_sum = jnp.zeros((1, units), F32)
+        finish(0)
+        tops = keep_ref[:, :, 2 * width : 2 * width + local].reshape(total // 2, local)
+        lows = keep_ref[:, :, 2 * width + local : 2 * width + 2 * local].reshape(total // 2, local)
         for i in range(n):
-            rows = slice(i * chosen, (i + 1) * chosen)
-            pre = nn(keep_ref[i, :, :width], up_w_ref[...]) + line(up_bias_ref)
-            cdf = cdf_of(pre)
-            act_ref[rows] = (pre * cdf).astype(BF16)
-            slope = cdf + pre * jnp.exp(-0.5 * pre * pre) * 0.3989422804014327
-            grad_pre = (nt(keep_ref[i, :, width : 2 * width], down_w_ref[...]) * slope).astype(BF16)
-            pre_ref[rows] = grad_pre
-            up_sum += column_sum(grad_pre.astype(F32))
-        up_sum_ref[...] = up_sum.reshape(units)
-        up_ref[...] = tn(keep_ref[:, :, :width].reshape(total, width), pre_ref[...])
-        finish(0)
-        grad_ref[...] = tn(act_ref[...], keep_ref[:, :, width : 2 * width].reshape(total, width))
-        finish(2)
-        out_ref[...] = tn(keep_ref[:, :, 2 * width :].reshape(total, local), attn_ref[...])
-
-    grad_up, up_sum, grad_down, grad_out = run(
-        weights_body,
-        [((width, units), F32), ((units,), F32), ((units, width), F32), ((local, width), F32)],
-        (keeps, attn_all, up_weight, up_bias, down_weight),
-        "weights",
-        far=(0, 1, 3),
-        far_out=(0, 1, 2, 3),
+            context_ref[i * chosen : i * chosen + mid] = tops[i * mid : (i + 1) * mid]
+            context_ref[i * chosen + mid : (i + 1) * chosen] = lows[i * mid : (i + 1) * mid]
+        grad_out_ref[...] = tn(context_ref[...], all_ref[...])
+
+    output, grad_out, grad_value = run(
+        last_body,
+        [((tokens, width), BF16), ((local, width), F32), ((local, width), F32)],
+        (ids, *rest_parts, *attn_shares, value_back, rest_first, down_bias, second_gain, second_shift, out_chosen,
+         order, keeps[0]),
+        "last",
+        smem=1,
+        far=tuple(range(2 * tp + 2, 2 * tp + 9)),
+        late=tuple(range(2 * tp + 2, 2 * tp + 9)),
+        far_out=(0, 1, 2),
         early=(0, 2),
-        scratch=[pltpu.VMEM((total, units), BF16)] * 2,
-        us=9,
-    )
-
+        scratch=[pltpu.VMEM((tokens, width), BF16), pltpu.VMEM((total, width), BF16),
+                 pltpu.VMEM((total, local), BF16)],
+        us=0.05,
+    )
     return (
         output,
         input_grad,
-        value_grad,
+        grad_value.T,
         grad_value_bias,
         grad_out,
         vectors[5],

time: 170 us -> 160 us (0.941)
  waiting for transfers between devices: 43.2 us -> 30.4 us
  local copies, waits for them, and re-layouts: 0.02 us -> 5.29 us
  Pallas kernels: 68.2 us -> 65.1 us
    all_to_all x5, waiting for transfers between devices: 23.5 us -> 11 us  [exchange(): return lax.all_to_all(array, 'seq', 0, 0)]
    unnamed x10 -> x48, local copies, waits for them, and re-layouts: 0.02 us -> 5.29 us
    pallas_call x16 -> x17, Pallas kernels: 68.2 us -> 65.1 us  [call(): pl.pallas_call(kernel, out_shape=[spaces[i](arrays[i].shape, arrays[i].dt...]
    ppermute x25 -> x28, waiting for transfers between devices: 19.6 us -> 19.3 us  [swap(): return lax.ppermute(array, 'tp', [(i, i ^ k) for i in range(tp)])]
    ppermute x25 -> x28, starting transfers between devices: 16.8 us -> 17 us  [swap(): return lax.ppermute(array, 'tp', [(i, i ^ k) for i in range(tp)])]
  transfers between devices with their start and end apart: 32 -> 35, of which waited for: 13 -> 11; matrix products, arithmetic and copies ran while one was open for 0% -> 0% of each run, Pallas kernels for 39% -> 37%
where the time goes in v3:
time: 160 us; the launch traced here: 159 us
  Pallas kernels  65.1 us (41%)
  starting transfers between devices  43.4 us (27%)
  waiting for transfers between devices  30.4 us (19%)
  between operations  14.5 us (9%)
  local copies, waits for them, and re-layouts  5.29 us (3%)
    pallas_call x17, Pallas kernels, call(): pl.pallas_call(kernel, out_shape=[spaces[i](arrays[i].shape, arrays[i].dt...  65.1 us
    all_to_all x5, starting transfers between devices, exchange(): return lax.all_to_all(array, 'seq', 0, 0)  26.3 us
    ppermute x28, waiting for transfers between devices, swap(): return lax.ppermute(array, 'tp', [(i, i ^ k) for i in range(tp)])  19.3 us
    ppermute x28, starting transfers between devices, swap(): return lax.ppermute(array, 'tp', [(i, i ^ k) for i in range(tp)])  17 us
    all_to_all x5, waiting for transfers between devices, exchange(): return lax.all_to_all(array, 'seq', 0, 0)  11 us
    unnamed x48, local copies, waits for them, and re-layouts  5.29 us
  transfers between devices with their start and end apart: 35, of which 11 were waited for; matrix products, arithmetic and copies ran while one was open for 0% of the time, Pallas kernels for 37%

profile of v3, /device:TPU:0, one launch (start us, length us, event | category | flops | bytes accessed | tf_op | source)
XLA Modules:
  0.0 158.8 jit_solution(2108767520209859563)
XLA Ops:
  7.2 1.9 %order.1.refs_8_ = bf16[8,64,128]{2,1,0:T(8,128)(2,1)} custom-call(s32[256]{0:T(256)} %refs_6_.2, s32[96,256]{1,0:T(8,128)} %bitcast.20), custom_call_target="tpu_custom_call" | custom-call | flops 2200000000 | tf_op jit(solution)/shard_map/order/pallas_call | solution.py:106
  9.1 7.3 %all-to-all-start = ((bf16[8,64,128]{2,1,0:T(8,128)(2,1)}), bf16[8,64,128]{2,1,0:T(8,128)(2,1)S(1)}, u32[]{:S(2)}, u32[]{:S(2)}) async-start(bf16[8,64,128]{2,1,0:T(8,128)(2,1)} %order.1.refs_8_), calls=%async_computation | async-start | bytes 262144 | tf_op jit(solution)/shard_map/all_to_all | solution.py:238
  16.5 6.3 %prepare.1 = (bf16[256,192]{1,0:T(8,128)(2,1)}, bf16[288,256]{1,0:T(8,128)(2,1)}, bf16[64,768]{1,0:T(8,128)(2,1)}, bf16[192,768]{1,0:T(8,128)(2,1)}, f32[64,768]...) custom-call(bf16[256,768]{1,0:T(8,128)(2,1)} %refs_0_.5, ...), custom_call_target="tpu_custom_call" | custom-call | flops 4400000000 | tf_op jit(solution)/shard_map/prepare/pallas_call | solution.py:106
  23.7 5.3 %count.1 = (bf16[3,512,256]{2,1,0:T(8,128)(2,1)}, bf16[8,96,192]{2,1,0:T(8,128)(2,1)}) custom-call(s32[2]{0:T(128)S(1)} %pad_add_fusion.refs_0_, bf16[8,64,128]{2,1,0:T(8,128)(2,1)S(1)} %all-to-all-done.refs_1_.refs_4_, bf16[288,256]{1,0:T(8,128)(2,1)} %get-tuple-element.68.refs_2_, bf16[256,192]{1,0:T(8,128)(2,1)} %get-tuple-element.69.refs_3_.refs_6_.refs_2_, ...), custom_call_target="tpu_custom_call" | custom-call | flops 5500000256 | tf_op jit(solution)/shard_map/count/pallas_call | solution.py:106
  29.1 5.1 %all-to-all-start.1 = ((bf16[8,96,192]{2,1,0:T(8,128)(2,1)}), bf16[8,96,192]{2,1,0:T(8,128)(2,1)S(1)}, u32[]{:S(2)}, u32[]{:S(2)}) async-start(bf16[8,96,192]{2,1,0:T(8,128)(2,1)} %get-tuple-element.70), calls=%async_computation.1 | async-start | bytes 786432 | tf_op jit(solution)/shard_map/all_to_all | solution.py:238
  34.2 1.6 %collective-permute-start.4 = (bf16[192,768]{1,0:T(8,128)(2,1)S(1)}, bf16[192,768]{1,0:T(8,128)(2,1)S(1)}, u32[]{:S(2)}, u32[]{:S(2)}) collective-permute-start(bf16[192,768]{1,0:T(8,128)(2,1)S(1)} %copy-done.6), channel_id=1, source_target_pairs={{0,2},{1,3},{2,0},{3,1},{4,6},{5,7},{6,4},{7,5},{8,10},{9,11},{10,... | collective-permute-start | bytes 884744 | tf_op jit(solution)/shard_map/ppermute | solution.py:228
  36.3 7.9 %collective-permute-done.4.refs_6_ = bf16[192,768]{1,0:T(8,128)(2,1)S(1)} collective-permute-done((bf16[192,768]{1,0:T(8,128)(2,1)S(1)}, bf16[192,768]{1,0:T(8,128)(2,1)S(1)}, u32[]{:S(2)}, u32[]{:S(2)}) %collective-permute-start.4) | collective-permute-done | bytes 294944 | tf_op jit(solution)/shard_map/ppermute | solution.py:228
  44.2 5.0 %all-to-all-done.1.refs_1_ = bf16[8,96,192]{2,1,0:T(8,128)(2,1)S(1)} async-done(((bf16[8,96,192]{2,1,0:T(8,128)(2,1)}), bf16[8,96,192]{2,1,0:T(8,128)(2,1)S(1)}, u32[]{:S(2)}, u32[]{:S(2)}) %all-to-all-start.1) | async-done | bytes 294944 | tf_op jit(solution)/shard_map/all_to_all | solution.py:238
  49.2 2.4 %context.1 = (bf16[64,192]{1,0:T(8,128)(2,1)S(1)}, f32[64,192]{1,0:T(8,128)S(1)}, bf16[384,192]{1,0:T(8,128)(2,1)}) custom-call(s32[2]{0:T(128)S(1)} %pad_add_fusion.refs_0_, bf16[8,96,192]{2,1,0:T(8,128)(2,1)S(1)} %all-to-all-done.1.refs_1_, bf16[256,192]{1,0:T(8,128)(2,1)} %get-tuple-element.69.refs_3_.refs_6_.refs_2_, ...), custom_call_target="tpu_custom_call" | custom-call | flops 2200000000 | tf_op jit(solution)/shard_map/context/pallas_call | solution.py:106
  52.3 1.5 collective-permute-start.1
  54.7 1.3 collective-permute-done.2.refs_3_
  56.3 3.0 %first.1 = (bf16[64,768]{1,0:T(8,128)(2,1)S(1)}, f32[64,768]{1,0:T(8,128)}, f32[64,768]{1,0:T(8,128)}, f32[64,768]{1,0:T(8,128)}) custom-call(bf16[64,192]{1,0:T(8,128)(2,1)S(1)} %get-tuple-element.73.refs_0_.refs_15_.refs_13_, bf16[64,192]{1,0:T(8,128)(2,1)S(1)} %collective-permute-done.refs_1_, bf16[64,192]{1,0:T(8,128)(2,1)S(1)} %collective-permute-done.1.refs_2_, ...), custom_call_target="tpu_custom_call" | custom-call | flops 3300000000 | tf_op jit(solution)/shard_map/first/pallas_call | solution.py:106
  63.7 2.9 %collective-permute-done.7.refs_3_ = bf16[64,768]{1,0:T(8,128)(2,1)S(1)} collective-permute-done((bf16[64,768]{1,0:T(8,128)(2,1)S(1)}, bf16[64,768]{1,0:T(8,128)(2,1)S(1)}, u32[]{:S(2)}, u32[]{:S(2)}) %collective-permute-start.7) | collective-permute-done | bytes 98336 | tf_op jit(solution)/shard_map/ppermute | solution.py:228
  66.6 3.4 %second.1 = (bf16[64,768]{1,0:T(8,128)(2,1)}, f32[64,768]{1,0:T(8,128)S(1)}, bf16[64,768]{1,0:T(8,128)(2,1)S(1)}, f32[8,768]{1,0:T(8,128)S(1)}, bf16[32,2048]{1,0:T(8,128)(2,1)}) custom-call(s32[2]{0:T(128)S(1)} %pad_add_fusion.refs_0_, bf16[64,768]{1,0:T(8,128)(2,1)S(1)} %get-tuple-element.75.refs_1_, bf16[64,768]{1,0:T(8,128)(2,1)S(1)} %collective-permute-done.6.refs_2_, ...), custom_call_target="tpu_custom_call" | custom-call | flops 3300000000 | tf_op jit(solution)/shard_map/second/pallas_call | solution.py:106
  72.7 5.8 %rest_words.1 = (s32[192,128]{1,0:T(8,128)S(1)}, s32[32,2048]{1,0:T(8,128)S(1)}, f32[192,64]{1,0:T(8,128)S(1)}) custom-call(bf16[192,128]{1,0:T(8,128)(2,1)} %get-tuple-element.67.refs_0_, bf16[8,288,256]{2,1,0:T(8,128)(2,1)} %bitcast.15, bf16[1024,256]{1,0:T(8,128)(2,1)} %constant.13.clone.refs_4_.refs_2_, bf16[64,768]{1,0:T(8,128)(2,1)} %constant.14.clone.refs_5_.refs_3_, ...), custom_call_target="tpu_custom_call" | custom-call | flops 5500000256 | tf_op jit(solution)/shard_map/rest_words/pallas_call | solution.py:106
  78.6 3.4 %hidden.1 = (f32[64,768]{1,0:T(8,128)}, bf16[8,64,384]{2,1,0:T(8,128)(2,1)}, bf16[16,768]{1,0:T(8,128)(2,1)}, f32[8,768]{1,0:T(8,128)}) custom-call(s32[2]{0:T(128)S(1)} %pad_add_fusion.refs_0_, bf16[64,768]{1,0:T(8,128)(2,1)S(1)} %get-tuple-element.85.refs_1_, bf16[64,768]{1,0:T(8,128)(2,1)S(1)} %collective-permute-done.12.refs_2_, ...), custom_call_target="tpu_custom_call" | custom-call | flops 2200000000 | tf_op jit(solution)/shard_map/hidden/pallas_call | solution.py:106
  82.0 4.3 %all-to-all-start.2 = ((bf16[8,64,384]{2,1,0:T(8,128)(2,1)}), bf16[8,64,384]{2,1,0:T(8,128)(2,1)S(1)}, u32[]{:S(2)}, u32[]{:S(2)}) async-start(bf16[8,64,384]{2,1,0:T(8,128)(2,1)} %get-tuple-element.92), calls=%async_computation.2 | async-start | bytes 786432 | tf_op jit(solution)/shard_map/all_to_all | solution.py:238
  86.3 6.2 %rest_context.1.refs_5_.refs_0_ = bf16[192,192]{1,0:T(8,128)(2,1)S(1)} custom-call(s32[192,128]{1,0:T(8,128)S(1)} %get-tuple-element.80.refs_11_.refs_0_, s32[32,2048]{1,0:T(8,128)S(1)} %get-tuple-element.81.refs_1_, f32[192,64]{1,0:T(8,128)S(1)} %get-tuple-element.82.refs_2_, bf16[8,288,256]{2,1,0:T(8,128)(2,1)} %bitcast.17, ...), custom_call_target="tpu_custom_call" | custom-call | flops 6600000000 | tf_op jit(solution)/shard_map/rest_context/pallas_call | solution.py:106
  94.5 5.1 %all-to-all-done.2.refs_1_ = bf16[8,64,384]{2,1,0:T(8,128)(2,1)S(1)} async-done(((bf16[8,64,384]{2,1,0:T(8,128)(2,1)}), bf16[8,64,384]{2,1,0:T(8,128)(2,1)S(1)}, u32[]{:S(2)}, u32[]{:S(2)}) %all-to-all-start.2) | async-done | bytes 393248 | tf_op jit(solution)/shard_map/all_to_all | solution.py:238
  99.6 3.4 %values_back.1 = (bf16[256,192]{1,0:T(8,128)(2,1)S(1)}, bf16[384,192]{1,0:T(8,128)(2,1)S(1)}) custom-call(s32[2]{0:T(128)S(1)} %pad_add_fusion.refs_0_, bf16[8,64,384]{2,1,0:T(8,128)(2,1)S(1)} %all-to-all-done.2.refs_1_, bf16[3,512,256]{2,1,0:T(8,128)(2,1)} %get-tuple-element.72.refs_4_.refs_2_, bf16[3,256,768]{2,1,0:T(8,128)(2,1)} %get-tuple-element.93.refs_3_, ...), custom_call_target="tpu_custom_call" | custom-call | flops 4400000000 | tf_op jit(solution)/shard_map/values_back/pallas_call | solution.py:106
  103.8 2.6 %value_grad.1.refs_15_ = bf16[8,48,768]{2,1,0:T(8,128)(2,1)} custom-call(bf16[256,768]{1,0:T(8,128)(2,1)} %refs_0_.5, bf16[256,192]{1,0:T(8,128)(2,1)S(1)} %get-tuple-element.94.refs_1_.refs_6_.refs_0_, bf16[384,192]{1,0:T(8,128)(2,1)S(1)} %get-tuple-element.95.refs_2_, bf16[384,192]{1,0:T(8,128)(2,1)} %get-tuple-element.84.refs_5_.refs_3_, ...), custom_call_target="tpu_custom_call" | custom-call | flops 2750000128 | tf_op jit(solution)/shard_map/value_grad/pallas_call | solution.py:106
  106.3 3.7 %all-to-all-start.3 = ((bf16[8,48,768]{2,1,0:T(8,128)(2,1)}), bf16[8,48,768]{2,1,0:T(8,128)(2,1)S(1)}, u32[]{:S(2)}, u32[]{:S(2)}) async-start(bf16[8,48,768]{2,1,0:T(8,128)(2,1)} %value_grad.1.refs_15_), calls=%async_computation.3 | async-start | bytes 1179648 | tf_op jit(solution)/shard_map/all_to_all | solution.py:238
  110.0 1.3 copy-done.4
  111.3 4.3 %rest_first.1 = (bf16[192,768]{1,0:T(8,128)(2,1)S(1)}, f32[192,768]{1,0:T(8,128)}) custom-call(bf16[192,192]{1,0:T(8,128)(2,1)} %copy-done.8, bf16[192,192]{1,0:T(8,128)(2,1)} %copy-done.23, bf16[192,192]{1,0:T(8,128)(2,1)} %copy-done.22, bf16[192,192]{1,0:T(8,128)(2,1)} %copy-done.21, bf16[192,768]{1,0:T(8,128)(2,1)} %refs_4_.5, ...), custom_call_target="tpu_custom_call" | custom-call | flops 4400000000 | tf_op jit(solution)/shard_map/rest_first/pallas_call | solution.py:106
  119.1 2.0 %collective-permute-done.23.refs_3_ = bf16[256,192]{1,0:T(8,128)(2,1)S(1)} collective-permute-done((bf16[256,192]{1,0:T(8,128)(2,1)S(1)}, bf16[256,192]{1,0:T(8,128)(2,1)S(1)}, u32[]{:S(2)}, u32[]{:S(2)}) %collective-permute-start.23) | collective-permute-done | bytes 98336 | tf_op jit(solution)/shard_map/ppermute | solution.py:228
  122.1 2.9 %collective-permute-done.22.refs_2_ = bf16[256,192]{1,0:T(8,128)(2,1)S(1)} collective-permute-done((bf16[256,192]{1,0:T(8,128)(2,1)S(1)}, bf16[256,192]{1,0:T(8,128)(2,1)S(1)}, u32[]{:S(2)}, u32[]{:S(2)}) %collective-permute-start.22) | collective-permute-done | bytes 98336 | tf_op jit(solution)/shard_map/ppermute | solution.py:228
  125.7 3.5 %input_grad.1.refs_1_ = f32[256,768]{1,0:T(8,128)} custom-call(bf16[256,192]{1,0:T(8,128)(2,1)} %copy-done, bf16[256,192]{1,0:T(8,128)(2,1)} %copy-done.19, bf16[256,192]{1,0:T(8,128)(2,1)} %copy-done.18, bf16[256,192]{1,0:T(8,128)(2,1)} %copy-done.17, bf16[192,768]{1,0:T(8,128)(2,1)} %bitcast.2.refs_1_.refs_4_, bf16[192,768]{1,0:T(8,128)(2,1)} %copy-done.15, ...), custom_call_target="tpu_custom_call" | custom-call | flops 55000000 | tf_op jit(solution)/shard_map/input_grad/pallas_call | solution.py:106
  129.1 1.4 value_sums.1
  130.6 6.0 %all-to-all-start.4 = ((bf16[8,24,768]{2,1,0:T(8,128)(2,1)}), bf16[8,24,768]{2,1,0:T(8,128)(2,1)S(1)}, u32[]{:S(2)}, u32[]{:S(2)}) async-start(bf16[8,24,768]{2,1,0:T(8,128)(2,1)} %get-tuple-element.101.refs_5_), calls=%async_computation.4 | async-start | bytes 589824 | tf_op jit(solution)/shard_map/all_to_all | solution.py:238
  138.4 1.3 copy-done.5
  139.7 7.2 %weights.1 = (f32[768,768]{1,0:T(8,128)}, f32[768]{0:T(1024)}, f32[768,768]{1,0:T(8,128)}) custom-call(bf16[8,32,2048]{2,1,0:T(8,128)(2,1)} %bitcast.13, bf16[8,32,2048]{2,1,0:T(8,128)(2,1)} %collective-permute-done.27.refs_1_, bf16[768,768]{1,0:T(8,128)(2,1)S(1)} %copy-done.2, f32[768]{0:T(1024)} %refs_3_.2, bf16[768,768]{1,0:T(8,128)(2,1)S(1)} %copy-done.5, ...), custom_call_target="tpu_custom_call" | custom-call | flops 3300000000 | tf_op jit(solution)/shard_map/weights/pallas_call | solution.py:106
  148.0 3.9 %last.1 = (bf16[256,768]{1,0:T(8,128)(2,1)}, f32[192,768]{1,0:T(8,128)}, f32[192,768]{1,0:T(8,128)}) custom-call(s32[2]{0:T(128)S(1)} %pad_add_fusion.refs_0_, bf16[192,768]{1,0:T(8,128)(2,1)S(1)} %get-tuple-element.98.refs_10_.refs_1_, bf16[192,768]{1,0:T(8,128)(2,1)S(1)} %collective-permute-done.18.refs_6_.refs_2_, ...), custom_call_target="tpu_custom_call" | custom-call | flops 55000000 | tf_op jit(solution)/shard_map/last/pallas_call | solution.py:106
  (106 shorter events, 21.2 us)
Async XLA Ops:
  9.1 14.6 %all-to-all-start = ((bf16[8,64,128]{2,1,0:T(8,128)(2,1)}), bf16[8,64,128]{2,1,0:T(8,128)(2,1)S(1)}, u32[]{:S(2)}, u32[]{:S(2)}) async-start(bf16[8,64,128]{2,1,0:T(8,128)(2,1)} %order.1.refs_8_), calls=%async_computation | async-start | bytes 262144 | tf_op jit(solution)/shard_map/all_to_all | solution.py:238
  16.4 56.2 %all-gather.5.cloned.1.call-start = ((), (), s32[]{:S(2)}) async-start(), calls=%async_computation.5 | async-start | bytes 1327104 | tf_op jit(solution)/shard_map/all_gather | solution.py:328
  29.1 20.1 %all-to-all-start.1 = ((bf16[8,96,192]{2,1,0:T(8,128)(2,1)}), bf16[8,96,192]{2,1,0:T(8,128)(2,1)S(1)}, u32[]{:S(2)}, u32[]{:S(2)}) async-start(bf16[8,96,192]{2,1,0:T(8,128)(2,1)} %get-tuple-element.70), calls=%async_computation.1 | async-start | bytes 786432 | tf_op jit(solution)/shard_map/all_to_all | solution.py:238
  34.1 81.5 %all-gather.7.cloned.1.call-start = ((), (), s32[]{:S(2)}) async-start(), calls=%async_computation.6 | async-start | bytes 1179648 | tf_op jit(solution)/shard_map/all_gather | solution.py:510
  34.2 10.0 %collective-permute-start.4 = (bf16[192,768]{1,0:T(8,128)(2,1)S(1)}, bf16[192,768]{1,0:T(8,128)(2,1)S(1)}, u32[]{:S(2)}, u32[]{:S(2)}) collective-permute-start(bf16[192,768]{1,0:T(8,128)(2,1)S(1)} %copy-done.6), channel_id=1, source_target_pairs={{0,2},{1,3},{2,0},{3,1},{4,6},{5,7},{6,4},{7,5},{8,10},{9,11},{10,... | collective-permute-start | bytes 884744 | tf_op jit(solution)/shard_map/ppermute | solution.py:228
  35.8 18.1 %collective-permute-start.10 = (bf16[192,768]{1,0:T(8,128)(2,1)}, bf16[192,768]{1,0:T(8,128)(2,1)}, u32[]{:S(2)}, u32[]{:S(2)}) collective-permute-start(bf16[192,768]{1,0:T(8,128)(2,1)} %bitcast.2.refs_1_.refs_4_), channel_id=1, source_target_pairs={{0,2},{1,3},{2,0},{3,1},{4,6},{5,7},{6,4},{7,5},{8,10},{9,11},{10,... | collective-permute-start | bytes 884744 | tf_op jit(solution)/shard_map/ppermute | solution.py:228
  36.3 17.9 %collective-permute-start.3 = (bf16[192,768]{1,0:T(8,128)(2,1)S(1)}, bf16[192,768]{1,0:T(8,128)(2,1)}, u32[]{:S(2)}, u32[]{:S(2)}) collective-permute-start(bf16[192,768]{1,0:T(8,128)(2,1)S(1)} %copy-done.6), channel_id=1, source_target_pairs={{0,1},{1,0},{2,3},{3,2},{4,5},{5,4},{6,7},{7,6},{8,9},{9,8},{10,11... | collective-permute-start | bytes 884744 | tf_op jit(solution)/shard_map/ppermute | solution.py:228
  44.2 10.1 %collective-permute-start.5 = (bf16[192,768]{1,0:T(8,128)(2,1)S(1)}, bf16[192,768]{1,0:T(8,128)(2,1)}, u32[]{:S(2)}, u32[]{:S(2)}) collective-permute-start(bf16[192,768]{1,0:T(8,128)(2,1)S(1)} %collective-permute-done.4.refs_6_), channel_id=1, source_target_pairs={{0,1},{1,0},{2,3},{3,2},{4,5},{5,4},{6,7},{7,6},{8,9},{9,8},{10,11... | collective-permute-start | bytes 884744 | tf_op jit(solution)/shard_map/ppermute | solution.py:228
  54.2 8.6 %collective-permute-start.9 = (bf16[192,768]{1,0:T(8,128)(2,1)}, bf16[192,768]{1,0:T(8,128)(2,1)S(1)}, u32[]{:S(2)}, u32[]{:S(2)}) collective-permute-start(bf16[192,768]{1,0:T(8,128)(2,1)} %bitcast.2.refs_1_.refs_4_), channel_id=1, source_target_pairs={{0,1},{1,0},{2,3},{3,2},{4,5},{5,4},{6,7},{7,6},{8,9},{9,8},{10,11... | collective-permute-start | bytes 884744 | tf_op jit(solution)/shard_map/ppermute | solution.py:228
  54.3 8.5 %collective-permute-start.11 = (bf16[192,768]{1,0:T(8,128)(2,1)}, bf16[192,768]{1,0:T(8,128)(2,1)S(1)}, u32[]{:S(2)}, u32[]{:S(2)}) collective-permute-start(bf16[192,768]{1,0:T(8,128)(2,1)} %collective-permute-done.10.refs_16_.refs_6_), channel_id=1, source_target_pairs={{0,1},{1,0},{2,3},{3,2},{4,5},{5,4},{6,7},{7,6},{8,9},{9,8},{10,11... | collective-permute-start | bytes 884744 | tf_op jit(solution)/shard_map/ppermute | solution.py:228
  59.3 4.4 %collective-permute-start.8 = (bf16[64,768]{1,0:T(8,128)(2,1)S(1)}, bf16[64,768]{1,0:T(8,128)(2,1)S(1)}, u32[]{:S(2)}, u32[]{:S(2)}) collective-permute-start(bf16[64,768]{1,0:T(8,128)(2,1)S(1)} %get-tuple-element.75.refs_1_), channel_id=1, source_target_pairs={{0,3},{1,2},{2,1},{3,0},{4,7},{5,6},{6,5},{7,4},{8,11},{9,10},{10,... | collective-permute-start | bytes 294920 | tf_op jit(solution)/shard_map/ppermute | solution.py:228
  60.5 6.1 %collective-permute-start.7 = (bf16[64,768]{1,0:T(8,128)(2,1)S(1)}, bf16[64,768]{1,0:T(8,128)(2,1)S(1)}, u32[]{:S(2)}, u32[]{:S(2)}) collective-permute-start(bf16[64,768]{1,0:T(8,128)(2,1)S(1)} %get-tuple-element.75.refs_1_), channel_id=1, source_target_pairs={{0,2},{1,3},{2,0},{3,1},{4,6},{5,7},{6,4},{7,5},{8,10},{9,11},{10,... | collective-permute-start | bytes 294920 | tf_op jit(solution)/shard_map/ppermute | solution.py:228
  61.7 4.8 %collective-permute-start.6 = (bf16[64,768]{1,0:T(8,128)(2,1)S(1)}, bf16[64,768]{1,0:T(8,128)(2,1)S(1)}, u32[]{:S(2)}, u32[]{:S(2)}) collective-permute-start(bf16[64,768]{1,0:T(8,128)(2,1)S(1)} %get-tuple-element.75.refs_1_), channel_id=1, source_target_pairs={{0,1},{1,0},{2,3},{3,2},{4,5},{5,4},{6,7},{7,6},{8,9},{9,8},{10,11... | collective-permute-start | bytes 294920 | tf_op jit(solution)/shard_map/ppermute | solution.py:228
  70.7 7.8 %collective-permute-start.14 = (bf16[64,768]{1,0:T(8,128)(2,1)S(1)}, bf16[64,768]{1,0:T(8,128)(2,1)S(1)}, u32[]{:S(2)}, u32[]{:S(2)}) collective-permute-start(bf16[64,768]{1,0:T(8,128)(2,1)S(1)} %get-tuple-element.85.refs_1_), channel_id=1, source_target_pairs={{0,3},{1,2},{2,1},{3,0},{4,7},{5,6},{6,5},{7,4},{8,11},{9,10},{10,... | collective-permute-start | bytes 294920 | tf_op jit(solution)/shard_map/ppermute | solution.py:228
  71.8 6.7 %collective-permute-start.13 = (bf16[64,768]{1,0:T(8,128)(2,1)S(1)}, bf16[64,768]{1,0:T(8,128)(2,1)S(1)}, u32[]{:S(2)}, u32[]{:S(2)}) collective-permute-start(bf16[64,768]{1,0:T(8,128)(2,1)S(1)} %get-tuple-element.85.refs_1_), channel_id=1, source_target_pairs={{0,2},{1,3},{2,0},{3,1},{4,6},{5,7},{6,4},{7,5},{8,10},{9,11},{10,... | collective-permute-start | bytes 294920 | tf_op jit(solution)/shard_map/ppermute | solution.py:228
  72.2 6.3 %collective-permute-start.12 = (bf16[64,768]{1,0:T(8,128)(2,1)S(1)}, bf16[64,768]{1,0:T(8,128)(2,1)S(1)}, u32[]{:S(2)}, u32[]{:S(2)}) collective-permute-start(bf16[64,768]{1,0:T(8,128)(2,1)S(1)} %get-tuple-element.85.refs_1_), channel_id=1, source_target_pairs={{0,1},{1,0},{2,3},{3,2},{4,5},{5,4},{6,7},{7,6},{8,9},{9,8},{10,11... | collective-permute-start | bytes 294920 | tf_op jit(solution)/shard_map/ppermute | solution.py:228
  82.0 17.6 %all-to-all-start.2 = ((bf16[8,64,384]{2,1,0:T(8,128)(2,1)}), bf16[8,64,384]{2,1,0:T(8,128)(2,1)S(1)}, u32[]{:S(2)}, u32[]{:S(2)}) async-start(bf16[8,64,384]{2,1,0:T(8,128)(2,1)} %get-tuple-element.92), calls=%async_computation.2 | async-start | bytes 786432 | tf_op jit(solution)/shard_map/all_to_all | solution.py:238
  92.5 10.5 %collective-permute-start.17 = (bf16[192,192]{1,0:T(8,128)(2,1)S(1)}, bf16[192,192]{1,0:T(8,128)(2,1)S(1)}, u32[]{:S(2)}, u32[]{:S(2)}) collective-permute-start(bf16[192,192]{1,0:T(8,128)(2,1)S(1)} %rest_context.1.refs_5_.refs_0_), channel_id=1, source_target_pairs={{0,3},{1,2},{2,1},{3,0},{4,7},{5,6},{6,5},{7,4},{8,11},{9,10},{10,... | collective-permute-start | bytes 221192 | tf_op jit(solution)/shard_map/ppermute | solution.py:228
  93.4 9.7 %collective-permute-start.16 = (bf16[192,192]{1,0:T(8,128)(2,1)S(1)}, bf16[192,192]{1,0:T(8,128)(2,1)S(1)}, u32[]{:S(2)}, u32[]{:S(2)}) collective-permute-start(bf16[192,192]{1,0:T(8,128)(2,1)S(1)} %rest_context.1.refs_5_.refs_0_), channel_id=1, source_target_pairs={{0,2},{1,3},{2,0},{3,1},{4,6},{5,7},{6,4},{7,5},{8,10},{9,11},{10,... | collective-permute-start | bytes 221192 | tf_op jit(solution)/shard_map/ppermute | solution.py:228
  94.3 8.7 %collective-permute-start.15 = (bf16[192,192]{1,0:T(8,128)(2,1)S(1)}, bf16[192,192]{1,0:T(8,128)(2,1)S(1)}, u32[]{:S(2)}, u32[]{:S(2)}) collective-permute-start(bf16[192,192]{1,0:T(8,128)(2,1)S(1)} %rest_context.1.refs_5_.refs_0_), channel_id=1, source_target_pairs={{0,1},{1,0},{2,3},{3,2},{4,5},{5,4},{6,7},{7,6},{8,9},{9,8},{10,11... | collective-permute-start | bytes 221192 | tf_op jit(solution)/shard_map/ppermute | solution.py:228
  106.3 22.8 %all-to-all-start.3 = ((bf16[8,48,768]{2,1,0:T(8,128)(2,1)}), bf16[8,48,768]{2,1,0:T(8,128)(2,1)S(1)}, u32[]{:S(2)}, u32[]{:S(2)}) async-start(bf16[8,48,768]{2,1,0:T(8,128)(2,1)} %value_grad.1.refs_15_), calls=%async_computation.3 | async-start | bytes 1179648 | tf_op jit(solution)/shard_map/all_to_all | solution.py:238
  115.7 22.8 %collective-permute-start.27 = (bf16[8,32,2048]{2,1,0:T(8,128)(2,1)}, bf16[8,32,2048]{2,1,0:T(8,128)(2,1)}, u32[]{:S(2)}, u32[]{:S(2)}) collective-permute-start(bf16[8,32,2048]{2,1,0:T(8,128)(2,1)} %bitcast.12), channel_id=1, source_target_pairs={{0,1},{1,0},{2,3},{3,2},{4,5},{5,4},{6,7},{7,6},{8,9},{9,8},{10,11... | collective-permute-start | bytes 3145736 | tf_op jit(solution)/shard_map/ppermute | solution.py:228
  115.7 5.3 %collective-permute-start.23 = (bf16[256,192]{1,0:T(8,128)(2,1)S(1)}, bf16[256,192]{1,0:T(8,128)(2,1)S(1)}, u32[]{:S(2)}, u32[]{:S(2)}) collective-permute-start(bf16[256,192]{1,0:T(8,128)(2,1)S(1)} %get-tuple-element.94.refs_1_.refs_6_.refs_0_), channel_id=1, source_target_pairs={{0,3},{1,2},{2,1},{3,0},{4,7},{5,6},{6,5},{7,4},{8,11},{9,10},{10,... | collective-permute-start | bytes 294920 | tf_op jit(solution)/shard_map/ppermute | solution.py:228
  116.9 8.0 %collective-permute-start.22 = (bf16[256,192]{1,0:T(8,128)(2,1)S(1)}, bf16[256,192]{1,0:T(8,128)(2,1)S(1)}, u32[]{:S(2)}, u32[]{:S(2)}) collective-permute-start(bf16[256,192]{1,0:T(8,128)(2,1)S(1)} %get-tuple-element.94.refs_1_.refs_6_.refs_0_), channel_id=1, source_target_pairs={{0,2},{1,3},{2,0},{3,1},{4,6},{5,7},{6,4},{7,5},{8,10},{9,11},{10,... | collective-permute-start | bytes 294920 | tf_op jit(solution)/shard_map/ppermute | solution.py:228
  117.9 7.1 %collective-permute-start.21 = (bf16[256,192]{1,0:T(8,128)(2,1)S(1)}, bf16[256,192]{1,0:T(8,128)(2,1)S(1)}, u32[]{:S(2)}, u32[]{:S(2)}) collective-permute-start(bf16[256,192]{1,0:T(8,128)(2,1)S(1)} %get-tuple-element.94.refs_1_.refs_6_.refs_0_), channel_id=1, source_target_pairs={{0,1},{1,0},{2,3},{3,2},{4,5},{5,4},{6,7},{7,6},{8,9},{9,8},{10,11... | collective-permute-start | bytes 294920 | tf_op jit(solution)/shard_map/ppermute | solution.py:228
  117.9 19.6 %collective-permute-start.20 = (bf16[192,768]{1,0:T(8,128)(2,1)S(1)}, bf16[192,768]{1,0:T(8,128)(2,1)S(1)}, u32[]{:S(2)}, u32[]{:S(2)}) collective-permute-start(bf16[192,768]{1,0:T(8,128)(2,1)S(1)} %get-tuple-element.98.refs_10_.refs_1_), channel_id=1, source_target_pairs={{0,3},{1,2},{2,1},{3,0},{4,7},{5,6},{6,5},{7,4},{8,11},{9,10},{10,... | collective-permute-start | bytes 884744 | tf_op jit(solution)/shard_map/ppermute | solution.py:228
  121.0 17.4 %collective-permute-start.19 = (bf16[192,768]{1,0:T(8,128)(2,1)S(1)}, bf16[192,768]{1,0:T(8,128)(2,1)S(1)}, u32[]{:S(2)}, u32[]{:S(2)}) collective-permute-start(bf16[192,768]{1,0:T(8,128)(2,1)S(1)} %get-tuple-element.98.refs_10_.refs_1_), channel_id=1, source_target_pairs={{0,2},{1,3},{2,0},{3,1},{4,6},{5,7},{6,4},{7,5},{8,10},{9,11},{10,... | collective-permute-start | bytes 884744 | tf_op jit(solution)/shard_map/ppermute | solution.py:228
  125.0 13.5 %collective-permute-start.18 = (bf16[192,768]{1,0:T(8,128)(2,1)S(1)}, bf16[192,768]{1,0:T(8,128)(2,1)S(1)}, u32[]{:S(2)}, u32[]{:S(2)}) collective-permute-start(bf16[192,768]{1,0:T(8,128)(2,1)S(1)} %get-tuple-element.98.refs_10_.refs_1_), channel_id=1, source_target_pairs={{0,1},{1,0},{2,3},{3,2},{4,5},{5,4},{6,7},{7,6},{8,9},{9,8},{10,11... | collective-permute-start | bytes 884744 | tf_op jit(solution)/shard_map/ppermute | solution.py:228
  130.6 17.4 %all-to-all-start.4 = ((bf16[8,24,768]{2,1,0:T(8,128)(2,1)}), bf16[8,24,768]{2,1,0:T(8,128)(2,1)S(1)}, u32[]{:S(2)}, u32[]{:S(2)}) async-start(bf16[8,24,768]{2,1,0:T(8,128)(2,1)} %get-tuple-element.101.refs_5_), calls=%async_computation.4 | async-start | bytes 589824 | tf_op jit(solution)/shard_map/all_to_all | solution.py:238
  136.6 10.4 %collective-permute-start.26 = (bf16[8,16,768]{2,1,0:T(8,128)(2,1)S(1)}, bf16[8,16,768]{2,1,0:T(8,128)(2,1)S(1)}, u32[]{:S(2)}, u32[]{:S(2)}) collective-permute-start(bf16[8,16,768]{2,1,0:T(8,128)(2,1)S(1)} %get-tuple-element.100.refs_5_), channel_id=1, source_target_pairs={{0,3},{1,2},{2,1},{3,0},{4,7},{5,6},{6,5},{7,4},{8,11},{9,10},{10,... | collective-permute-start | bytes 589832 | tf_op jit(solution)/shard_map/ppermute | solution.py:228
  137.4 10.5 %collective-permute-start.25 = (bf16[8,16,768]{2,1,0:T(8,128)(2,1)S(1)}, bf16[8,16,768]{2,1,0:T(8,128)(2,1)S(1)}, u32[]{:S(2)}, u32[]{:S(2)}) collective-permute-start(bf16[8,16,768]{2,1,0:T(8,128)(2,1)S(1)} %get-tuple-element.100.refs_5_), channel_id=1, source_target_pairs={{0,2},{1,3},{2,0},{3,1},{4,6},{5,7},{6,4},{7,5},{8,10},{9,11},{10,... | collective-permute-start | bytes 589832 | tf_op jit(solution)/shard_map/ppermute | solution.py:228
  138.4 9.6 %collective-permute-start.24 = (bf16[8,16,768]{2,1,0:T(8,128)(2,1)S(1)}, bf16[8,16,768]{2,1,0:T(8,128)(2,1)S(1)}, u32[]{:S(2)}, u32[]{:S(2)}) collective-permute-start(bf16[8,16,768]{2,1,0:T(8,128)(2,1)S(1)} %get-tuple-element.100.refs_5_), channel_id=1, source_target_pairs={{0,1},{1,0},{2,3},{3,2},{4,5},{5,4},{6,7},{7,6},{8,9},{9,8},{10,11... | collective-permute-start | bytes 589832 | tf_op jit(solution)/shard_map/ppermute | solution.py:228
  (27 other events, 124.2 us)
Sparse Core Ops, SparseCore 0:
  22.9 45.0 all-gather.4
  72.7 41.1 all-gather.6

commit v4 on v3

--- a/solution.py
+++ b/solution.py
@@ -698,8 +698,9 @@
         (*rest_contexts, *out_all, low_inputs, out_bias, first_gain, first_shift, up_weight, up_bias,
          down_weight),
         "rest_first",
-        far=tuple(range(2 * tp + 4)) + (2 * tp + 5,),
-        late=tuple(range(2 * tp, 2 * tp + 4)) + (2 * tp + 5,),
+        also=tuple((array, pltpu.HBM) for array in grads[1:]),
+        far=tuple(range(2 * tp + 7)),
+        late=tuple(range(2 * tp, 2 * tp + 7)),
         far_out=(1,),
         us=4,
     )
@@ -780,7 +781,7 @@
         (*keeps, up_weight, up_bias, down_weight),
         "weights",
         also=tuple((array, pltpu.VMEM) for array in rest_parts[1:]),
-        far=(0, 1, 3),
+        far=(0, 1, 2, 3, 4),
         far_out=(0, 1, 2),
         early=(0,),
         scratch=[pltpu.VMEM((total, units), BF16)] * 2 + [pltpu.VMEM((total, units), F32)] * 2,

time: 160 us -> 157 us (0.981)
  starting transfers between devices: 43.4 us -> 40.7 us
  local copies, waits for them, and re-layouts: 5.29 us -> 3.68 us
    all_to_all x5, waiting for transfers between devices: 11 us -> 16.4 us  [exchange(): return lax.all_to_all(array, 'seq', 0, 0)]
    ppermute x28, waiting for transfers between devices: 19.3 us -> 14 us  [swap(): return lax.ppermute(array, 'tp', [(i, i ^ k) for i in range(tp)])]
    all_to_all x5, starting transfers between devices: 26.3 us -> 23.9 us  [exchange(): return lax.all_to_all(array, 'seq', 0, 0)]
    unnamed x48 -> x46, local copies, waits for them, and re-layouts: 5.29 us -> 3.68 us
  transfers between devices with their start and end apart: 35 -> 35, of which waited for: 11 -> 10; matrix products, arithmetic and copies ran while one was open for 0% -> 0% of each run, Pallas kernels for 37% -> 39%
where the time goes in v4:
time: 157 us; the launch traced here: 155 us
  Pallas kernels  66 us (42%)
  starting transfers between devices  40.7 us (26%)
  waiting for transfers between devices  30.5 us (19%)
  between operations  14.5 us (9%)
  local copies, waits for them, and re-layouts  3.68 us (2%)
    pallas_call x17, Pallas kernels, call(): pl.pallas_call(kernel, out_shape=[spaces[i](arrays[i].shape, arrays[i].dt...  66 us
    all_to_all x5, starting transfers between devices, exchange(): return lax.all_to_all(array, 'seq', 0, 0)  23.9 us
    ppermute x28, starting transfers between devices, swap(): return lax.ppermute(array, 'tp', [(i, i ^ k) for i in range(tp)])  16.7 us
    all_to_all x5, waiting for transfers between devices, exchange(): return lax.all_to_all(array, 'seq', 0, 0)  16.4 us
    ppermute x28, waiting for transfers between devices, swap(): return lax.ppermute(array, 'tp', [(i, i ^ k) for i in range(tp)])  14 us
    unnamed x46, local copies, waits for them, and re-layouts  3.68 us
  transfers between devices with their start and end apart: 35, of which 10 were waited for; matrix products, arithmetic and copies ran while one was open for 0% of the time, Pallas kernels for 39%

profile of v4, /device:TPU:0, one launch (start us, length us, event | category | flops | bytes accessed | tf_op | source)
XLA Modules:
  0.0 155.5 jit_solution(969922987366366516)
XLA Ops:
  7.2 1.9 %order.1.refs_8_ = bf16[8,64,128]{2,1,0:T(8,128)(2,1)} custom-call(s32[256]{0:T(256)} %refs_6_.2, s32[96,256]{1,0:T(8,128)} %bitcast.20), custom_call_target="tpu_custom_call" | custom-call | flops 2200000000 | tf_op jit(solution)/shard_map/order/pallas_call | solution.py:106
  9.1 7.3 %all-to-all-start = ((bf16[8,64,128]{2,1,0:T(8,128)(2,1)}), bf16[8,64,128]{2,1,0:T(8,128)(2,1)S(1)}, u32[]{:S(2)}, u32[]{:S(2)}) async-start(bf16[8,64,128]{2,1,0:T(8,128)(2,1)} %order.1.refs_8_), calls=%async_computation | async-start | bytes 262144 | tf_op jit(solution)/shard_map/all_to_all | solution.py:238
  16.5 6.3 %prepare.1 = (bf16[256,192]{1,0:T(8,128)(2,1)}, bf16[288,256]{1,0:T(8,128)(2,1)}, bf16[64,768]{1,0:T(8,128)(2,1)}, bf16[192,768]{1,0:T(8,128)(2,1)}, f32[64,768]...) custom-call(bf16[256,768]{1,0:T(8,128)(2,1)} %refs_0_.5, ...), custom_call_target="tpu_custom_call" | custom-call | flops 4400000000 | tf_op jit(solution)/shard_map/prepare/pallas_call | solution.py:106
  23.7 5.3 %count.1 = (bf16[3,512,256]{2,1,0:T(8,128)(2,1)}, bf16[8,96,192]{2,1,0:T(8,128)(2,1)}) custom-call(s32[2]{0:T(128)S(1)} %pad_add_fusion.refs_0_, bf16[8,64,128]{2,1,0:T(8,128)(2,1)S(1)} %all-to-all-done.refs_1_.refs_4_, bf16[288,256]{1,0:T(8,128)(2,1)} %get-tuple-element.68.refs_2_, bf16[256,192]{1,0:T(8,128)(2,1)} %get-tuple-element.69.refs_3_.refs_6_.refs_2_, ...), custom_call_target="tpu_custom_call" | custom-call | flops 5500000256 | tf_op jit(solution)/shard_map/count/pallas_call | solution.py:106
  29.1 5.1 %all-to-all-start.1 = ((bf16[8,96,192]{2,1,0:T(8,128)(2,1)}), bf16[8,96,192]{2,1,0:T(8,128)(2,1)S(1)}, u32[]{:S(2)}, u32[]{:S(2)}) async-start(bf16[8,96,192]{2,1,0:T(8,128)(2,1)} %get-tuple-element.70), calls=%async_computation.1 | async-start | bytes 786432 | tf_op jit(solution)/shard_map/all_to_all | solution.py:238
  34.2 1.6 %collective-permute-start.4 = (bf16[192,768]{1,0:T(8,128)(2,1)S(1)}, bf16[192,768]{1,0:T(8,128)(2,1)S(1)}, u32[]{:S(2)}, u32[]{:S(2)}) collective-permute-start(bf16[192,768]{1,0:T(8,128)(2,1)S(1)} %copy-done.4), channel_id=1, source_target_pairs={{0,2},{1,3},{2,0},{3,1},{4,6},{5,7},{6,4},{7,5},{8,10},{9,11},{10,... | collective-permute-start | bytes 884744 | tf_op jit(solution)/shard_map/ppermute | solution.py:228
  36.3 7.9 %collective-permute-done.4.refs_6_ = bf16[192,768]{1,0:T(8,128)(2,1)S(1)} collective-permute-done((bf16[192,768]{1,0:T(8,128)(2,1)S(1)}, bf16[192,768]{1,0:T(8,128)(2,1)S(1)}, u32[]{:S(2)}, u32[]{:S(2)}) %collective-permute-start.4) | collective-permute-done | bytes 294944 | tf_op jit(solution)/shard_map/ppermute | solution.py:228
  44.2 5.0 %all-to-all-done.1.refs_1_ = bf16[8,96,192]{2,1,0:T(8,128)(2,1)S(1)} async-done(((bf16[8,96,192]{2,1,0:T(8,128)(2,1)}), bf16[8,96,192]{2,1,0:T(8,128)(2,1)S(1)}, u32[]{:S(2)}, u32[]{:S(2)}) %all-to-all-start.1) | async-done | bytes 294944 | tf_op jit(solution)/shard_map/all_to_all | solution.py:238
  49.2 2.5 %context.1 = (bf16[64,192]{1,0:T(8,128)(2,1)S(1)}, f32[64,192]{1,0:T(8,128)S(1)}, bf16[384,192]{1,0:T(8,128)(2,1)}) custom-call(s32[2]{0:T(128)S(1)} %pad_add_fusion.refs_0_, bf16[8,96,192]{2,1,0:T(8,128)(2,1)S(1)} %all-to-all-done.1.refs_1_, bf16[256,192]{1,0:T(8,128)(2,1)} %get-tuple-element.69.refs_3_.refs_6_.refs_2_, ...), custom_call_target="tpu_custom_call" | custom-call | flops 2200000000 | tf_op jit(solution)/shard_map/context/pallas_call | solution.py:106
  52.3 1.5 collective-permute-start.1
  54.7 1.3 collective-permute-done.2.refs_3_
  56.4 3.0 %first.1 = (bf16[64,768]{1,0:T(8,128)(2,1)S(1)}, f32[64,768]{1,0:T(8,128)}, f32[64,768]{1,0:T(8,128)}, f32[64,768]{1,0:T(8,128)}) custom-call(bf16[64,192]{1,0:T(8,128)(2,1)S(1)} %get-tuple-element.73.refs_0_.refs_15_.refs_13_, bf16[64,192]{1,0:T(8,128)(2,1)S(1)} %collective-permute-done.refs_1_, bf16[64,192]{1,0:T(8,128)(2,1)S(1)} %collective-permute-done.1.refs_2_, ...), custom_call_target="tpu_custom_call" | custom-call | flops 3300000000 | tf_op jit(solution)/shard_map/first/pallas_call | solution.py:106
  59.3 1.2 collective-permute-start.8
  60.5 1.2 collective-permute-start.7
  63.7 2.9 %collective-permute-done.7.refs_3_ = bf16[64,768]{1,0:T(8,128)(2,1)S(1)} collective-permute-done((bf16[64,768]{1,0:T(8,128)(2,1)S(1)}, bf16[64,768]{1,0:T(8,128)(2,1)S(1)}, u32[]{:S(2)}, u32[]{:S(2)}) %collective-permute-start.7) | collective-permute-done | bytes 98336 | tf_op jit(solution)/shard_map/ppermute | solution.py:228
  66.6 3.4 %second.1 = (bf16[64,768]{1,0:T(8,128)(2,1)}, f32[64,768]{1,0:T(8,128)S(1)}, bf16[64,768]{1,0:T(8,128)(2,1)S(1)}, f32[8,768]{1,0:T(8,128)S(1)}, bf16[32,2048]{1,0:T(8,128)(2,1)}) custom-call(s32[2]{0:T(128)S(1)} %pad_add_fusion.refs_0_, bf16[64,768]{1,0:T(8,128)(2,1)S(1)} %get-tuple-element.75.refs_1_, bf16[64,768]{1,0:T(8,128)(2,1)S(1)} %collective-permute-done.6.refs_2_, ...), custom_call_target="tpu_custom_call" | custom-call | flops 3300000000 | tf_op jit(solution)/shard_map/second/pallas_call | solution.py:106
  72.7 5.8 %rest_words.1 = (s32[192,128]{1,0:T(8,128)S(1)}, s32[32,2048]{1,0:T(8,128)S(1)}, f32[192,64]{1,0:T(8,128)S(1)}) custom-call(bf16[192,128]{1,0:T(8,128)(2,1)} %get-tuple-element.67.refs_0_, bf16[8,288,256]{2,1,0:T(8,128)(2,1)} %bitcast.15, bf16[1024,256]{1,0:T(8,128)(2,1)} %constant.13.clone.refs_4_.refs_2_, bf16[64,768]{1,0:T(8,128)(2,1)} %constant.14.clone.refs_5_.refs_3_, ...), custom_call_target="tpu_custom_call" | custom-call | flops 5500000256 | tf_op jit(solution)/shard_map/rest_words/pallas_call | solution.py:106
  78.6 3.5 %hidden.1 = (f32[64,768]{1,0:T(8,128)}, bf16[8,64,384]{2,1,0:T(8,128)(2,1)}, bf16[16,768]{1,0:T(8,128)(2,1)}, f32[8,768]{1,0:T(8,128)}) custom-call(s32[2]{0:T(128)S(1)} %pad_add_fusion.refs_0_, bf16[64,768]{1,0:T(8,128)(2,1)S(1)} %get-tuple-element.85.refs_1_, bf16[64,768]{1,0:T(8,128)(2,1)S(1)} %collective-permute-done.12.refs_2_, ...), custom_call_target="tpu_custom_call" | custom-call | flops 2200000000 | tf_op jit(solution)/shard_map/hidden/pallas_call | solution.py:106
  82.0 4.3 %all-to-all-start.2 = ((bf16[8,64,384]{2,1,0:T(8,128)(2,1)}), bf16[8,64,384]{2,1,0:T(8,128)(2,1)S(1)}, u32[]{:S(2)}, u32[]{:S(2)}) async-start(bf16[8,64,384]{2,1,0:T(8,128)(2,1)} %get-tuple-element.92), calls=%async_computation.2 | async-start | bytes 786432 | tf_op jit(solution)/shard_map/all_to_all | solution.py:238
  86.4 6.2 %rest_context.1.refs_5_.refs_0_ = bf16[192,192]{1,0:T(8,128)(2,1)S(1)} custom-call(s32[192,128]{1,0:T(8,128)S(1)} %get-tuple-element.80.refs_11_.refs_0_, s32[32,2048]{1,0:T(8,128)S(1)} %get-tuple-element.81.refs_1_, f32[192,64]{1,0:T(8,128)S(1)} %get-tuple-element.82.refs_2_, bf16[8,288,256]{2,1,0:T(8,128)(2,1)} %bitcast.17, ...), custom_call_target="tpu_custom_call" | custom-call | flops 6600000000 | tf_op jit(solution)/shard_map/rest_context/pallas_call | solution.py:106
  94.5 5.1 %all-to-all-done.2.refs_1_ = bf16[8,64,384]{2,1,0:T(8,128)(2,1)S(1)} async-done(((bf16[8,64,384]{2,1,0:T(8,128)(2,1)}), bf16[8,64,384]{2,1,0:T(8,128)(2,1)S(1)}, u32[]{:S(2)}, u32[]{:S(2)}) %all-to-all-start.2) | async-done | bytes 393248 | tf_op jit(solution)/shard_map/all_to_all | solution.py:238
  99.6 3.4 %values_back.1 = (bf16[256,192]{1,0:T(8,128)(2,1)S(1)}, bf16[384,192]{1,0:T(8,128)(2,1)S(1)}) custom-call(s32[2]{0:T(128)S(1)} %pad_add_fusion.refs_0_, bf16[8,64,384]{2,1,0:T(8,128)(2,1)S(1)} %all-to-all-done.2.refs_1_, bf16[3,512,256]{2,1,0:T(8,128)(2,1)} %get-tuple-element.72.refs_4_.refs_2_, bf16[3,256,768]{2,1,0:T(8,128)(2,1)} %get-tuple-element.93.refs_3_, ...), custom_call_target="tpu_custom_call" | custom-call | flops 4400000000 | tf_op jit(solution)/shard_map/values_back/pallas_call | solution.py:106
  103.1 1.4 collective-permute-start.19
  105.6 2.6 %value_grad.1.refs_15_ = bf16[8,48,768]{2,1,0:T(8,128)(2,1)} custom-call(bf16[256,768]{1,0:T(8,128)(2,1)} %refs_0_.5, bf16[256,192]{1,0:T(8,128)(2,1)S(1)} %get-tuple-element.94.refs_1_.refs_6_.refs_0_, bf16[384,192]{1,0:T(8,128)(2,1)S(1)} %get-tuple-element.95.refs_2_, bf16[384,192]{1,0:T(8,128)(2,1)} %get-tuple-element.84.refs_5_.refs_3_, ...), custom_call_target="tpu_custom_call" | custom-call | flops 2750000128 | tf_op jit(solution)/shard_map/value_grad/pallas_call | solution.py:106
  108.2 3.6 %all-to-all-start.3 = ((bf16[8,48,768]{2,1,0:T(8,128)(2,1)}), bf16[8,48,768]{2,1,0:T(8,128)(2,1)S(1)}, u32[]{:S(2)}, u32[]{:S(2)}) async-start(bf16[8,48,768]{2,1,0:T(8,128)(2,1)} %value_grad.1.refs_15_), calls=%async_computation.3 | async-start | bytes 1179648 | tf_op jit(solution)/shard_map/all_to_all | solution.py:238
  112.6 4.6 %rest_first.1 = (bf16[192,768]{1,0:T(8,128)(2,1)S(1)}, f32[192,768]{1,0:T(8,128)}) custom-call(bf16[192,192]{1,0:T(8,128)(2,1)} %copy-done.6, bf16[192,192]{1,0:T(8,128)(2,1)} %copy-done.22, bf16[192,192]{1,0:T(8,128)(2,1)} %copy-done.21, bf16[192,192]{1,0:T(8,128)(2,1)} %copy-done.20, bf16[192,768]{1,0:T(8,128)(2,1)} %refs_4_.5, ...), custom_call_target="tpu_custom_call" | custom-call | flops 4400000000 | tf_op jit(solution)/shard_map/rest_first/pallas_call | solution.py:106
  119.4 3.5 %input_grad.1.refs_1_ = f32[256,768]{1,0:T(8,128)} custom-call(bf16[256,192]{1,0:T(8,128)(2,1)} %copy-done, bf16[256,192]{1,0:T(8,128)(2,1)} %copy-done.17, bf16[256,192]{1,0:T(8,128)(2,1)} %copy-done.16, bf16[256,192]{1,0:T(8,128)(2,1)} %copy-done.15, bf16[192,768]{1,0:T(8,128)(2,1)} %bitcast.2.refs_1_.refs_4_, bf16[192,768]{1,0:T(8,128)(2,1)} %copy-done.13, ...), custom_call_target="tpu_custom_call" | custom-call | flops 55000000 | tf_op jit(solution)/shard_map/input_grad/pallas_call | solution.py:106
  122.9 5.4 %all-to-all-done.3.refs_0_ = bf16[8,48,768]{2,1,0:T(8,128)(2,1)S(1)} async-done(((bf16[8,48,768]{2,1,0:T(8,128)(2,1)}), bf16[8,48,768]{2,1,0:T(8,128)(2,1)S(1)}, u32[]{:S(2)}, u32[]{:S(2)}) %all-to-all-start.3) | async-done | bytes 589856 | tf_op jit(solution)/shard_map/all_to_all | solution.py:238
  128.3 1.4 value_sums.1
  129.8 3.6 %all-to-all-start.4 = ((bf16[8,24,768]{2,1,0:T(8,128)(2,1)}), bf16[8,24,768]{2,1,0:T(8,128)(2,1)S(1)}, u32[]{:S(2)}, u32[]{:S(2)}) async-start(bf16[8,24,768]{2,1,0:T(8,128)(2,1)} %get-tuple-element.101.refs_5_), calls=%async_computation.4 | async-start | bytes 589824 | tf_op jit(solution)/shard_map/all_to_all | solution.py:238
  136.2 7.9 %weights.1 = (f32[768,768]{1,0:T(8,128)}, f32[768]{0:T(1024)}, f32[768,768]{1,0:T(8,128)}) custom-call(bf16[8,32,2048]{2,1,0:T(8,128)(2,1)} %bitcast.13, bf16[8,32,2048]{2,1,0:T(8,128)(2,1)} %copy-done.18, bf16[768,768]{1,0:T(8,128)(2,1)} %refs_2_.4, f32[768]{0:T(1024)} %refs_3_.2, bf16[768,768]{1,0:T(8,128)(2,1)} %refs_4_.6, ...), custom_call_target="tpu_custom_call" | custom-call | flops 3300000000 | tf_op jit(solution)/shard_map/weights/pallas_call | solution.py:106
  144.7 3.9 %last.1 = (bf16[256,768]{1,0:T(8,128)(2,1)}, f32[192,768]{1,0:T(8,128)}, f32[192,768]{1,0:T(8,128)}) custom-call(s32[2]{0:T(128)S(1)} %pad_add_fusion.refs_0_, bf16[192,768]{1,0:T(8,128)(2,1)S(1)} %get-tuple-element.98.refs_10_.refs_1_, bf16[192,768]{1,0:T(8,128)(2,1)S(1)} %collective-permute-done.21.refs_6_.refs_2_, ...), custom_call_target="tpu_custom_call" | custom-call | flops 55000000 | tf_op jit(solution)/shard_map/last/pallas_call | solution.py:106
  (104 shorter events, 17.5 us)
Async XLA Ops:
  9.1 14.6 %all-to-all-start = ((bf16[8,64,128]{2,1,0:T(8,128)(2,1)}), bf16[8,64,128]{2,1,0:T(8,128)(2,1)S(1)}, u32[]{:S(2)}, u32[]{:S(2)}) async-start(bf16[8,64,128]{2,1,0:T(8,128)(2,1)} %order.1.refs_8_), calls=%async_computation | async-start | bytes 262144 | tf_op jit(solution)/shard_map/all_to_all | solution.py:238
  16.4 56.2 %all-gather.5.cloned.1.call-start = ((), (), s32[]{:S(2)}) async-start(), calls=%async_computation.5 | async-start | bytes 1327104 | tf_op jit(solution)/shard_map/all_gather | solution.py:328
  29.1 20.1 %all-to-all-start.1 = ((bf16[8,96,192]{2,1,0:T(8,128)(2,1)}), bf16[8,96,192]{2,1,0:T(8,128)(2,1)S(1)}, u32[]{:S(2)}, u32[]{:S(2)}) async-start(bf16[8,96,192]{2,1,0:T(8,128)(2,1)} %get-tuple-element.70), calls=%async_computation.1 | async-start | bytes 786432 | tf_op jit(solution)/shard_map/all_to_all | solution.py:238
  34.1 83.1 %all-gather.7.cloned.1.call-start = ((), (), s32[]{:S(2)}) async-start(), calls=%async_computation.6 | async-start | bytes 1179648 | tf_op jit(solution)/shard_map/all_gather | solution.py:510
  34.2 10.0 %collective-permute-start.4 = (bf16[192,768]{1,0:T(8,128)(2,1)S(1)}, bf16[192,768]{1,0:T(8,128)(2,1)S(1)}, u32[]{:S(2)}, u32[]{:S(2)}) collective-permute-start(bf16[192,768]{1,0:T(8,128)(2,1)S(1)} %copy-done.4), channel_id=1, source_target_pairs={{0,2},{1,3},{2,0},{3,1},{4,6},{5,7},{6,4},{7,5},{8,10},{9,11},{10,... | collective-permute-start | bytes 884744 | tf_op jit(solution)/shard_map/ppermute | solution.py:228
  35.8 18.1 %collective-permute-start.10 = (bf16[192,768]{1,0:T(8,128)(2,1)}, bf16[192,768]{1,0:T(8,128)(2,1)}, u32[]{:S(2)}, u32[]{:S(2)}) collective-permute-start(bf16[192,768]{1,0:T(8,128)(2,1)} %bitcast.2.refs_1_.refs_4_), channel_id=1, source_target_pairs={{0,2},{1,3},{2,0},{3,1},{4,6},{5,7},{6,4},{7,5},{8,10},{9,11},{10,... | collective-permute-start | bytes 884744 | tf_op jit(solution)/shard_map/ppermute | solution.py:228
  36.3 17.9 %collective-permute-start.3 = (bf16[192,768]{1,0:T(8,128)(2,1)S(1)}, bf16[192,768]{1,0:T(8,128)(2,1)}, u32[]{:S(2)}, u32[]{:S(2)}) collective-permute-start(bf16[192,768]{1,0:T(8,128)(2,1)S(1)} %copy-done.4), channel_id=1, source_target_pairs={{0,1},{1,0},{2,3},{3,2},{4,5},{5,4},{6,7},{7,6},{8,9},{9,8},{10,11... | collective-permute-start | bytes 884744 | tf_op jit(solution)/shard_map/ppermute | solution.py:228
  44.2 10.2 %collective-permute-start.5 = (bf16[192,768]{1,0:T(8,128)(2,1)S(1)}, bf16[192,768]{1,0:T(8,128)(2,1)}, u32[]{:S(2)}, u32[]{:S(2)}) collective-permute-start(bf16[192,768]{1,0:T(8,128)(2,1)S(1)} %collective-permute-done.4.refs_6_), channel_id=1, source_target_pairs={{0,1},{1,0},{2,3},{3,2},{4,5},{5,4},{6,7},{7,6},{8,9},{9,8},{10,11... | collective-permute-start | bytes 884744 | tf_op jit(solution)/shard_map/ppermute | solution.py:228
  54.2 8.6 %collective-permute-start.9 = (bf16[192,768]{1,0:T(8,128)(2,1)}, bf16[192,768]{1,0:T(8,128)(2,1)S(1)}, u32[]{:S(2)}, u32[]{:S(2)}) collective-permute-start(bf16[192,768]{1,0:T(8,128)(2,1)} %bitcast.2.refs_1_.refs_4_), channel_id=1, source_target_pairs={{0,1},{1,0},{2,3},{3,2},{4,5},{5,4},{6,7},{7,6},{8,9},{9,8},{10,11... | collective-permute-start | bytes 884744 | tf_op jit(solution)/shard_map/ppermute | solution.py:228
  54.4 8.4 %collective-permute-start.11 = (bf16[192,768]{1,0:T(8,128)(2,1)}, bf16[192,768]{1,0:T(8,128)(2,1)S(1)}, u32[]{:S(2)}, u32[]{:S(2)}) collective-permute-start(bf16[192,768]{1,0:T(8,128)(2,1)} %collective-permute-done.10.refs_16_.refs_6_), channel_id=1, source_target_pairs={{0,1},{1,0},{2,3},{3,2},{4,5},{5,4},{6,7},{7,6},{8,9},{9,8},{10,11... | collective-permute-start | bytes 884744 | tf_op jit(solution)/shard_map/ppermute | solution.py:228
  59.3 4.4 %collective-permute-start.8 = (bf16[64,768]{1,0:T(8,128)(2,1)S(1)}, bf16[64,768]{1,0:T(8,128)(2,1)S(1)}, u32[]{:S(2)}, u32[]{:S(2)}) collective-permute-start(bf16[64,768]{1,0:T(8,128)(2,1)S(1)} %get-tuple-element.75.refs_1_), channel_id=1, source_target_pairs={{0,3},{1,2},{2,1},{3,0},{4,7},{5,6},{6,5},{7,4},{8,11},{9,10},{10,... | collective-permute-start | bytes 294920 | tf_op jit(solution)/shard_map/ppermute | solution.py:228
  60.5 6.1 %collective-permute-start.7 = (bf16[64,768]{1,0:T(8,128)(2,1)S(1)}, bf16[64,768]{1,0:T(8,128)(2,1)S(1)}, u32[]{:S(2)}, u32[]{:S(2)}) collective-permute-start(bf16[64,768]{1,0:T(8,128)(2,1)S(1)} %get-tuple-element.75.refs_1_), channel_id=1, source_target_pairs={{0,2},{1,3},{2,0},{3,1},{4,6},{5,7},{6,4},{7,5},{8,10},{9,11},{10,... | collective-permute-start | bytes 294920 | tf_op jit(solution)/shard_map/ppermute | solution.py:228
  61.7 4.9 %collective-permute-start.6 = (bf16[64,768]{1,0:T(8,128)(2,1)S(1)}, bf16[64,768]{1,0:T(8,128)(2,1)S(1)}, u32[]{:S(2)}, u32[]{:S(2)}) collective-permute-start(bf16[64,768]{1,0:T(8,128)(2,1)S(1)} %get-tuple-element.75.refs_1_), channel_id=1, source_target_pairs={{0,1},{1,0},{2,3},{3,2},{4,5},{5,4},{6,7},{7,6},{8,9},{9,8},{10,11... | collective-permute-start | bytes 294920 | tf_op jit(solution)/shard_map/ppermute | solution.py:228
  70.7 7.8 %collective-permute-start.14 = (bf16[64,768]{1,0:T(8,128)(2,1)S(1)}, bf16[64,768]{1,0:T(8,128)(2,1)S(1)}, u32[]{:S(2)}, u32[]{:S(2)}) collective-permute-start(bf16[64,768]{1,0:T(8,128)(2,1)S(1)} %get-tuple-element.85.refs_1_), channel_id=1, source_target_pairs={{0,3},{1,2},{2,1},{3,0},{4,7},{5,6},{6,5},{7,4},{8,11},{9,10},{10,... | collective-permute-start | bytes 294920 | tf_op jit(solution)/shard_map/ppermute | solution.py:228
  71.8 6.7 %collective-permute-start.13 = (bf16[64,768]{1,0:T(8,128)(2,1)S(1)}, bf16[64,768]{1,0:T(8,128)(2,1)S(1)}, u32[]{:S(2)}, u32[]{:S(2)}) collective-permute-start(bf16[64,768]{1,0:T(8,128)(2,1)S(1)} %get-tuple-element.85.refs_1_), channel_id=1, source_target_pairs={{0,2},{1,3},{2,0},{3,1},{4,6},{5,7},{6,4},{7,5},{8,10},{9,11},{10,... | collective-permute-start | bytes 294920 | tf_op jit(solution)/shard_map/ppermute | solution.py:228
  72.2 6.3 %collective-permute-start.12 = (bf16[64,768]{1,0:T(8,128)(2,1)S(1)}, bf16[64,768]{1,0:T(8,128)(2,1)S(1)}, u32[]{:S(2)}, u32[]{:S(2)}) collective-permute-start(bf16[64,768]{1,0:T(8,128)(2,1)S(1)} %get-tuple-element.85.refs_1_), channel_id=1, source_target_pairs={{0,1},{1,0},{2,3},{3,2},{4,5},{5,4},{6,7},{7,6},{8,9},{9,8},{10,11... | collective-permute-start | bytes 294920 | tf_op jit(solution)/shard_map/ppermute | solution.py:228
  82.0 17.6 %all-to-all-start.2 = ((bf16[8,64,384]{2,1,0:T(8,128)(2,1)}), bf16[8,64,384]{2,1,0:T(8,128)(2,1)S(1)}, u32[]{:S(2)}, u32[]{:S(2)}) async-start(bf16[8,64,384]{2,1,0:T(8,128)(2,1)} %get-tuple-element.92), calls=%async_computation.2 | async-start | bytes 786432 | tf_op jit(solution)/shard_map/all_to_all | solution.py:238
  92.6 11.9 %collective-permute-start.17 = (bf16[192,192]{1,0:T(8,128)(2,1)S(1)}, bf16[192,192]{1,0:T(8,128)(2,1)S(1)}, u32[]{:S(2)}, u32[]{:S(2)}) collective-permute-start(bf16[192,192]{1,0:T(8,128)(2,1)S(1)} %rest_context.1.refs_5_.refs_0_), channel_id=1, source_target_pairs={{0,3},{1,2},{2,1},{3,0},{4,7},{5,6},{6,5},{7,4},{8,11},{9,10},{10,... | collective-permute-start | bytes 221192 | tf_op jit(solution)/shard_map/ppermute | solution.py:228
  93.4 11.6 %collective-permute-start.16 = (bf16[192,192]{1,0:T(8,128)(2,1)S(1)}, bf16[192,192]{1,0:T(8,128)(2,1)S(1)}, u32[]{:S(2)}, u32[]{:S(2)}) collective-permute-start(bf16[192,192]{1,0:T(8,128)(2,1)S(1)} %rest_context.1.refs_5_.refs_0_), channel_id=1, source_target_pairs={{0,2},{1,3},{2,0},{3,1},{4,6},{5,7},{6,4},{7,5},{8,10},{9,11},{10,... | collective-permute-start | bytes 221192 | tf_op jit(solution)/shard_map/ppermute | solution.py:228
  94.3 10.6 %collective-permute-start.15 = (bf16[192,192]{1,0:T(8,128)(2,1)S(1)}, bf16[192,192]{1,0:T(8,128)(2,1)S(1)}, u32[]{:S(2)}, u32[]{:S(2)}) collective-permute-start(bf16[192,192]{1,0:T(8,128)(2,1)S(1)} %rest_context.1.refs_5_.refs_0_), channel_id=1, source_target_pairs={{0,1},{1,0},{2,3},{3,2},{4,5},{5,4},{6,7},{7,6},{8,9},{9,8},{10,11... | collective-permute-start | bytes 221192 | tf_op jit(solution)/shard_map/ppermute | solution.py:228
  103.0 8.8 %collective-permute-start.20 = (bf16[256,192]{1,0:T(8,128)(2,1)S(1)}, bf16[256,192]{1,0:T(8,128)(2,1)S(1)}, u32[]{:S(2)}, u32[]{:S(2)}) collective-permute-start(bf16[256,192]{1,0:T(8,128)(2,1)S(1)} %get-tuple-element.94.refs_1_.refs_6_.refs_0_), channel_id=1, source_target_pairs={{0,3},{1,2},{2,1},{3,0},{4,7},{5,6},{6,5},{7,4},{8,11},{9,10},{10,... | collective-permute-start | bytes 294920 | tf_op jit(solution)/shard_map/ppermute | solution.py:228
  103.1 8.8 %collective-permute-start.19 = (bf16[256,192]{1,0:T(8,128)(2,1)S(1)}, bf16[256,192]{1,0:T(8,128)(2,1)S(1)}, u32[]{:S(2)}, u32[]{:S(2)}) collective-permute-start(bf16[256,192]{1,0:T(8,128)(2,1)S(1)} %get-tuple-element.94.refs_1_.refs_6_.refs_0_), channel_id=1, source_target_pairs={{0,2},{1,3},{2,0},{3,1},{4,6},{5,7},{6,4},{7,5},{8,10},{9,11},{10,... | collective-permute-start | bytes 294920 | tf_op jit(solution)/shard_map/ppermute | solution.py:228
  104.5 7.4 %collective-permute-start.18 = (bf16[256,192]{1,0:T(8,128)(2,1)S(1)}, bf16[256,192]{1,0:T(8,128)(2,1)S(1)}, u32[]{:S(2)}, u32[]{:S(2)}) collective-permute-start(bf16[256,192]{1,0:T(8,128)(2,1)S(1)} %get-tuple-element.94.refs_1_.refs_6_.refs_0_), channel_id=1, source_target_pairs={{0,1},{1,0},{2,3},{3,2},{4,5},{5,4},{6,7},{7,6},{8,9},{9,8},{10,11... | collective-permute-start | bytes 294920 | tf_op jit(solution)/shard_map/ppermute | solution.py:228
  108.2 20.1 %all-to-all-start.3 = ((bf16[8,48,768]{2,1,0:T(8,128)(2,1)}), bf16[8,48,768]{2,1,0:T(8,128)(2,1)S(1)}, u32[]{:S(2)}, u32[]{:S(2)}) async-start(bf16[8,48,768]{2,1,0:T(8,128)(2,1)} %value_grad.1.refs_15_), calls=%async_computation.3 | async-start | bytes 1179648 | tf_op jit(solution)/shard_map/all_to_all | solution.py:238
  117.2 18.0 %collective-permute-start.27 = (bf16[8,32,2048]{2,1,0:T(8,128)(2,1)}, bf16[8,32,2048]{2,1,0:T(8,128)(2,1)S(1)}, u32[]{:S(2)}, u32[]{:S(2)}) collective-permute-start(bf16[8,32,2048]{2,1,0:T(8,128)(2,1)} %bitcast.12), channel_id=1, source_target_pairs={{0,1},{1,0},{2,3},{3,2},{4,5},{5,4},{6,7},{7,6},{8,9},{9,8},{10,11... | collective-permute-start | bytes 3145736 | tf_op jit(solution)/shard_map/ppermute | solution.py:228
  117.5 16.3 %collective-permute-start.23 = (bf16[192,768]{1,0:T(8,128)(2,1)S(1)}, bf16[192,768]{1,0:T(8,128)(2,1)S(1)}, u32[]{:S(2)}, u32[]{:S(2)}) collective-permute-start(bf16[192,768]{1,0:T(8,128)(2,1)S(1)} %get-tuple-element.98.refs_10_.refs_1_), channel_id=1, source_target_pairs={{0,3},{1,2},{2,1},{3,0},{4,7},{5,6},{6,5},{7,4},{8,11},{9,10},{10,... | collective-permute-start | bytes 884744 | tf_op jit(solution)/shard_map/ppermute | solution.py:228
  118.5 16.3 %collective-permute-start.22 = (bf16[192,768]{1,0:T(8,128)(2,1)S(1)}, bf16[192,768]{1,0:T(8,128)(2,1)S(1)}, u32[]{:S(2)}, u32[]{:S(2)}) collective-permute-start(bf16[192,768]{1,0:T(8,128)(2,1)S(1)} %get-tuple-element.98.refs_10_.refs_1_), channel_id=1, source_target_pairs={{0,2},{1,3},{2,0},{3,1},{4,6},{5,7},{6,4},{7,5},{8,10},{9,11},{10,... | collective-permute-start | bytes 884744 | tf_op jit(solution)/shard_map/ppermute | solution.py:228
  119.4 15.8 %collective-permute-start.21 = (bf16[192,768]{1,0:T(8,128)(2,1)S(1)}, bf16[192,768]{1,0:T(8,128)(2,1)S(1)}, u32[]{:S(2)}, u32[]{:S(2)}) collective-permute-start(bf16[192,768]{1,0:T(8,128)(2,1)S(1)} %get-tuple-element.98.refs_10_.refs_1_), channel_id=1, source_target_pairs={{0,1},{1,0},{2,3},{3,2},{4,5},{5,4},{6,7},{7,6},{8,9},{9,8},{10,11... | collective-permute-start | bytes 884744 | tf_op jit(solution)/shard_map/ppermute | solution.py:228
  129.8 14.9 %all-to-all-start.4 = ((bf16[8,24,768]{2,1,0:T(8,128)(2,1)}), bf16[8,24,768]{2,1,0:T(8,128)(2,1)S(1)}, u32[]{:S(2)}, u32[]{:S(2)}) async-start(bf16[8,24,768]{2,1,0:T(8,128)(2,1)} %get-tuple-element.101.refs_5_), calls=%async_computation.4 | async-start | bytes 589824 | tf_op jit(solution)/shard_map/all_to_all | solution.py:238
  133.4 10.7 %collective-permute-start.26 = (bf16[8,16,768]{2,1,0:T(8,128)(2,1)S(1)}, bf16[8,16,768]{2,1,0:T(8,128)(2,1)S(1)}, u32[]{:S(2)}, u32[]{:S(2)}) collective-permute-start(bf16[8,16,768]{2,1,0:T(8,128)(2,1)S(1)} %get-tuple-element.100.refs_5_), channel_id=1, source_target_pairs={{0,3},{1,2},{2,1},{3,0},{4,7},{5,6},{6,5},{7,4},{8,11},{9,10},{10,... | collective-permute-start | bytes 589832 | tf_op jit(solution)/shard_map/ppermute | solution.py:228
  133.7 10.9 %collective-permute-start.25 = (bf16[8,16,768]{2,1,0:T(8,128)(2,1)S(1)}, bf16[8,16,768]{2,1,0:T(8,128)(2,1)S(1)}, u32[]{:S(2)}, u32[]{:S(2)}) collective-permute-start(bf16[8,16,768]{2,1,0:T(8,128)(2,1)S(1)} %get-tuple-element.100.refs_5_), channel_id=1, source_target_pairs={{0,2},{1,3},{2,0},{3,1},{4,6},{5,7},{6,4},{7,5},{8,10},{9,11},{10,... | collective-permute-start | bytes 589832 | tf_op jit(solution)/shard_map/ppermute | solution.py:228
  134.8 9.9 %collective-permute-start.24 = (bf16[8,16,768]{2,1,0:T(8,128)(2,1)S(1)}, bf16[8,16,768]{2,1,0:T(8,128)(2,1)S(1)}, u32[]{:S(2)}, u32[]{:S(2)}) collective-permute-start(bf16[8,16,768]{2,1,0:T(8,128)(2,1)S(1)} %get-tuple-element.100.refs_5_), channel_id=1, source_target_pairs={{0,1},{1,0},{2,3},{3,2},{4,5},{5,4},{6,7},{7,6},{8,9},{9,8},{10,11... | collective-permute-start | bytes 589832 | tf_op jit(solution)/shard_map/ppermute | solution.py:228
  (26 other events, 109.6 us)
Sparse Core Ops, SparseCore 0:
  22.9 45.0 all-gather.4
  72.7 41.0 all-gather.6

commit v5 on v4

--- a/solution.py
+++ b/solution.py
@@ -327,8 +327,7 @@
     )
     all_keys = lax.all_gather(value_send, "seq", axis=0)
 
-    def count_body(ids_ref, codes_ref, send_ref, value_ref, wide_ref, tall_ref, count_ref, out_ref, ready, finish):
-        me = ids_ref[0]
+    def count_body(codes_ref, send_ref, wide_ref, tall_ref, count_ref, out_ref, finish):
         keys = key_words(send_ref[:codes_rows], tall_ref[...])
         queries = query_words(codes_ref[...].reshape(total, 128), wide_ref[...])
         for h in range(heads):
@@ -343,42 +342,34 @@
             read = nt(count_ref[h], turned).astype(BF16)
             for i in range(n):
                 out_ref[i, :chosen, h * dim : (h + 1) * dim] = read[i * chosen : (i + 1) * chosen]
-        ready()
-        for i in range(n):
-            last, head_rows = value_ref[tokens - half :], value_ref[:half]
-            rows = jnp.where(i == me + 1, last.astype(F32), head_rows.astype(F32))
-            out_ref[i, chosen:] = rows.astype(BF16)
 
     counts, reads = run(
         count_body,
-        [((heads, total, tokens), BF16), ((n, chosen + half, local), BF16)],
-        (ids, all_codes, value_send, values, wide, tall),
+        [((heads, total, tokens), BF16), ((n, chosen, local), BF16)],
+        (all_codes, value_send, wide, tall),
         "count",
-        far=(3,),
-        late=(3,),
         far_out=(0,),
         early=(0,),
-        smem=1,
         us=5,
     )
+    edges = lax.optimization_barrier((values, reads))[0]
+    before = lax.ppermute(edges[tokens - half :], "seq", [(i, i + 1) for i in range(n - 1)])
+    behind = lax.ppermute(edges[:half], "seq", [(i + 1, i) for i in range(n - 1)])
     reads = exchange(reads)
 
     def unit_rows(value_sum):
         return lax.rsqrt(jnp.mean(value_sum * value_sum, -1, keepdims=True) + 1e-05)
 
-    def context_body(ids_ref, reads_ref, value_ref, band_ref, context_ref, sum_ref, near_ref, ready, finish):
-        me = ids_ref[0]
-        total_read = reads_ref[0, :chosen].astype(F32)
+    def context_body(reads_ref, value_ref, band_ref, before_ref, behind_ref, context_ref, sum_ref, near_ref, ready, finish):
+        total_read = reads_ref[0].astype(F32)
         for i in range(1, n):
-            total_read += reads_ref[i, :chosen].astype(F32)
+            total_read += reads_ref[i].astype(F32)
         total_read = total_read * (1.0 / hashes)
         sum_ref[...] = total_read
-        before = reads_ref[jnp.maximum(me - 1, 0), chosen:].astype(F32)
-        after = reads_ref[jnp.minimum(me + 1, n - 1), chosen:].astype(F32)
-        near_ref[:half] = jnp.where(me > 0, before, 0.0).astype(BF16)
+        near_ref[:half] = before_ref[...]
         ready()
         near_ref[half : half + tokens] = value_ref[...]
-        near_ref[half + tokens : 2 * half + tokens] = jnp.where(me < n - 1, after, 0.0).astype(BF16)
+        near_ref[half + tokens : 2 * half + tokens] = behind_ref[...]
         near_ref[2 * half + tokens :] = jnp.zeros((window - tokens - 2 * half, local), BF16)
         finish(2)
         near = near_ref[...]
@@ -392,13 +383,12 @@
     context, value_sum, near = run(
         context_body,
         [((chosen, local), BF16), ((chosen, local), F32), ((window, local), BF16)],
-        (ids, reads, values, bands),
+        (reads, values, bands, before, behind),
         "context",
-        far=(2, 3),
-        late=(2, 3),
+        far=(1, 2),
+        late=(1, 2),
         far_out=(2,),
         early=(2,),
-        smem=1,
         us=2,
     )
     contexts = [context] + others(context)

time: 157 us -> 153 us (0.975)
  waiting for transfers between devices: 30.5 us -> 21.8 us
  starting transfers between devices: 40.7 us -> 47.4 us
    ppermute x28, waiting for transfers between devices: 14 us -> 7.85 us  [swap(): return lax.ppermute(array, 'tp', [(i, i ^ k) for i in range(tp)])]
    ppermute x0 -> x2, starting transfers between devices: none -> 5.83 us  [the longest x1 4.55 us: per_device(): lax.ppermute(edges[tokens - half:], 'seq', [(i, i + 1) for i in range(n -...]
    all_to_all x5, waiting for transfers between devices: 16.4 us -> 13.9 us  [exchange(): return lax.all_to_all(array, 'seq', 0, 0)]
    unnamed x46 -> x38, local copies, waits for them, and re-layouts: 3.68 us -> 2.4 us
  transfers between devices with their start and end apart: 35 -> 37, of which waited for: 10 -> 10; matrix products, arithmetic and copies ran while one was open for 0% -> 1% of each run, Pallas kernels for 39% -> 39%
where the time goes in v5:
time: 153 us; the launch traced here: 152 us
  Pallas kernels  65.4 us (43%)
  starting transfers between devices  47.4 us (31%)
  waiting for transfers between devices  21.8 us (14%)
  between operations  14.5 us (9%)
  local copies, waits for them, and re-layouts  3.13 us (2%)
    pallas_call x17, Pallas kernels, call(): pl.pallas_call(kernel, out_shape=[spaces[i](arrays[i].shape, arrays[i].dt...  65.4 us
    all_to_all x5, starting transfers between devices, exchange(): return lax.all_to_all(array, 'seq', 0, 0)  25.1 us
    ppermute x28, starting transfers between devices, swap(): return lax.ppermute(array, 'tp', [(i, i ^ k) for i in range(tp)])  16.5 us
    all_to_all x5, waiting for transfers between devices, exchange(): return lax.all_to_all(array, 'seq', 0, 0)  13.9 us
    ppermute x28, waiting for transfers between devices, swap(): return lax.ppermute(array, 'tp', [(i, i ^ k) for i in range(tp)])  7.85 us
    ppermute x1, starting transfers between devices, per_device(): lax.ppermute(edges[tokens - half:], 'seq', [(i, i + 1) for i in range(n -...  4.55 us
  transfers between devices with their start and end apart: 37, of which 10 were waited for; matrix products, arithmetic and copies ran while one was open for 1% of the time, Pallas kernels for 39%

profile of v5, /device:TPU:0, one launch (start us, length us, event | category | flops | bytes accessed | tf_op | source)
XLA Modules:
  0.0 152.3 jit_solution(11443840047283121437)
XLA Ops:
  7.2 1.9 %order.1.refs_8_ = bf16[8,64,128]{2,1,0:T(8,128)(2,1)} custom-call(s32[256]{0:T(256)} %refs_6_.2, s32[96,256]{1,0:T(8,128)} %bitcast.24), custom_call_target="tpu_custom_call" | custom-call | flops 2200000000 | tf_op jit(solution)/shard_map/order/pallas_call | solution.py:106
  9.1 7.3 %all-to-all-start = ((bf16[8,64,128]{2,1,0:T(8,128)(2,1)}), bf16[8,64,128]{2,1,0:T(8,128)(2,1)S(1)}, u32[]{:S(2)}, u32[]{:S(2)}) async-start(bf16[8,64,128]{2,1,0:T(8,128)(2,1)} %order.1.refs_8_), calls=%async_computation | async-start | bytes 262144 | tf_op jit(solution)/shard_map/all_to_all | solution.py:238
  16.5 6.3 %prepare.1 = (bf16[256,192]{1,0:T(8,128)(2,1)}, bf16[288,256]{1,0:T(8,128)(2,1)}, bf16[64,768]{1,0:T(8,128)(2,1)}, bf16[192,768]{1,0:T(8,128)(2,1)}, f32[64,768]...) custom-call(bf16[256,768]{1,0:T(8,128)(2,1)} %refs_0_.5, ...), custom_call_target="tpu_custom_call" | custom-call | flops 4400000000 | tf_op jit(solution)/shard_map/prepare/pallas_call | solution.py:106
  23.8 5.2 %count.1 = (bf16[3,512,256]{2,1,0:T(8,128)(2,1)}, bf16[8,64,192]{2,1,0:T(8,128)(2,1)}) custom-call(bf16[8,64,128]{2,1,0:T(8,128)(2,1)S(1)} %all-to-all-done.refs_0_.refs_4_, bf16[288,256]{1,0:T(8,128)(2,1)} %get-tuple-element.69.refs_1_, bf16[1024,256]{1,0:T(8,128)(2,1)S(1)} %copy-done.7, bf16[64,768]{1,0:T(8,128)(2,1)S(1)} %copy-done.8, ...), custom_call_target="tpu_custom_call" | custom-call | flops 5500000256 | tf_op jit(solution)/shard_map/count/pallas_call | solution.py:106
  29.0 5.0 %all-to-all-start.1 = ((bf16[8,64,192]{2,1,0:T(8,128)(2,1)}), bf16[8,64,192]{2,1,0:T(8,128)(2,1)S(1)}, u32[]{:S(2)}, u32[]{:S(2)}) async-start(bf16[8,64,192]{2,1,0:T(8,128)(2,1)} %get-tuple-element.71), calls=%async_computation.1 | async-start | bytes 524288 | tf_op jit(solution)/shard_map/all_to_all | solution.py:238
  34.1 1.6 %collective-permute-start.6 = (bf16[192,768]{1,0:T(8,128)(2,1)S(1)}, bf16[192,768]{1,0:T(8,128)(2,1)}, u32[]{:S(2)}, u32[]{:S(2)}) collective-permute-start(bf16[192,768]{1,0:T(8,128)(2,1)S(1)} %copy-done.4), channel_id=1, source_target_pairs={{0,2},{1,3},{2,0},{3,1},{4,6},{5,7},{6,4},{7,5},{8,10},{9,11},{10,... | collective-permute-start | bytes 884744 | tf_op jit(solution)/shard_map/ppermute | solution.py:228
  38.2 4.5 %collective-permute-start = (bf16[32,192]{1,0:T(8,128)(2,1)S(1)}, bf16[32,192]{1,0:T(8,128)(2,1)S(1)}, u32[]{:S(2)}, u32[]{:S(2)}) collective-permute-start(bf16[32,192]{1,0:T(8,128)(2,1)S(1)} %get-tuple-element.122), channel_id=1, source_target_pairs={{0,4},{4,8},{8,12},{12,16},{16,20},{20,24},{24,28},{1,5},{5,9},{9,... | collective-permute-start | bytes 36872 | tf_op jit(solution)/shard_map/ppermute | solution.py:356
  42.8 1.4 collective-permute-done.6.refs_6_
  44.2 2.3 %all-to-all-done.1.refs_0_ = bf16[8,64,192]{2,1,0:T(8,128)(2,1)S(1)} async-done(((bf16[8,64,192]{2,1,0:T(8,128)(2,1)}), bf16[8,64,192]{2,1,0:T(8,128)(2,1)S(1)}, u32[]{:S(2)}, u32[]{:S(2)}) %all-to-all-start.1) | async-done | bytes 196640 | tf_op jit(solution)/shard_map/all_to_all | solution.py:238
  46.5 1.9 %context.1 = (bf16[64,192]{1,0:T(8,128)(2,1)S(1)}, f32[64,192]{1,0:T(8,128)S(1)}, bf16[384,192]{1,0:T(8,128)(2,1)}) custom-call(bf16[8,64,192]{2,1,0:T(8,128)(2,1)S(1)} %all-to-all-done.1.refs_0_, bf16[256,192]{1,0:T(8,128)(2,1)} %get-tuple-element.73.refs_4_.refs_1_, bf16[3,64,768]{2,1,0:T(8,128)(2,1)} %get-tuple-element.72.refs_2_, ...), custom_call_target="tpu_custom_call" | custom-call | flops 2200000000 | tf_op jit(solution)/shard_map/context/pallas_call | solution.py:106
  48.5 1.5 %collective-permute-start.3 = (bf16[64,192]{1,0:T(8,128)(2,1)S(1)}, bf16[64,192]{1,0:T(8,128)(2,1)S(1)}, u32[]{:S(2)}, u32[]{:S(2)}) collective-permute-start(bf16[64,192]{1,0:T(8,128)(2,1)S(1)} %get-tuple-element.75.refs_0_.refs_15_.refs_13_), channel_id=1, source_target_pairs={{0,2},{1,3},{2,0},{3,1},{4,6},{5,7},{6,4},{7,5},{8,10},{9,11},{10,... | collective-permute-start | bytes 73736 | tf_op jit(solution)/shard_map/ppermute | solution.py:228
  52.6 2.9 %first.1 = (bf16[64,768]{1,0:T(8,128)(2,1)S(1)}, f32[64,768]{1,0:T(8,128)}, f32[64,768]{1,0:T(8,128)}, f32[64,768]{1,0:T(8,128)}) custom-call(bf16[64,192]{1,0:T(8,128)(2,1)S(1)} %get-tuple-element.75.refs_0_.refs_15_.refs_13_, bf16[64,192]{1,0:T(8,128)(2,1)S(1)} %collective-permute-done.2.refs_1_, bf16[64,192]{1,0:T(8,128)(2,1)S(1)} %collective-permute-done.3.refs_2_, ...), custom_call_target="tpu_custom_call" | custom-call | flops 3300000000 | tf_op jit(solution)/shard_map/first/pallas_call | solution.py:106
  58.6 1.7 %collective-permute-done.10.refs_4_ = bf16[64,768]{1,0:T(8,128)(2,1)S(1)} collective-permute-done((bf16[64,768]{1,0:T(8,128)(2,1)S(1)}, bf16[64,768]{1,0:T(8,128)(2,1)S(1)}, u32[]{:S(2)}, u32[]{:S(2)}) %collective-permute-start.10) | collective-permute-done | bytes 98336 | tf_op jit(solution)/shard_map/ppermute | solution.py:228
  60.3 2.5 %collective-permute-done.9.refs_3_ = bf16[64,768]{1,0:T(8,128)(2,1)S(1)} collective-permute-done((bf16[64,768]{1,0:T(8,128)(2,1)S(1)}, bf16[64,768]{1,0:T(8,128)(2,1)S(1)}, u32[]{:S(2)}, u32[]{:S(2)}) %collective-permute-start.9) | collective-permute-done | bytes 98336 | tf_op jit(solution)/shard_map/ppermute | solution.py:228
  62.8 3.4 %second.1 = (bf16[64,768]{1,0:T(8,128)(2,1)}, f32[64,768]{1,0:T(8,128)S(1)}, bf16[64,768]{1,0:T(8,128)(2,1)S(1)}, f32[8,768]{1,0:T(8,128)S(1)}, bf16[32,2048]{1,0:T(8,128)(2,1)}) custom-call(s32[2]{0:T(128)S(1)} %pad_add_fusion.refs_0_, bf16[64,768]{1,0:T(8,128)(2,1)S(1)} %get-tuple-element.77.refs_1_, bf16[64,768]{1,0:T(8,128)(2,1)S(1)} %collective-permute-done.8.refs_2_, ...), custom_call_target="tpu_custom_call" | custom-call | flops 3300000000 | tf_op jit(solution)/shard_map/second/pallas_call | solution.py:106
  66.2 1.3 collective-permute-start.16
  68.2 5.8 %rest_words.1 = (s32[192,128]{1,0:T(8,128)S(1)}, s32[32,2048]{1,0:T(8,128)S(1)}, f32[192,64]{1,0:T(8,128)S(1)}) custom-call(bf16[192,128]{1,0:T(8,128)(2,1)} %get-tuple-element.68.refs_0_, bf16[8,288,256]{2,1,0:T(8,128)(2,1)} %bitcast.19, bf16[1024,256]{1,0:T(8,128)(2,1)} %constant.13.clone.refs_2_, bf16[64,768]{1,0:T(8,128)(2,1)} %constant.14.clone.refs_3_, ...), custom_call_target="tpu_custom_call" | custom-call | flops 5500000256 | tf_op jit(solution)/shard_map/rest_words/pallas_call | solution.py:106
  74.1 3.4 %hidden.1 = (f32[64,768]{1,0:T(8,128)}, bf16[8,64,384]{2,1,0:T(8,128)(2,1)}, bf16[16,768]{1,0:T(8,128)(2,1)}, f32[8,768]{1,0:T(8,128)}) custom-call(s32[2]{0:T(128)S(1)} %pad_add_fusion.refs_0_, bf16[64,768]{1,0:T(8,128)(2,1)S(1)} %get-tuple-element.87.refs_1_, bf16[64,768]{1,0:T(8,128)(2,1)S(1)} %collective-permute-done.14.refs_2_, ...), custom_call_target="tpu_custom_call" | custom-call | flops 2200000000 | tf_op jit(solution)/shard_map/hidden/pallas_call | solution.py:106
  77.5 5.4 %all-to-all-start.2 = ((bf16[8,64,384]{2,1,0:T(8,128)(2,1)}), bf16[8,64,384]{2,1,0:T(8,128)(2,1)S(1)}, u32[]{:S(2)}, u32[]{:S(2)}) async-start(bf16[8,64,384]{2,1,0:T(8,128)(2,1)} %get-tuple-element.94), calls=%async_computation.2 | async-start | bytes 786432 | tf_op jit(solution)/shard_map/all_to_all | solution.py:238
  82.9 6.2 %rest_context.1.refs_5_.refs_0_ = bf16[192,192]{1,0:T(8,128)(2,1)S(1)} custom-call(s32[192,128]{1,0:T(8,128)S(1)} %get-tuple-element.82.refs_11_.refs_0_, s32[32,2048]{1,0:T(8,128)S(1)} %get-tuple-element.83.refs_1_, f32[192,64]{1,0:T(8,128)S(1)} %get-tuple-element.84.refs_2_, bf16[8,288,256]{2,1,0:T(8,128)(2,1)} %bitcast.21, ...), custom_call_target="tpu_custom_call" | custom-call | flops 6600000000 | tf_op jit(solution)/shard_map/rest_context/pallas_call | solution.py:106
  91.0 5.3 %all-to-all-done.2.refs_1_ = bf16[8,64,384]{2,1,0:T(8,128)(2,1)S(1)} async-done(((bf16[8,64,384]{2,1,0:T(8,128)(2,1)}), bf16[8,64,384]{2,1,0:T(8,128)(2,1)S(1)}, u32[]{:S(2)}, u32[]{:S(2)}) %all-to-all-start.2) | async-done | bytes 393248 | tf_op jit(solution)/shard_map/all_to_all | solution.py:238
  96.3 3.4 %values_back.1 = (bf16[256,192]{1,0:T(8,128)(2,1)S(1)}, bf16[384,192]{1,0:T(8,128)(2,1)S(1)}) custom-call(s32[2]{0:T(128)S(1)} %pad_add_fusion.refs_0_, bf16[8,64,384]{2,1,0:T(8,128)(2,1)S(1)} %all-to-all-done.2.refs_1_, bf16[3,512,256]{2,1,0:T(8,128)(2,1)} %get-tuple-element.74.refs_5_.refs_2_, bf16[3,256,768]{2,1,0:T(8,128)(2,1)} %get-tuple-element.95.refs_3_, ...), custom_call_target="tpu_custom_call" | custom-call | flops 4400000000 | tf_op jit(solution)/shard_map/values_back/pallas_call | solution.py:106
  102.3 2.6 %value_grad.1.refs_15_ = bf16[8,48,768]{2,1,0:T(8,128)(2,1)} custom-call(bf16[256,768]{1,0:T(8,128)(2,1)} %refs_0_.5, bf16[256,192]{1,0:T(8,128)(2,1)S(1)} %get-tuple-element.96.refs_1_.refs_6_.refs_0_, bf16[384,192]{1,0:T(8,128)(2,1)S(1)} %get-tuple-element.97.refs_2_, bf16[384,192]{1,0:T(8,128)(2,1)} %get-tuple-element.86.refs_5_.refs_3_, ...), custom_call_target="tpu_custom_call" | custom-call | flops 2750000128 | tf_op jit(solution)/shard_map/value_grad/pallas_call | solution.py:106
  104.9 3.8 %all-to-all-start.3 = ((bf16[8,48,768]{2,1,0:T(8,128)(2,1)}), bf16[8,48,768]{2,1,0:T(8,128)(2,1)S(1)}, u32[]{:S(2)}, u32[]{:S(2)}) async-start(bf16[8,48,768]{2,1,0:T(8,128)(2,1)} %value_grad.1.refs_15_), calls=%async_computation.3 | async-start | bytes 1179648 | tf_op jit(solution)/shard_map/all_to_all | solution.py:238
  109.4 4.6 %rest_first.1 = (bf16[192,768]{1,0:T(8,128)(2,1)S(1)}, f32[192,768]{1,0:T(8,128)}) custom-call(bf16[192,192]{1,0:T(8,128)(2,1)} %copy-done.6, bf16[192,192]{1,0:T(8,128)(2,1)} %copy-done.18, bf16[192,192]{1,0:T(8,128)(2,1)} %copy-done.17, bf16[192,192]{1,0:T(8,128)(2,1)} %copy-done.16, bf16[192,768]{1,0:T(8,128)(2,1)} %refs_4_.4, ...), custom_call_target="tpu_custom_call" | custom-call | flops 4400000000 | tf_op jit(solution)/shard_map/rest_first/pallas_call | solution.py:106
  114.2 1.6 %collective-permute-start.25 = (bf16[192,768]{1,0:T(8,128)(2,1)S(1)}, bf16[192,768]{1,0:T(8,128)(2,1)S(1)}, u32[]{:S(2)}, u32[]{:S(2)}) collective-permute-start(bf16[192,768]{1,0:T(8,128)(2,1)S(1)} %get-tuple-element.100.refs_10_.refs_1_), channel_id=1, source_target_pairs={{0,3},{1,2},{2,1},{3,0},{4,7},{5,6},{6,5},{7,4},{8,11},{9,10},{10,... | collective-permute-start | bytes 884744 | tf_op jit(solution)/shard_map/ppermute | solution.py:228
  116.3 3.5 %input_grad.1.refs_1_ = f32[256,768]{1,0:T(8,128)} custom-call(bf16[256,192]{1,0:T(8,128)(2,1)} %copy-done, bf16[256,192]{1,0:T(8,128)(2,1)} %copy-done.14, bf16[256,192]{1,0:T(8,128)(2,1)} %copy-done.13, bf16[256,192]{1,0:T(8,128)(2,1)} %copy-done.12, bf16[192,768]{1,0:T(8,128)(2,1)} %bitcast.16, bf16[192,768]{1,0:T(8,128)(2,1)} %copy-done.10, ...), custom_call_target="tpu_custom_call" | custom-call | flops 55000000 | tf_op jit(solution)/shard_map/input_grad/pallas_call | solution.py:106
  119.8 5.3 %all-to-all-done.3.refs_0_ = bf16[8,48,768]{2,1,0:T(8,128)(2,1)S(1)} async-done(((bf16[8,48,768]{2,1,0:T(8,128)(2,1)}), bf16[8,48,768]{2,1,0:T(8,128)(2,1)S(1)}, u32[]{:S(2)}, u32[]{:S(2)}) %all-to-all-start.3) | async-done | bytes 589856 | tf_op jit(solution)/shard_map/all_to_all | solution.py:238
  125.1 1.4 value_sums.1
  126.5 3.6 %all-to-all-start.4 = ((bf16[8,24,768]{2,1,0:T(8,128)(2,1)}), bf16[8,24,768]{2,1,0:T(8,128)(2,1)S(1)}, u32[]{:S(2)}, u32[]{:S(2)}) async-start(bf16[8,24,768]{2,1,0:T(8,128)(2,1)} %get-tuple-element.103.refs_5_), calls=%async_computation.4 | async-start | bytes 589824 | tf_op jit(solution)/shard_map/all_to_all | solution.py:238
  133.0 7.9 %weights.1 = (f32[768,768]{1,0:T(8,128)}, f32[768]{0:T(1024)}, f32[768,768]{1,0:T(8,128)}) custom-call(bf16[8,32,2048]{2,1,0:T(8,128)(2,1)} %bitcast.13, bf16[8,32,2048]{2,1,0:T(8,128)(2,1)} %copy-done.15, bf16[768,768]{1,0:T(8,128)(2,1)} %refs_2_.5, f32[768]{0:T(1024)} %refs_3_.3, bf16[768,768]{1,0:T(8,128)(2,1)} %refs_4_.5, ...), custom_call_target="tpu_custom_call" | custom-call | flops 3300000000 | tf_op jit(solution)/shard_map/weights/pallas_call | solution.py:106
  141.5 3.9 %last.1 = (bf16[256,768]{1,0:T(8,128)(2,1)}, f32[192,768]{1,0:T(8,128)}, f32[192,768]{1,0:T(8,128)}) custom-call(s32[2]{0:T(128)S(1)} %pad_add_fusion.refs_0_, bf16[192,768]{1,0:T(8,128)(2,1)S(1)} %get-tuple-element.100.refs_10_.refs_1_, bf16[192,768]{1,0:T(8,128)(2,1)S(1)} %collective-permute-done.23.refs_6_.refs_2_, ...), custom_call_target="tpu_custom_call" | custom-call | flops 55000000 | tf_op jit(solution)/shard_map/last/pallas_call | solution.py:106
  (101 shorter events, 19.4 us)
Async XLA Ops:
  9.1 14.6 %all-to-all-start = ((bf16[8,64,128]{2,1,0:T(8,128)(2,1)}), bf16[8,64,128]{2,1,0:T(8,128)(2,1)S(1)}, u32[]{:S(2)}, u32[]{:S(2)}) async-start(bf16[8,64,128]{2,1,0:T(8,128)(2,1)} %order.1.refs_8_), calls=%async_computation | async-start | bytes 262144 | tf_op jit(solution)/shard_map/all_to_all | solution.py:238
  16.4 51.8 %all-gather.5.cloned.1.call-start = ((), (), s32[]{:S(2)}) async-start(), calls=%async_computation.5 | async-start | bytes 1327104 | tf_op jit(solution)/shard_map/all_gather | solution.py:328
  29.0 17.5 %all-to-all-start.1 = ((bf16[8,64,192]{2,1,0:T(8,128)(2,1)}), bf16[8,64,192]{2,1,0:T(8,128)(2,1)S(1)}, u32[]{:S(2)}, u32[]{:S(2)}) async-start(bf16[8,64,192]{2,1,0:T(8,128)(2,1)} %get-tuple-element.71), calls=%async_computation.1 | async-start | bytes 524288 | tf_op jit(solution)/shard_map/all_to_all | solution.py:238
  34.0 80.0 %all-gather.7.cloned.1.call-start = ((), (), s32[]{:S(2)}) async-start(), calls=%async_computation.6 | async-start | bytes 1179648 | tf_op jit(solution)/shard_map/all_gather | solution.py:500
  34.1 10.1 %collective-permute-start.6 = (bf16[192,768]{1,0:T(8,128)(2,1)S(1)}, bf16[192,768]{1,0:T(8,128)(2,1)}, u32[]{:S(2)}, u32[]{:S(2)}) collective-permute-start(bf16[192,768]{1,0:T(8,128)(2,1)S(1)} %copy-done.4), channel_id=1, source_target_pairs={{0,2},{1,3},{2,0},{3,1},{4,6},{5,7},{6,4},{7,5},{8,10},{9,11},{10,... | collective-permute-start | bytes 884744 | tf_op jit(solution)/shard_map/ppermute | solution.py:228
  35.7 14.4 %collective-permute-start.12 = (bf16[192,768]{1,0:T(8,128)(2,1)S(1)}, bf16[192,768]{1,0:T(8,128)(2,1)}, u32[]{:S(2)}, u32[]{:S(2)}) collective-permute-start(bf16[192,768]{1,0:T(8,128)(2,1)S(1)} %bitcast.17), channel_id=1, source_target_pairs={{0,2},{1,3},{2,0},{3,1},{4,6},{5,7},{6,4},{7,5},{8,10},{9,11},{10,... | collective-permute-start | bytes 884744 | tf_op jit(solution)/shard_map/ppermute | solution.py:228
  36.9 7.3 %collective-permute-start.1 = (bf16[32,192]{1,0:T(8,128)(2,1)S(1)}, bf16[32,192]{1,0:T(8,128)(2,1)S(1)}, u32[]{:S(2)}, u32[]{:S(2)}) collective-permute-start(bf16[32,192]{1,0:T(8,128)(2,1)S(1)} %get-tuple-element.121), channel_id=1, source_target_pairs={{4,0},{8,4},{12,8},{16,12},{20,16},{24,20},{28,24},{5,1},{9,5},{13... | collective-permute-start | bytes 36872 | tf_op jit(solution)/shard_map/ppermute | solution.py:357
  38.2 6.0 %collective-permute-start = (bf16[32,192]{1,0:T(8,128)(2,1)S(1)}, bf16[32,192]{1,0:T(8,128)(2,1)S(1)}, u32[]{:S(2)}, u32[]{:S(2)}) collective-permute-start(bf16[32,192]{1,0:T(8,128)(2,1)S(1)} %get-tuple-element.122), channel_id=1, source_target_pairs={{0,4},{4,8},{8,12},{12,16},{16,20},{20,24},{24,28},{1,5},{5,9},{9,... | collective-permute-start | bytes 36872 | tf_op jit(solution)/shard_map/ppermute | solution.py:356
  42.7 7.7 %collective-permute-start.5 = (bf16[192,768]{1,0:T(8,128)(2,1)S(1)}, bf16[192,768]{1,0:T(8,128)(2,1)}, u32[]{:S(2)}, u32[]{:S(2)}) collective-permute-start(bf16[192,768]{1,0:T(8,128)(2,1)S(1)} %copy-done.4), channel_id=1, source_target_pairs={{0,1},{1,0},{2,3},{3,2},{4,5},{5,4},{6,7},{7,6},{8,9},{9,8},{10,11... | collective-permute-start | bytes 884744 | tf_op jit(solution)/shard_map/ppermute | solution.py:228
  44.2 6.5 %collective-permute-start.7 = (bf16[192,768]{1,0:T(8,128)(2,1)}, bf16[192,768]{1,0:T(8,128)(2,1)}, u32[]{:S(2)}, u32[]{:S(2)}) collective-permute-start(bf16[192,768]{1,0:T(8,128)(2,1)} %collective-permute-done.6.refs_6_), channel_id=1, source_target_pairs={{0,1},{1,0},{2,3},{3,2},{4,5},{5,4},{6,7},{7,6},{8,9},{9,8},{10,11... | collective-permute-start | bytes 884744 | tf_op jit(solution)/shard_map/ppermute | solution.py:228
  50.5 8.1 %collective-permute-start.11 = (bf16[192,768]{1,0:T(8,128)(2,1)S(1)}, bf16[192,768]{1,0:T(8,128)(2,1)S(1)}, u32[]{:S(2)}, u32[]{:S(2)}) collective-permute-start(bf16[192,768]{1,0:T(8,128)(2,1)S(1)} %bitcast.18), channel_id=1, source_target_pairs={{0,1},{1,0},{2,3},{3,2},{4,5},{5,4},{6,7},{7,6},{8,9},{9,8},{10,11... | collective-permute-start | bytes 884744 | tf_op jit(solution)/shard_map/ppermute | solution.py:228
  50.7 7.9 %collective-permute-start.13 = (bf16[192,768]{1,0:T(8,128)(2,1)}, bf16[192,768]{1,0:T(8,128)(2,1)S(1)}, u32[]{:S(2)}, u32[]{:S(2)}) collective-permute-start(bf16[192,768]{1,0:T(8,128)(2,1)} %collective-permute-done.12.refs_16_.refs_6_), channel_id=1, source_target_pairs={{0,1},{1,0},{2,3},{3,2},{4,5},{5,4},{6,7},{7,6},{8,9},{9,8},{10,11... | collective-permute-start | bytes 884744 | tf_op jit(solution)/shard_map/ppermute | solution.py:228
  56.5 6.3 %collective-permute-start.9 = (bf16[64,768]{1,0:T(8,128)(2,1)S(1)}, bf16[64,768]{1,0:T(8,128)(2,1)S(1)}, u32[]{:S(2)}, u32[]{:S(2)}) collective-permute-start(bf16[64,768]{1,0:T(8,128)(2,1)S(1)} %get-tuple-element.77.refs_1_), channel_id=1, source_target_pairs={{0,2},{1,3},{2,0},{3,1},{4,6},{5,7},{6,4},{7,5},{8,10},{9,11},{10,... | collective-permute-start | bytes 294920 | tf_op jit(solution)/shard_map/ppermute | solution.py:228
  66.2 7.8 %collective-permute-start.16 = (bf16[64,768]{1,0:T(8,128)(2,1)S(1)}, bf16[64,768]{1,0:T(8,128)(2,1)S(1)}, u32[]{:S(2)}, u32[]{:S(2)}) collective-permute-start(bf16[64,768]{1,0:T(8,128)(2,1)S(1)} %get-tuple-element.87.refs_1_), channel_id=1, source_target_pairs={{0,3},{1,2},{2,1},{3,0},{4,7},{5,6},{6,5},{7,4},{8,11},{9,10},{10,... | collective-permute-start | bytes 294920 | tf_op jit(solution)/shard_map/ppermute | solution.py:228
  67.5 6.5 %collective-permute-start.15 = (bf16[64,768]{1,0:T(8,128)(2,1)S(1)}, bf16[64,768]{1,0:T(8,128)(2,1)S(1)}, u32[]{:S(2)}, u32[]{:S(2)}) collective-permute-start(bf16[64,768]{1,0:T(8,128)(2,1)S(1)} %get-tuple-element.87.refs_1_), channel_id=1, source_target_pairs={{0,2},{1,3},{2,0},{3,1},{4,6},{5,7},{6,4},{7,5},{8,10},{9,11},{10,... | collective-permute-start | bytes 294920 | tf_op jit(solution)/shard_map/ppermute | solution.py:228
  67.8 6.2 %collective-permute-start.14 = (bf16[64,768]{1,0:T(8,128)(2,1)S(1)}, bf16[64,768]{1,0:T(8,128)(2,1)S(1)}, u32[]{:S(2)}, u32[]{:S(2)}) collective-permute-start(bf16[64,768]{1,0:T(8,128)(2,1)S(1)} %get-tuple-element.87.refs_1_), channel_id=1, source_target_pairs={{0,1},{1,0},{2,3},{3,2},{4,5},{5,4},{6,7},{7,6},{8,9},{9,8},{10,11... | collective-permute-start | bytes 294920 | tf_op jit(solution)/shard_map/ppermute | solution.py:228
  77.5 18.8 %all-to-all-start.2 = ((bf16[8,64,384]{2,1,0:T(8,128)(2,1)}), bf16[8,64,384]{2,1,0:T(8,128)(2,1)S(1)}, u32[]{:S(2)}, u32[]{:S(2)}) async-start(bf16[8,64,384]{2,1,0:T(8,128)(2,1)} %get-tuple-element.94), calls=%async_computation.2 | async-start | bytes 786432 | tf_op jit(solution)/shard_map/all_to_all | solution.py:238
  89.1 12.2 %collective-permute-start.19 = (bf16[192,192]{1,0:T(8,128)(2,1)S(1)}, bf16[192,192]{1,0:T(8,128)(2,1)S(1)}, u32[]{:S(2)}, u32[]{:S(2)}) collective-permute-start(bf16[192,192]{1,0:T(8,128)(2,1)S(1)} %rest_context.1.refs_5_.refs_0_), channel_id=1, source_target_pairs={{0,3},{1,2},{2,1},{3,0},{4,7},{5,6},{6,5},{7,4},{8,11},{9,10},{10,... | collective-permute-start | bytes 221192 | tf_op jit(solution)/shard_map/ppermute | solution.py:228
  90.4 11.3 %collective-permute-start.18 = (bf16[192,192]{1,0:T(8,128)(2,1)S(1)}, bf16[192,192]{1,0:T(8,128)(2,1)S(1)}, u32[]{:S(2)}, u32[]{:S(2)}) collective-permute-start(bf16[192,192]{1,0:T(8,128)(2,1)S(1)} %rest_context.1.refs_5_.refs_0_), channel_id=1, source_target_pairs={{0,2},{1,3},{2,0},{3,1},{4,6},{5,7},{6,4},{7,5},{8,10},{9,11},{10,... | collective-permute-start | bytes 221192 | tf_op jit(solution)/shard_map/ppermute | solution.py:228
  90.9 10.8 %collective-permute-start.17 = (bf16[192,192]{1,0:T(8,128)(2,1)S(1)}, bf16[192,192]{1,0:T(8,128)(2,1)S(1)}, u32[]{:S(2)}, u32[]{:S(2)}) collective-permute-start(bf16[192,192]{1,0:T(8,128)(2,1)S(1)} %rest_context.1.refs_5_.refs_0_), channel_id=1, source_target_pairs={{0,1},{1,0},{2,3},{3,2},{4,5},{5,4},{6,7},{7,6},{8,9},{9,8},{10,11... | collective-permute-start | bytes 221192 | tf_op jit(solution)/shard_map/ppermute | solution.py:228
  99.7 9.0 %collective-permute-start.22 = (bf16[256,192]{1,0:T(8,128)(2,1)S(1)}, bf16[256,192]{1,0:T(8,128)(2,1)S(1)}, u32[]{:S(2)}, u32[]{:S(2)}) collective-permute-start(bf16[256,192]{1,0:T(8,128)(2,1)S(1)} %get-tuple-element.96.refs_1_.refs_6_.refs_0_), channel_id=1, source_target_pairs={{0,3},{1,2},{2,1},{3,0},{4,7},{5,6},{6,5},{7,4},{8,11},{9,10},{10,... | collective-permute-start | bytes 294920 | tf_op jit(solution)/shard_map/ppermute | solution.py:228
  100.0 8.7 %collective-permute-start.21 = (bf16[256,192]{1,0:T(8,128)(2,1)S(1)}, bf16[256,192]{1,0:T(8,128)(2,1)S(1)}, u32[]{:S(2)}, u32[]{:S(2)}) collective-permute-start(bf16[256,192]{1,0:T(8,128)(2,1)S(1)} %get-tuple-element.96.refs_1_.refs_6_.refs_0_), channel_id=1, source_target_pairs={{0,2},{1,3},{2,0},{3,1},{4,6},{5,7},{6,4},{7,5},{8,10},{9,11},{10,... | collective-permute-start | bytes 294920 | tf_op jit(solution)/shard_map/ppermute | solution.py:228
  101.3 7.4 %collective-permute-start.20 = (bf16[256,192]{1,0:T(8,128)(2,1)S(1)}, bf16[256,192]{1,0:T(8,128)(2,1)S(1)}, u32[]{:S(2)}, u32[]{:S(2)}) collective-permute-start(bf16[256,192]{1,0:T(8,128)(2,1)S(1)} %get-tuple-element.96.refs_1_.refs_6_.refs_0_), channel_id=1, source_target_pairs={{0,1},{1,0},{2,3},{3,2},{4,5},{5,4},{6,7},{7,6},{8,9},{9,8},{10,11... | collective-permute-start | bytes 294920 | tf_op jit(solution)/shard_map/ppermute | solution.py:228
  104.9 20.2 %all-to-all-start.3 = ((bf16[8,48,768]{2,1,0:T(8,128)(2,1)}), bf16[8,48,768]{2,1,0:T(8,128)(2,1)S(1)}, u32[]{:S(2)}, u32[]{:S(2)}) async-start(bf16[8,48,768]{2,1,0:T(8,128)(2,1)} %value_grad.1.refs_15_), calls=%async_computation.3 | async-start | bytes 1179648 | tf_op jit(solution)/shard_map/all_to_all | solution.py:238
  114.1 17.9 %collective-permute-start.29 = (bf16[8,32,2048]{2,1,0:T(8,128)(2,1)}, bf16[8,32,2048]{2,1,0:T(8,128)(2,1)S(1)}, u32[]{:S(2)}, u32[]{:S(2)}) collective-permute-start(bf16[8,32,2048]{2,1,0:T(8,128)(2,1)} %bitcast.12), channel_id=1, source_target_pairs={{0,1},{1,0},{2,3},{3,2},{4,5},{5,4},{6,7},{7,6},{8,9},{9,8},{10,11... | collective-permute-start | bytes 3145736 | tf_op jit(solution)/shard_map/ppermute | solution.py:228
  114.2 16.8 %collective-permute-start.25 = (bf16[192,768]{1,0:T(8,128)(2,1)S(1)}, bf16[192,768]{1,0:T(8,128)(2,1)S(1)}, u32[]{:S(2)}, u32[]{:S(2)}) collective-permute-start(bf16[192,768]{1,0:T(8,128)(2,1)S(1)} %get-tuple-element.100.refs_10_.refs_1_), channel_id=1, source_target_pairs={{0,3},{1,2},{2,1},{3,0},{4,7},{5,6},{6,5},{7,4},{8,11},{9,10},{10,... | collective-permute-start | bytes 884744 | tf_op jit(solution)/shard_map/ppermute | solution.py:228
  115.8 16.0 %collective-permute-start.24 = (bf16[192,768]{1,0:T(8,128)(2,1)S(1)}, bf16[192,768]{1,0:T(8,128)(2,1)S(1)}, u32[]{:S(2)}, u32[]{:S(2)}) collective-permute-start(bf16[192,768]{1,0:T(8,128)(2,1)S(1)} %get-tuple-element.100.refs_10_.refs_1_), channel_id=1, source_target_pairs={{0,2},{1,3},{2,0},{3,1},{4,6},{5,7},{6,4},{7,5},{8,10},{9,11},{10,... | collective-permute-start | bytes 884744 | tf_op jit(solution)/shard_map/ppermute | solution.py:228
  116.3 15.7 %collective-permute-start.23 = (bf16[192,768]{1,0:T(8,128)(2,1)S(1)}, bf16[192,768]{1,0:T(8,128)(2,1)S(1)}, u32[]{:S(2)}, u32[]{:S(2)}) collective-permute-start(bf16[192,768]{1,0:T(8,128)(2,1)S(1)} %get-tuple-element.100.refs_10_.refs_1_), channel_id=1, source_target_pairs={{0,1},{1,0},{2,3},{3,2},{4,5},{5,4},{6,7},{7,6},{8,9},{9,8},{10,11... | collective-permute-start | bytes 884744 | tf_op jit(solution)/shard_map/ppermute | solution.py:228
  126.5 15.1 %all-to-all-start.4 = ((bf16[8,24,768]{2,1,0:T(8,128)(2,1)}), bf16[8,24,768]{2,1,0:T(8,128)(2,1)S(1)}, u32[]{:S(2)}, u32[]{:S(2)}) async-start(bf16[8,24,768]{2,1,0:T(8,128)(2,1)} %get-tuple-element.103.refs_5_), calls=%async_computation.4 | async-start | bytes 589824 | tf_op jit(solution)/shard_map/all_to_all | solution.py:238
  130.1 10.7 %collective-permute-start.28 = (bf16[8,16,768]{2,1,0:T(8,128)(2,1)S(1)}, bf16[8,16,768]{2,1,0:T(8,128)(2,1)S(1)}, u32[]{:S(2)}, u32[]{:S(2)}) collective-permute-start(bf16[8,16,768]{2,1,0:T(8,128)(2,1)S(1)} %get-tuple-element.102.refs_5_), channel_id=1, source_target_pairs={{0,3},{1,2},{2,1},{3,0},{4,7},{5,6},{6,5},{7,4},{8,11},{9,10},{10,... | collective-permute-start | bytes 589832 | tf_op jit(solution)/shard_map/ppermute | solution.py:228
  131.0 10.5 %collective-permute-start.27 = (bf16[8,16,768]{2,1,0:T(8,128)(2,1)S(1)}, bf16[8,16,768]{2,1,0:T(8,128)(2,1)S(1)}, u32[]{:S(2)}, u32[]{:S(2)}) collective-permute-start(bf16[8,16,768]{2,1,0:T(8,128)(2,1)S(1)} %get-tuple-element.102.refs_5_), channel_id=1, source_target_pairs={{0,2},{1,3},{2,0},{3,1},{4,6},{5,7},{6,4},{7,5},{8,10},{9,11},{10,... | collective-permute-start | bytes 589832 | tf_op jit(solution)/shard_map/ppermute | solution.py:228
  131.7 9.8 %collective-permute-start.26 = (bf16[8,16,768]{2,1,0:T(8,128)(2,1)S(1)}, bf16[8,16,768]{2,1,0:T(8,128)(2,1)S(1)}, u32[]{:S(2)}, u32[]{:S(2)}) collective-permute-start(bf16[8,16,768]{2,1,0:T(8,128)(2,1)S(1)} %get-tuple-element.102.refs_5_), channel_id=1, source_target_pairs={{0,1},{1,0},{2,3},{3,2},{4,5},{5,4},{6,7},{7,6},{8,9},{9,8},{10,11... | collective-permute-start | bytes 589832 | tf_op jit(solution)/shard_map/ppermute | solution.py:228
  (24 other events, 109.4 us)
Sparse Core Ops, SparseCore 0:
  22.9 44.2 all-gather.4
  69.3 41.7 all-gather.6

commit v6 on v5

--- a/solution.py
+++ b/solution.py
@@ -664,7 +664,6 @@
         ((n, piece_rows + extra + part_rows, width), BF16),
         (inputs, grad_values, dense, near, sums, share),
         "value_grad",
-        also=tuple((array, pltpu.HBM) for array in rest_contexts[1:]),
         far=(0, 3, 4, 5),
         scratch=[pltpu.VMEM((extra, width), F32)],
         us=2.5,

time: 153 us -> 153 us (level)
  transfers between devices with their start and end apart: 37 -> 37, of which waited for: 10 -> 11; matrix products, arithmetic and copies ran while one was open for 1% -> 1% of each run, Pallas kernels for 39% -> 39%
where the time goes in v6:
time: 153 us; the launch traced here: 152 us
  Pallas kernels  65.4 us (43%)
  starting transfers between devices  47.4 us (31%)
  waiting for transfers between devices  21.8 us (14%)
  between operations  14.5 us (9%)
  local copies, waits for them, and re-layouts  2.48 us (2%)
    pallas_call x17, Pallas kernels, call(): pl.pallas_call(kernel, out_shape=[spaces[i](arrays[i].shape, arrays[i].dt...  65.4 us
    all_to_all x5, starting transfers between devices, exchange(): return lax.all_to_all(array, 'seq', 0, 0)  25.1 us
    ppermute x28, starting transfers between devices, swap(): return lax.ppermute(array, 'tp', [(i, i ^ k) for i in range(tp)])  16.5 us
    all_to_all x5, waiting for transfers between devices, exchange(): return lax.all_to_all(array, 'seq', 0, 0)  13.6 us
    ppermute x28, waiting for transfers between devices, swap(): return lax.ppermute(array, 'tp', [(i, i ^ k) for i in range(tp)])  8.15 us
    ppermute x1, starting transfers between devices, per_device(): lax.ppermute(edges[tokens - half:], 'seq', [(i, i + 1) for i in range(n -...  4.55 us
  transfers between devices with their start and end apart: 37, of which 11 were waited for; matrix products, arithmetic and copies ran while one was open for 1% of the time, Pallas kernels for 39%

profile of v6, /device:TPU:0, one launch (start us, length us, event | category | flops | bytes accessed | tf_op | source)
XLA Modules:
  0.0 151.7 jit_solution(17125991002851607416)
XLA Ops:
  7.2 1.9 %order.1.refs_8_ = bf16[8,64,128]{2,1,0:T(8,128)(2,1)} custom-call(s32[256]{0:T(256)} %refs_6_.2, s32[96,256]{1,0:T(8,128)} %bitcast.24), custom_call_target="tpu_custom_call" | custom-call | flops 2200000000 | tf_op jit(solution)/shard_map/order/pallas_call | solution.py:106
  9.1 7.3 %all-to-all-start = ((bf16[8,64,128]{2,1,0:T(8,128)(2,1)}), bf16[8,64,128]{2,1,0:T(8,128)(2,1)S(1)}, u32[]{:S(2)}, u32[]{:S(2)}) async-start(bf16[8,64,128]{2,1,0:T(8,128)(2,1)} %order.1.refs_8_), calls=%async_computation | async-start | bytes 262144 | tf_op jit(solution)/shard_map/all_to_all | solution.py:238
  16.5 6.3 %prepare.1 = (bf16[256,192]{1,0:T(8,128)(2,1)}, bf16[288,256]{1,0:T(8,128)(2,1)}, bf16[64,768]{1,0:T(8,128)(2,1)}, bf16[192,768]{1,0:T(8,128)(2,1)}, f32[64,768]...) custom-call(bf16[256,768]{1,0:T(8,128)(2,1)} %refs_0_.5, ...), custom_call_target="tpu_custom_call" | custom-call | flops 4400000000 | tf_op jit(solution)/shard_map/prepare/pallas_call | solution.py:106
  23.8 5.2 %count.1 = (bf16[3,512,256]{2,1,0:T(8,128)(2,1)}, bf16[8,64,192]{2,1,0:T(8,128)(2,1)}) custom-call(bf16[8,64,128]{2,1,0:T(8,128)(2,1)S(1)} %all-to-all-done.refs_0_.refs_4_, bf16[288,256]{1,0:T(8,128)(2,1)} %get-tuple-element.69.refs_1_, bf16[1024,256]{1,0:T(8,128)(2,1)S(1)} %copy-done.7, bf16[64,768]{1,0:T(8,128)(2,1)S(1)} %copy-done.8, ...), custom_call_target="tpu_custom_call" | custom-call | flops 5500000256 | tf_op jit(solution)/shard_map/count/pallas_call | solution.py:106
  29.0 5.0 %all-to-all-start.1 = ((bf16[8,64,192]{2,1,0:T(8,128)(2,1)}), bf16[8,64,192]{2,1,0:T(8,128)(2,1)S(1)}, u32[]{:S(2)}, u32[]{:S(2)}) async-start(bf16[8,64,192]{2,1,0:T(8,128)(2,1)} %get-tuple-element.71), calls=%async_computation.1 | async-start | bytes 524288 | tf_op jit(solution)/shard_map/all_to_all | solution.py:238
  34.1 1.6 %collective-permute-start.6 = (bf16[192,768]{1,0:T(8,128)(2,1)S(1)}, bf16[192,768]{1,0:T(8,128)(2,1)}, u32[]{:S(2)}, u32[]{:S(2)}) collective-permute-start(bf16[192,768]{1,0:T(8,128)(2,1)S(1)} %copy-done.4), channel_id=1, source_target_pairs={{0,2},{1,3},{2,0},{3,1},{4,6},{5,7},{6,4},{7,5},{8,10},{9,11},{10,... | collective-permute-start | bytes 884744 | tf_op jit(solution)/shard_map/ppermute | solution.py:228
  38.2 4.5 %collective-permute-start = (bf16[32,192]{1,0:T(8,128)(2,1)S(1)}, bf16[32,192]{1,0:T(8,128)(2,1)S(1)}, u32[]{:S(2)}, u32[]{:S(2)}) collective-permute-start(bf16[32,192]{1,0:T(8,128)(2,1)S(1)} %get-tuple-element.122), channel_id=1, source_target_pairs={{0,4},{4,8},{8,12},{12,16},{16,20},{20,24},{24,28},{1,5},{5,9},{9,... | collective-permute-start | bytes 36872 | tf_op jit(solution)/shard_map/ppermute | solution.py:356
  42.8 1.4 collective-permute-done.6.refs_6_
  44.2 2.3 %all-to-all-done.1.refs_0_ = bf16[8,64,192]{2,1,0:T(8,128)(2,1)S(1)} async-done(((bf16[8,64,192]{2,1,0:T(8,128)(2,1)}), bf16[8,64,192]{2,1,0:T(8,128)(2,1)S(1)}, u32[]{:S(2)}, u32[]{:S(2)}) %all-to-all-start.1) | async-done | bytes 196640 | tf_op jit(solution)/shard_map/all_to_all | solution.py:238
  46.5 1.9 %context.1 = (bf16[64,192]{1,0:T(8,128)(2,1)S(1)}, f32[64,192]{1,0:T(8,128)S(1)}, bf16[384,192]{1,0:T(8,128)(2,1)}) custom-call(bf16[8,64,192]{2,1,0:T(8,128)(2,1)S(1)} %all-to-all-done.1.refs_0_, bf16[256,192]{1,0:T(8,128)(2,1)} %get-tuple-element.73.refs_4_.refs_1_, bf16[3,64,768]{2,1,0:T(8,128)(2,1)} %get-tuple-element.72.refs_2_, ...), custom_call_target="tpu_custom_call" | custom-call | flops 2200000000 | tf_op jit(solution)/shard_map/context/pallas_call | solution.py:106
  48.5 1.5 %collective-permute-start.3 = (bf16[64,192]{1,0:T(8,128)(2,1)S(1)}, bf16[64,192]{1,0:T(8,128)(2,1)S(1)}, u32[]{:S(2)}, u32[]{:S(2)}) collective-permute-start(bf16[64,192]{1,0:T(8,128)(2,1)S(1)} %get-tuple-element.75.refs_0_.refs_15_.refs_13_), channel_id=1, source_target_pairs={{0,2},{1,3},{2,0},{3,1},{4,6},{5,7},{6,4},{7,5},{8,10},{9,11},{10,... | collective-permute-start | bytes 73736 | tf_op jit(solution)/shard_map/ppermute | solution.py:228
  52.6 2.9 %first.1 = (bf16[64,768]{1,0:T(8,128)(2,1)S(1)}, f32[64,768]{1,0:T(8,128)}, f32[64,768]{1,0:T(8,128)}, f32[64,768]{1,0:T(8,128)}) custom-call(bf16[64,192]{1,0:T(8,128)(2,1)S(1)} %get-tuple-element.75.refs_0_.refs_15_.refs_13_, bf16[64,192]{1,0:T(8,128)(2,1)S(1)} %collective-permute-done.2.refs_1_, bf16[64,192]{1,0:T(8,128)(2,1)S(1)} %collective-permute-done.3.refs_2_, ...), custom_call_target="tpu_custom_call" | custom-call | flops 3300000000 | tf_op jit(solution)/shard_map/first/pallas_call | solution.py:106
  58.6 1.7 %collective-permute-done.10.refs_4_ = bf16[64,768]{1,0:T(8,128)(2,1)S(1)} collective-permute-done((bf16[64,768]{1,0:T(8,128)(2,1)S(1)}, bf16[64,768]{1,0:T(8,128)(2,1)S(1)}, u32[]{:S(2)}, u32[]{:S(2)}) %collective-permute-start.10) | collective-permute-done | bytes 98336 | tf_op jit(solution)/shard_map/ppermute | solution.py:228
  60.3 2.5 %collective-permute-done.9.refs_3_ = bf16[64,768]{1,0:T(8,128)(2,1)S(1)} collective-permute-done((bf16[64,768]{1,0:T(8,128)(2,1)S(1)}, bf16[64,768]{1,0:T(8,128)(2,1)S(1)}, u32[]{:S(2)}, u32[]{:S(2)}) %collective-permute-start.9) | collective-permute-done | bytes 98336 | tf_op jit(solution)/shard_map/ppermute | solution.py:228
  62.8 3.4 %second.1 = (bf16[64,768]{1,0:T(8,128)(2,1)}, f32[64,768]{1,0:T(8,128)S(1)}, bf16[64,768]{1,0:T(8,128)(2,1)S(1)}, f32[8,768]{1,0:T(8,128)S(1)}, bf16[32,2048]{1,0:T(8,128)(2,1)}) custom-call(s32[2]{0:T(128)S(1)} %pad_add_fusion.refs_0_, bf16[64,768]{1,0:T(8,128)(2,1)S(1)} %get-tuple-element.77.refs_1_, bf16[64,768]{1,0:T(8,128)(2,1)S(1)} %collective-permute-done.8.refs_2_, ...), custom_call_target="tpu_custom_call" | custom-call | flops 3300000000 | tf_op jit(solution)/shard_map/second/pallas_call | solution.py:106
  66.2 1.3 collective-permute-start.16
  68.2 5.8 %rest_words.1 = (s32[192,128]{1,0:T(8,128)S(1)}, s32[32,2048]{1,0:T(8,128)S(1)}, f32[192,64]{1,0:T(8,128)S(1)}) custom-call(bf16[192,128]{1,0:T(8,128)(2,1)} %get-tuple-element.68.refs_0_, bf16[8,288,256]{2,1,0:T(8,128)(2,1)} %bitcast.19, bf16[1024,256]{1,0:T(8,128)(2,1)} %constant.13.clone.refs_2_, bf16[64,768]{1,0:T(8,128)(2,1)} %constant.14.clone.refs_3_, ...), custom_call_target="tpu_custom_call" | custom-call | flops 5500000256 | tf_op jit(solution)/shard_map/rest_words/pallas_call | solution.py:106
  74.1 3.4 %hidden.1 = (f32[64,768]{1,0:T(8,128)}, bf16[8,64,384]{2,1,0:T(8,128)(2,1)}, bf16[16,768]{1,0:T(8,128)(2,1)}, f32[8,768]{1,0:T(8,128)}) custom-call(s32[2]{0:T(128)S(1)} %pad_add_fusion.refs_0_, bf16[64,768]{1,0:T(8,128)(2,1)S(1)} %get-tuple-element.87.refs_1_, bf16[64,768]{1,0:T(8,128)(2,1)S(1)} %collective-permute-done.14.refs_2_, ...), custom_call_target="tpu_custom_call" | custom-call | flops 2200000000 | tf_op jit(solution)/shard_map/hidden/pallas_call | solution.py:106
  77.5 5.4 %all-to-all-start.2 = ((bf16[8,64,384]{2,1,0:T(8,128)(2,1)}), bf16[8,64,384]{2,1,0:T(8,128)(2,1)S(1)}, u32[]{:S(2)}, u32[]{:S(2)}) async-start(bf16[8,64,384]{2,1,0:T(8,128)(2,1)} %get-tuple-element.94), calls=%async_computation.2 | async-start | bytes 786432 | tf_op jit(solution)/shard_map/all_to_all | solution.py:238
  82.9 6.2 %rest_context.1.refs_5_.refs_0_ = bf16[192,192]{1,0:T(8,128)(2,1)S(1)} custom-call(s32[192,128]{1,0:T(8,128)S(1)} %get-tuple-element.82.refs_11_.refs_0_, s32[32,2048]{1,0:T(8,128)S(1)} %get-tuple-element.83.refs_1_, f32[192,64]{1,0:T(8,128)S(1)} %get-tuple-element.84.refs_2_, bf16[8,288,256]{2,1,0:T(8,128)(2,1)} %bitcast.21, ...), custom_call_target="tpu_custom_call" | custom-call | flops 6600000000 | tf_op jit(solution)/shard_map/rest_context/pallas_call | solution.py:106
  91.0 5.3 %all-to-all-done.2.refs_1_ = bf16[8,64,384]{2,1,0:T(8,128)(2,1)S(1)} async-done(((bf16[8,64,384]{2,1,0:T(8,128)(2,1)}), bf16[8,64,384]{2,1,0:T(8,128)(2,1)S(1)}, u32[]{:S(2)}, u32[]{:S(2)}) %all-to-all-start.2) | async-done | bytes 393248 | tf_op jit(solution)/shard_map/all_to_all | solution.py:238
  96.3 3.4 %values_back.1 = (bf16[256,192]{1,0:T(8,128)(2,1)S(1)}, bf16[384,192]{1,0:T(8,128)(2,1)S(1)}) custom-call(s32[2]{0:T(128)S(1)} %pad_add_fusion.refs_0_, bf16[8,64,384]{2,1,0:T(8,128)(2,1)S(1)} %all-to-all-done.2.refs_1_, bf16[3,512,256]{2,1,0:T(8,128)(2,1)} %get-tuple-element.74.refs_5_.refs_2_, bf16[3,256,768]{2,1,0:T(8,128)(2,1)} %get-tuple-element.95.refs_3_, ...), custom_call_target="tpu_custom_call" | custom-call | flops 4400000000 | tf_op jit(solution)/shard_map/values_back/pallas_call | solution.py:106
  100.0 1.3 collective-permute-start.21
  101.7 2.6 %value_grad.1.refs_15_ = bf16[8,48,768]{2,1,0:T(8,128)(2,1)} custom-call(bf16[256,768]{1,0:T(8,128)(2,1)} %refs_0_.5, bf16[256,192]{1,0:T(8,128)(2,1)S(1)} %get-tuple-element.96.refs_1_.refs_6_.refs_0_, bf16[384,192]{1,0:T(8,128)(2,1)S(1)} %get-tuple-element.97.refs_2_, bf16[384,192]{1,0:T(8,128)(2,1)} %get-tuple-element.86.refs_5_.refs_3_, ...), custom_call_target="tpu_custom_call" | custom-call | flops 2750000128 | tf_op jit(solution)/shard_map/value_grad/pallas_call | solution.py:106
  104.2 3.8 %all-to-all-start.3 = ((bf16[8,48,768]{2,1,0:T(8,128)(2,1)}), bf16[8,48,768]{2,1,0:T(8,128)(2,1)S(1)}, u32[]{:S(2)}, u32[]{:S(2)}) async-start(bf16[8,48,768]{2,1,0:T(8,128)(2,1)} %value_grad.1.refs_15_), calls=%async_computation.3 | async-start | bytes 1179648 | tf_op jit(solution)/shard_map/all_to_all | solution.py:238
  109.1 4.6 %rest_first.1 = (bf16[192,768]{1,0:T(8,128)(2,1)S(1)}, f32[192,768]{1,0:T(8,128)}) custom-call(bf16[192,192]{1,0:T(8,128)(2,1)} %copy-done.6, bf16[192,192]{1,0:T(8,128)(2,1)} %copy-done.18, bf16[192,192]{1,0:T(8,128)(2,1)} %copy-done.17, bf16[192,192]{1,0:T(8,128)(2,1)} %copy-done.16, bf16[192,768]{1,0:T(8,128)(2,1)} %refs_4_.4, ...), custom_call_target="tpu_custom_call" | custom-call | flops 4400000000 | tf_op jit(solution)/shard_map/rest_first/pallas_call | solution.py:106
  115.9 3.5 %input_grad.1.refs_1_ = f32[256,768]{1,0:T(8,128)} custom-call(bf16[256,192]{1,0:T(8,128)(2,1)} %copy-done, bf16[256,192]{1,0:T(8,128)(2,1)} %copy-done.14, bf16[256,192]{1,0:T(8,128)(2,1)} %copy-done.13, bf16[256,192]{1,0:T(8,128)(2,1)} %copy-done.12, bf16[192,768]{1,0:T(8,128)(2,1)} %bitcast.16, bf16[192,768]{1,0:T(8,128)(2,1)} %copy-done.10, ...), custom_call_target="tpu_custom_call" | custom-call | flops 55000000 | tf_op jit(solution)/shard_map/input_grad/pallas_call | solution.py:106
  119.4 5.0 %all-to-all-done.3.refs_0_ = bf16[8,48,768]{2,1,0:T(8,128)(2,1)S(1)} async-done(((bf16[8,48,768]{2,1,0:T(8,128)(2,1)}), bf16[8,48,768]{2,1,0:T(8,128)(2,1)S(1)}, u32[]{:S(2)}, u32[]{:S(2)}) %all-to-all-start.3) | async-done | bytes 589856 | tf_op jit(solution)/shard_map/all_to_all | solution.py:238
  124.4 1.4 value_sums.1
  125.8 3.6 %all-to-all-start.4 = ((bf16[8,24,768]{2,1,0:T(8,128)(2,1)}), bf16[8,24,768]{2,1,0:T(8,128)(2,1)S(1)}, u32[]{:S(2)}, u32[]{:S(2)}) async-start(bf16[8,24,768]{2,1,0:T(8,128)(2,1)} %get-tuple-element.103.refs_5_), calls=%async_computation.4 | async-start | bytes 589824 | tf_op jit(solution)/shard_map/all_to_all | solution.py:238
  132.3 7.9 %weights.1 = (f32[768,768]{1,0:T(8,128)}, f32[768]{0:T(1024)}, f32[768,768]{1,0:T(8,128)}) custom-call(bf16[8,32,2048]{2,1,0:T(8,128)(2,1)} %bitcast.13, bf16[8,32,2048]{2,1,0:T(8,128)(2,1)} %copy-done.15, bf16[768,768]{1,0:T(8,128)(2,1)} %refs_2_.5, f32[768]{0:T(1024)} %refs_3_.3, bf16[768,768]{1,0:T(8,128)(2,1)} %refs_4_.5, ...), custom_call_target="tpu_custom_call" | custom-call | flops 3300000000 | tf_op jit(solution)/shard_map/weights/pallas_call | solution.py:106
  140.9 3.9 %last.1 = (bf16[256,768]{1,0:T(8,128)(2,1)}, f32[192,768]{1,0:T(8,128)}, f32[192,768]{1,0:T(8,128)}) custom-call(s32[2]{0:T(128)S(1)} %pad_add_fusion.refs_0_, bf16[192,768]{1,0:T(8,128)(2,1)S(1)} %get-tuple-element.100.refs_10_.refs_1_, bf16[192,768]{1,0:T(8,128)(2,1)S(1)} %collective-permute-done.23.refs_6_.refs_2_, ...), custom_call_target="tpu_custom_call" | custom-call | flops 55000000 | tf_op jit(solution)/shard_map/last/pallas_call | solution.py:106
  (101 shorter events, 19.3 us)
Async XLA Ops:
  9.1 14.6 %all-to-all-start = ((bf16[8,64,128]{2,1,0:T(8,128)(2,1)}), bf16[8,64,128]{2,1,0:T(8,128)(2,1)S(1)}, u32[]{:S(2)}, u32[]{:S(2)}) async-start(bf16[8,64,128]{2,1,0:T(8,128)(2,1)} %order.1.refs_8_), calls=%async_computation | async-start | bytes 262144 | tf_op jit(solution)/shard_map/all_to_all | solution.py:238
  16.4 51.8 %all-gather.5.cloned.1.call-start = ((), (), s32[]{:S(2)}) async-start(), calls=%async_computation.5 | async-start | bytes 1327104 | tf_op jit(solution)/shard_map/all_gather | solution.py:328
  29.0 17.5 %all-to-all-start.1 = ((bf16[8,64,192]{2,1,0:T(8,128)(2,1)}), bf16[8,64,192]{2,1,0:T(8,128)(2,1)S(1)}, u32[]{:S(2)}, u32[]{:S(2)}) async-start(bf16[8,64,192]{2,1,0:T(8,128)(2,1)} %get-tuple-element.71), calls=%async_computation.1 | async-start | bytes 524288 | tf_op jit(solution)/shard_map/all_to_all | solution.py:238
  34.0 79.7 %all-gather.7.cloned.1.call-start = ((), (), s32[]{:S(2)}) async-start(), calls=%async_computation.6 | async-start | bytes 1179648 | tf_op jit(solution)/shard_map/all_gather | solution.py:500
  34.1 10.1 %collective-permute-start.6 = (bf16[192,768]{1,0:T(8,128)(2,1)S(1)}, bf16[192,768]{1,0:T(8,128)(2,1)}, u32[]{:S(2)}, u32[]{:S(2)}) collective-permute-start(bf16[192,768]{1,0:T(8,128)(2,1)S(1)} %copy-done.4), channel_id=1, source_target_pairs={{0,2},{1,3},{2,0},{3,1},{4,6},{5,7},{6,4},{7,5},{8,10},{9,11},{10,... | collective-permute-start | bytes 884744 | tf_op jit(solution)/shard_map/ppermute | solution.py:228
  35.7 14.4 %collective-permute-start.12 = (bf16[192,768]{1,0:T(8,128)(2,1)S(1)}, bf16[192,768]{1,0:T(8,128)(2,1)}, u32[]{:S(2)}, u32[]{:S(2)}) collective-permute-start(bf16[192,768]{1,0:T(8,128)(2,1)S(1)} %bitcast.17), channel_id=1, source_target_pairs={{0,2},{1,3},{2,0},{3,1},{4,6},{5,7},{6,4},{7,5},{8,10},{9,11},{10,... | collective-permute-start | bytes 884744 | tf_op jit(solution)/shard_map/ppermute | solution.py:228
  36.9 7.3 %collective-permute-start.1 = (bf16[32,192]{1,0:T(8,128)(2,1)S(1)}, bf16[32,192]{1,0:T(8,128)(2,1)S(1)}, u32[]{:S(2)}, u32[]{:S(2)}) collective-permute-start(bf16[32,192]{1,0:T(8,128)(2,1)S(1)} %get-tuple-element.121), channel_id=1, source_target_pairs={{4,0},{8,4},{12,8},{16,12},{20,16},{24,20},{28,24},{5,1},{9,5},{13... | collective-permute-start | bytes 36872 | tf_op jit(solution)/shard_map/ppermute | solution.py:357
  38.2 6.0 %collective-permute-start = (bf16[32,192]{1,0:T(8,128)(2,1)S(1)}, bf16[32,192]{1,0:T(8,128)(2,1)S(1)}, u32[]{:S(2)}, u32[]{:S(2)}) collective-permute-start(bf16[32,192]{1,0:T(8,128)(2,1)S(1)} %get-tuple-element.122), channel_id=1, source_target_pairs={{0,4},{4,8},{8,12},{12,16},{16,20},{20,24},{24,28},{1,5},{5,9},{9,... | collective-permute-start | bytes 36872 | tf_op jit(solution)/shard_map/ppermute | solution.py:356
  42.7 7.7 %collective-permute-start.5 = (bf16[192,768]{1,0:T(8,128)(2,1)S(1)}, bf16[192,768]{1,0:T(8,128)(2,1)}, u32[]{:S(2)}, u32[]{:S(2)}) collective-permute-start(bf16[192,768]{1,0:T(8,128)(2,1)S(1)} %copy-done.4), channel_id=1, source_target_pairs={{0,1},{1,0},{2,3},{3,2},{4,5},{5,4},{6,7},{7,6},{8,9},{9,8},{10,11... | collective-permute-start | bytes 884744 | tf_op jit(solution)/shard_map/ppermute | solution.py:228
  44.2 6.5 %collective-permute-start.7 = (bf16[192,768]{1,0:T(8,128)(2,1)}, bf16[192,768]{1,0:T(8,128)(2,1)}, u32[]{:S(2)}, u32[]{:S(2)}) collective-permute-start(bf16[192,768]{1,0:T(8,128)(2,1)} %collective-permute-done.6.refs_6_), channel_id=1, source_target_pairs={{0,1},{1,0},{2,3},{3,2},{4,5},{5,4},{6,7},{7,6},{8,9},{9,8},{10,11... | collective-permute-start | bytes 884744 | tf_op jit(solution)/shard_map/ppermute | solution.py:228
  50.5 8.1 %collective-permute-start.11 = (bf16[192,768]{1,0:T(8,128)(2,1)S(1)}, bf16[192,768]{1,0:T(8,128)(2,1)S(1)}, u32[]{:S(2)}, u32[]{:S(2)}) collective-permute-start(bf16[192,768]{1,0:T(8,128)(2,1)S(1)} %bitcast.18), channel_id=1, source_target_pairs={{0,1},{1,0},{2,3},{3,2},{4,5},{5,4},{6,7},{7,6},{8,9},{9,8},{10,11... | collective-permute-start | bytes 884744 | tf_op jit(solution)/shard_map/ppermute | solution.py:228
  50.7 7.9 %collective-permute-start.13 = (bf16[192,768]{1,0:T(8,128)(2,1)}, bf16[192,768]{1,0:T(8,128)(2,1)S(1)}, u32[]{:S(2)}, u32[]{:S(2)}) collective-permute-start(bf16[192,768]{1,0:T(8,128)(2,1)} %collective-permute-done.12.refs_16_.refs_6_), channel_id=1, source_target_pairs={{0,1},{1,0},{2,3},{3,2},{4,5},{5,4},{6,7},{7,6},{8,9},{9,8},{10,11... | collective-permute-start | bytes 884744 | tf_op jit(solution)/shard_map/ppermute | solution.py:228
  56.5 6.3 %collective-permute-start.9 = (bf16[64,768]{1,0:T(8,128)(2,1)S(1)}, bf16[64,768]{1,0:T(8,128)(2,1)S(1)}, u32[]{:S(2)}, u32[]{:S(2)}) collective-permute-start(bf16[64,768]{1,0:T(8,128)(2,1)S(1)} %get-tuple-element.77.refs_1_), channel_id=1, source_target_pairs={{0,2},{1,3},{2,0},{3,1},{4,6},{5,7},{6,4},{7,5},{8,10},{9,11},{10,... | collective-permute-start | bytes 294920 | tf_op jit(solution)/shard_map/ppermute | solution.py:228
  66.2 7.8 %collective-permute-start.16 = (bf16[64,768]{1,0:T(8,128)(2,1)S(1)}, bf16[64,768]{1,0:T(8,128)(2,1)S(1)}, u32[]{:S(2)}, u32[]{:S(2)}) collective-permute-start(bf16[64,768]{1,0:T(8,128)(2,1)S(1)} %get-tuple-element.87.refs_1_), channel_id=1, source_target_pairs={{0,3},{1,2},{2,1},{3,0},{4,7},{5,6},{6,5},{7,4},{8,11},{9,10},{10,... | collective-permute-start | bytes 294920 | tf_op jit(solution)/shard_map/ppermute | solution.py:228
  67.5 6.5 %collective-permute-start.15 = (bf16[64,768]{1,0:T(8,128)(2,1)S(1)}, bf16[64,768]{1,0:T(8,128)(2,1)S(1)}, u32[]{:S(2)}, u32[]{:S(2)}) collective-permute-start(bf16[64,768]{1,0:T(8,128)(2,1)S(1)} %get-tuple-element.87.refs_1_), channel_id=1, source_target_pairs={{0,2},{1,3},{2,0},{3,1},{4,6},{5,7},{6,4},{7,5},{8,10},{9,11},{10,... | collective-permute-start | bytes 294920 | tf_op jit(solution)/shard_map/ppermute | solution.py:228
  67.8 6.2 %collective-permute-start.14 = (bf16[64,768]{1,0:T(8,128)(2,1)S(1)}, bf16[64,768]{1,0:T(8,128)(2,1)S(1)}, u32[]{:S(2)}, u32[]{:S(2)}) collective-permute-start(bf16[64,768]{1,0:T(8,128)(2,1)S(1)} %get-tuple-element.87.refs_1_), channel_id=1, source_target_pairs={{0,1},{1,0},{2,3},{3,2},{4,5},{5,4},{6,7},{7,6},{8,9},{9,8},{10,11... | collective-permute-start | bytes 294920 | tf_op jit(solution)/shard_map/ppermute | solution.py:228
  77.5 18.8 %all-to-all-start.2 = ((bf16[8,64,384]{2,1,0:T(8,128)(2,1)}), bf16[8,64,384]{2,1,0:T(8,128)(2,1)S(1)}, u32[]{:S(2)}, u32[]{:S(2)}) async-start(bf16[8,64,384]{2,1,0:T(8,128)(2,1)} %get-tuple-element.94), calls=%async_computation.2 | async-start | bytes 786432 | tf_op jit(solution)/shard_map/all_to_all | solution.py:238
  89.1 12.2 %collective-permute-start.19 = (bf16[192,192]{1,0:T(8,128)(2,1)S(1)}, bf16[192,192]{1,0:T(8,128)(2,1)S(1)}, u32[]{:S(2)}, u32[]{:S(2)}) collective-permute-start(bf16[192,192]{1,0:T(8,128)(2,1)S(1)} %rest_context.1.refs_5_.refs_0_), channel_id=1, source_target_pairs={{0,3},{1,2},{2,1},{3,0},{4,7},{5,6},{6,5},{7,4},{8,11},{9,10},{10,... | collective-permute-start | bytes 221192 | tf_op jit(solution)/shard_map/ppermute | solution.py:228
  90.4 17.7 %collective-permute-start.18 = (bf16[192,192]{1,0:T(8,128)(2,1)S(1)}, bf16[192,192]{1,0:T(8,128)(2,1)S(1)}, u32[]{:S(2)}, u32[]{:S(2)}) collective-permute-start(bf16[192,192]{1,0:T(8,128)(2,1)S(1)} %rest_context.1.refs_5_.refs_0_), channel_id=1, source_target_pairs={{0,2},{1,3},{2,0},{3,1},{4,6},{5,7},{6,4},{7,5},{8,10},{9,11},{10,... | collective-permute-start | bytes 221192 | tf_op jit(solution)/shard_map/ppermute | solution.py:228
  90.9 17.2 %collective-permute-start.17 = (bf16[192,192]{1,0:T(8,128)(2,1)S(1)}, bf16[192,192]{1,0:T(8,128)(2,1)S(1)}, u32[]{:S(2)}, u32[]{:S(2)}) collective-permute-start(bf16[192,192]{1,0:T(8,128)(2,1)S(1)} %rest_context.1.refs_5_.refs_0_), channel_id=1, source_target_pairs={{0,1},{1,0},{2,3},{3,2},{4,5},{5,4},{6,7},{7,6},{8,9},{9,8},{10,11... | collective-permute-start | bytes 221192 | tf_op jit(solution)/shard_map/ppermute | solution.py:228
  99.7 8.3 %collective-permute-start.22 = (bf16[256,192]{1,0:T(8,128)(2,1)S(1)}, bf16[256,192]{1,0:T(8,128)(2,1)S(1)}, u32[]{:S(2)}, u32[]{:S(2)}) collective-permute-start(bf16[256,192]{1,0:T(8,128)(2,1)S(1)} %get-tuple-element.96.refs_1_.refs_6_.refs_0_), channel_id=1, source_target_pairs={{0,3},{1,2},{2,1},{3,0},{4,7},{5,6},{6,5},{7,4},{8,11},{9,10},{10,... | collective-permute-start | bytes 294920 | tf_op jit(solution)/shard_map/ppermute | solution.py:228
  100.0 8.4 %collective-permute-start.21 = (bf16[256,192]{1,0:T(8,128)(2,1)S(1)}, bf16[256,192]{1,0:T(8,128)(2,1)S(1)}, u32[]{:S(2)}, u32[]{:S(2)}) collective-permute-start(bf16[256,192]{1,0:T(8,128)(2,1)S(1)} %get-tuple-element.96.refs_1_.refs_6_.refs_0_), channel_id=1, source_target_pairs={{0,2},{1,3},{2,0},{3,1},{4,6},{5,7},{6,4},{7,5},{8,10},{9,11},{10,... | collective-permute-start | bytes 294920 | tf_op jit(solution)/shard_map/ppermute | solution.py:228
  101.3 7.1 %collective-permute-start.20 = (bf16[256,192]{1,0:T(8,128)(2,1)S(1)}, bf16[256,192]{1,0:T(8,128)(2,1)S(1)}, u32[]{:S(2)}, u32[]{:S(2)}) collective-permute-start(bf16[256,192]{1,0:T(8,128)(2,1)S(1)} %get-tuple-element.96.refs_1_.refs_6_.refs_0_), channel_id=1, source_target_pairs={{0,1},{1,0},{2,3},{3,2},{4,5},{5,4},{6,7},{7,6},{8,9},{9,8},{10,11... | collective-permute-start | bytes 294920 | tf_op jit(solution)/shard_map/ppermute | solution.py:228
  104.2 20.2 %all-to-all-start.3 = ((bf16[8,48,768]{2,1,0:T(8,128)(2,1)}), bf16[8,48,768]{2,1,0:T(8,128)(2,1)S(1)}, u32[]{:S(2)}, u32[]{:S(2)}) async-start(bf16[8,48,768]{2,1,0:T(8,128)(2,1)} %value_grad.1.refs_15_), calls=%async_computation.3 | async-start | bytes 1179648 | tf_op jit(solution)/shard_map/all_to_all | solution.py:238
  113.7 17.6 %collective-permute-start.29 = (bf16[8,32,2048]{2,1,0:T(8,128)(2,1)}, bf16[8,32,2048]{2,1,0:T(8,128)(2,1)S(1)}, u32[]{:S(2)}, u32[]{:S(2)}) collective-permute-start(bf16[8,32,2048]{2,1,0:T(8,128)(2,1)} %bitcast.12), channel_id=1, source_target_pairs={{0,1},{1,0},{2,3},{3,2},{4,5},{5,4},{6,7},{7,6},{8,9},{9,8},{10,11... | collective-permute-start | bytes 3145736 | tf_op jit(solution)/shard_map/ppermute | solution.py:228
  114.0 16.4 %collective-permute-start.25 = (bf16[192,768]{1,0:T(8,128)(2,1)S(1)}, bf16[192,768]{1,0:T(8,128)(2,1)S(1)}, u32[]{:S(2)}, u32[]{:S(2)}) collective-permute-start(bf16[192,768]{1,0:T(8,128)(2,1)S(1)} %get-tuple-element.100.refs_10_.refs_1_), channel_id=1, source_target_pairs={{0,3},{1,2},{2,1},{3,0},{4,7},{5,6},{6,5},{7,4},{8,11},{9,10},{10,... | collective-permute-start | bytes 884744 | tf_op jit(solution)/shard_map/ppermute | solution.py:228
  115.2 15.9 %collective-permute-start.24 = (bf16[192,768]{1,0:T(8,128)(2,1)S(1)}, bf16[192,768]{1,0:T(8,128)(2,1)S(1)}, u32[]{:S(2)}, u32[]{:S(2)}) collective-permute-start(bf16[192,768]{1,0:T(8,128)(2,1)S(1)} %get-tuple-element.100.refs_10_.refs_1_), channel_id=1, source_target_pairs={{0,2},{1,3},{2,0},{3,1},{4,6},{5,7},{6,4},{7,5},{8,10},{9,11},{10,... | collective-permute-start | bytes 884744 | tf_op jit(solution)/shard_map/ppermute | solution.py:228
  115.9 15.4 %collective-permute-start.23 = (bf16[192,768]{1,0:T(8,128)(2,1)S(1)}, bf16[192,768]{1,0:T(8,128)(2,1)S(1)}, u32[]{:S(2)}, u32[]{:S(2)}) collective-permute-start(bf16[192,768]{1,0:T(8,128)(2,1)S(1)} %get-tuple-element.100.refs_10_.refs_1_), channel_id=1, source_target_pairs={{0,1},{1,0},{2,3},{3,2},{4,5},{5,4},{6,7},{7,6},{8,9},{9,8},{10,11... | collective-permute-start | bytes 884744 | tf_op jit(solution)/shard_map/ppermute | solution.py:228
  125.8 15.1 %all-to-all-start.4 = ((bf16[8,24,768]{2,1,0:T(8,128)(2,1)}), bf16[8,24,768]{2,1,0:T(8,128)(2,1)S(1)}, u32[]{:S(2)}, u32[]{:S(2)}) async-start(bf16[8,24,768]{2,1,0:T(8,128)(2,1)} %get-tuple-element.103.refs_5_), calls=%async_computation.4 | async-start | bytes 589824 | tf_op jit(solution)/shard_map/all_to_all | solution.py:238
  129.5 10.7 %collective-permute-start.28 = (bf16[8,16,768]{2,1,0:T(8,128)(2,1)S(1)}, bf16[8,16,768]{2,1,0:T(8,128)(2,1)S(1)}, u32[]{:S(2)}, u32[]{:S(2)}) collective-permute-start(bf16[8,16,768]{2,1,0:T(8,128)(2,1)S(1)} %get-tuple-element.102.refs_5_), channel_id=1, source_target_pairs={{0,3},{1,2},{2,1},{3,0},{4,7},{5,6},{6,5},{7,4},{8,11},{9,10},{10,... | collective-permute-start | bytes 589832 | tf_op jit(solution)/shard_map/ppermute | solution.py:228
  130.3 10.5 %collective-permute-start.27 = (bf16[8,16,768]{2,1,0:T(8,128)(2,1)S(1)}, bf16[8,16,768]{2,1,0:T(8,128)(2,1)S(1)}, u32[]{:S(2)}, u32[]{:S(2)}) collective-permute-start(bf16[8,16,768]{2,1,0:T(8,128)(2,1)S(1)} %get-tuple-element.102.refs_5_), channel_id=1, source_target_pairs={{0,2},{1,3},{2,0},{3,1},{4,6},{5,7},{6,4},{7,5},{8,10},{9,11},{10,... | collective-permute-start | bytes 589832 | tf_op jit(solution)/shard_map/ppermute | solution.py:228
  131.1 9.8 %collective-permute-start.26 = (bf16[8,16,768]{2,1,0:T(8,128)(2,1)S(1)}, bf16[8,16,768]{2,1,0:T(8,128)(2,1)S(1)}, u32[]{:S(2)}, u32[]{:S(2)}) collective-permute-start(bf16[8,16,768]{2,1,0:T(8,128)(2,1)S(1)} %get-tuple-element.102.refs_5_), channel_id=1, source_target_pairs={{0,1},{1,0},{2,3},{3,2},{4,5},{5,4},{6,7},{7,6},{8,9},{9,8},{10,11... | collective-permute-start | bytes 589832 | tf_op jit(solution)/shard_map/ppermute | solution.py:228
  (24 other events, 111.0 us)
Sparse Core Ops, SparseCore 0:
  22.9 44.2 all-gather.4
  69.3 41.7 all-gather.6
